TPU v7x, 32 devices: a whole 2x2x4 slice. The times are simulated.
32 devices in a mesh: groups: 1, gx: 4 (over y, x), yz: 8 (over z, core).
Axes of the slice: x: 2, y: 2, z: 4, core: 2. Of those that a mesh axis runs over, the one named last changes fastest.
Arguments:
- hidden_in: bfloat16 [128, 8192], P(('groups', 'gx'), 'yz'), may hold values from -12 to 12
- norm_gain_a: float32 [8192], P('yz'), may hold values from 0.1 to 1.9
- mixer_projection: bfloat16 [2, 16384, 8192], P(None, 'gx', 'yz'), may hold values from -0.0625 to 0.0625
- conv_weight: float32 [4, 16384], P(None, ('gx', 'yz')), may hold values from -3 to 3
- conv_bias: float32 [16384], P(('gx', 'yz')), may hold values from -0.5 to 0.5
- conv_state: bfloat16 [16384, 3, 128], P(('gx', 'yz'), None, 'groups'), may hold values from -6 to 6
- ssm_state: bfloat16 [16384, 16, 128], P(('gx', 'yz'), None, 'groups'), may hold values from -6 to 6
- reset_ids: int32 [16], P('groups'), may hold values from 0 to 127
- x_proj: bfloat16 [16384, 544], P(('gx', 'yz')), may hold values from -0.09375 to 0.09375
- dt_proj: bfloat16 [512, 16384], P(None, ('gx', 'yz')), may hold values from -0.25 to 0.25
- dt_bias: float32 [16384], P(('gx', 'yz')), may hold values from -4 to -1
- a_log: float32 [16, 16384], P(None, ('gx', 'yz')), may hold values from 0 to 3
- d_skip: float32 [16384], P(('gx', 'yz')), may hold values from -1 to 2
- mixer_output: bfloat16 [16384, 8192], P('gx', 'yz'), may hold values from -0.046875 to 0.046875
- norm_gain_b: float32 [8192], P('yz'), may hold values from 0.5 to 1.5
- attention_projection: bfloat16 [8192, 8, 1280], P('yz', 'gx'), may hold values from -0.0625 to 0.0625
- head_output: bfloat16 [8192, 8192], P('gx', 'yz'), may hold values from -0.0625 to 0.0625
- kv_cache: bfloat16 [128, 64, 8, 256], P(('groups', 'yz'), None, 'gx'), as said below
- lengths: int32 [128], P(('groups', 'yz')), may hold values from 1 to 64, 4096 in all
- assign: int32 [128], P('groups'), may hold values from 0 to 127, each once
Outputs:
- hidden_out: bfloat16 [128, 8192], P(('groups', 'gx'), 'yz')
- ssm_new: bfloat16 [16384, 16, 128], P(('gx', 'yz'), None, 'groups')
- conv_new: bfloat16 [16384, 3, 128], P(('gx', 'yz'), None, 'groups')
- fresh_kv: bfloat16 [128, 8, 256], P(('groups', 'yz'), 'gx')
Inputs may be any that keep to these rules, and one draw needn't show every extreme that they name: `reset_ids`: ids of admitted requests whose conv and recurrent states start from zero; an id may repeat. `lengths`: at least one slot holds 64 valid positions. `assign`: each request is held by exactly one slot. `kv_cache`: positions at or past a slot's length hold arbitrary values that must not be read.
All inputs are finite; a program needn't handle non-finite values. No bound on the sum of `lengths` on one device may be relied on, other than what follows from the above.
Results may differ from a plain program's by a relative error of at most 0.03.
Values may be sent and summed in bfloat16 or wider, within the bound.
No kernel may reach another device: no remote copies, remote signals or barrier semaphores. Data moves between devices by JAX's collectives and lax.ppermute only.
A program may use at most 128 MiB of HBM per device.

v0:
```python
import math

import jax
import jax.numpy as jnp
from jax import lax
from jax.sharding import PartitionSpec as P


def normalize(values, gain):
    wide = values.astype(jnp.float32)
    squares = lax.psum(jnp.sum(wide * wide, axis=1), "yz")
    width = wide.shape[1] * lax.axis_size("yz")
    scale = lax.rsqrt(squares / width + 1e-05)
    return (wide * scale[:, None] * gain[None, :]).astype(jnp.bfloat16)


def spread(values):
    return lax.all_gather(values, "gx", axis=0, tiled=True)


def owner_sum(term_fn, owned_rows):
    return lax.psum_scatter(
        term_fn(jnp.int32(0), owned_rows * lax.axis_size("yz")).astype(jnp.bfloat16),
        "yz",
        scatter_dimension=0,
        tiled=True,
    ).astype(jnp.float32)


def to_rows(partial_value):
    return lax.psum_scatter(
        partial_value.astype(jnp.bfloat16), "gx", scatter_dimension=0, tiled=True
    ).astype(jnp.float32)


def on_device(
    hidden_in,
    norm_gain_a,
    mixer_projection,
    conv_weight,
    conv_bias,
    conv_state,
    ssm_state,
    reset_ids,
    x_proj,
    dt_proj,
    dt_bias,
    a_log,
    d_skip,
    mixer_output,
    norm_gain_b,
    attention_projection,
    head_output,
    kv_cache,
    lengths,
    assign,
):
    batch = assign.shape[0]
    normed = normalize(hidden_in, norm_gain_a)
    normalized_rows = spread(normed)

    def mixer_term(start, count):
        return jnp.einsum(
            "rfz,uz->fru", mixer_projection, normalized_rows, preferred_element_type=jnp.float32
        )

    owned = owner_sum(mixer_term, mixer_projection.shape[1] // lax.axis_size("yz")).astype(
        jnp.bfloat16
    )
    xval = owned[:, 0, :]
    zval = owned[:, 1, :]
    reset = jnp.any(reset_ids[:, None] == jnp.arange(batch, dtype=jnp.int32)[None, :], axis=0)
    conv_old = jnp.where(reset[None, None, :], jnp.zeros_like(conv_state), conv_state)
    window = jnp.concatenate([conv_old, xval[:, None, :]], axis=1)
    conv_new = window[:, 1:, :]
    mixed_conv = (
        jnp.sum(jnp.transpose(conv_weight)[:, :, None] * window.astype(jnp.float32), axis=1)
        + conv_bias[:, None]
    )
    activated = jax.nn.silu(mixed_conv).astype(jnp.bfloat16)
    partial_value = lax.dot_general(
        x_proj, activated, (((0,), (0,)), ((), ())), preferred_element_type=jnp.float32
    )
    proj = lax.psum(partial_value, ("gx", "yz"))
    rank = dt_proj.shape[0]
    nstate = a_log.shape[0]
    dt_low = proj[:rank].astype(jnp.bfloat16)
    bmat = proj[rank : rank + nstate]
    cmat = proj[rank + nstate :]
    step_pre = lax.dot_general(
        dt_proj, dt_low, (((0,), (0,)), ((), ())), preferred_element_type=jnp.float32
    )
    step = jax.nn.softplus(step_pre + dt_bias[:, None])
    rates = -jnp.exp(jnp.transpose(a_log))
    old = jnp.where(reset[None, None, :], jnp.zeros((), jnp.float32), ssm_state.astype(jnp.float32))
    act_wide = activated.astype(jnp.float32)
    state = (
        jnp.exp(step[:, None, :] * rates[:, :, None]) * old
        + step[:, None, :] * bmat[None, :, :] * act_wide[:, None, :]
    )
    ssm_new = state.astype(jnp.bfloat16)
    yval = jnp.sum(state * cmat[None, :, :], axis=1) + d_skip[:, None] * act_wide
    gated = (yval * jax.nn.silu(zval.astype(jnp.float32))).astype(jnp.bfloat16)
    weights = mixer_output
    mixed = lax.dot_general(
        lax.all_gather(gated, "yz", axis=0, tiled=True),
        weights,
        (((0,), (0,)), ((), ())),
        preferred_element_type=jnp.float32,
    )
    first_out = (hidden_in.astype(jnp.float32) + to_rows(mixed)).astype(jnp.bfloat16)
    second_normed = normalize(first_out, norm_gain_b)
    second_all = spread(second_normed)
    group_count = attention_projection.shape[1]
    group_cols = attention_projection.shape[2]
    flattened = attention_projection.reshape(
        attention_projection.shape[0], group_count * group_cols
    )
    slot_count = kv_cache.shape[0]
    slot_requests = lax.dynamic_slice_in_dim(
        assign, lax.axis_index("yz") * slot_count, slot_count, 0
    )

    def head_term(start, count):
        return jnp.dot(second_all, flattened, preferred_element_type=jnp.float32)

    block_rows = owner_sum(head_term, slot_count).astype(jnp.bfloat16)
    every_row = lax.all_gather(block_rows, "yz", axis=0, tiled=True)
    newest_entry = jnp.take(every_row, slot_requests, axis=0)
    newest_entry = newest_entry.reshape(slot_count, group_count, group_cols)
    head_dim = kv_cache.shape[3] // 2
    per_group = group_cols // head_dim - 2
    fresh_kv = newest_entry[:, :, per_group * head_dim :]
    query_vector = newest_entry[:, :, : per_group * head_dim].reshape(
        slot_count, group_count, per_group, head_dim
    )
    key_new = newest_entry[:, :, per_group * head_dim : (per_group + 1) * head_dim]
    value_new = newest_entry[:, :, (per_group + 1) * head_dim :]
    keys = kv_cache[..., :head_dim]
    values = kv_cache[..., head_dim:]
    factor = 1.0 / math.sqrt(head_dim)
    scores = (
        jnp.einsum("sghd,stgd->sght", query_vector, keys, preferred_element_type=jnp.float32)
        * factor
    )
    own = (
        jnp.einsum("sghd,sgd->sgh", query_vector, key_new, preferred_element_type=jnp.float32)
        * factor
    )
    positions = jnp.arange(kv_cache.shape[1], dtype=jnp.int32)
    valid = (positions[None, :] < lengths[:, None])[:, None, None, :]
    top = jnp.maximum(jnp.max(jnp.where(valid, scores, -1e30), axis=-1), own)
    expo = jnp.where(valid, jnp.exp(scores - top[..., None]), 0.0)
    expo_own = jnp.exp(own - top)
    total = jnp.sum(expo, axis=-1) + expo_own
    weights = (expo / total[..., None]).astype(jnp.bfloat16)
    weight_own = (expo_own / total).astype(jnp.bfloat16)
    attended = jnp.einsum("sght,stgd->sghd", weights, values, preferred_element_type=jnp.float32)
    attended = (
        attended
        + weight_own.astype(jnp.float32)[..., None] * value_new.astype(jnp.float32)[:, :, None, :]
    )
    heads = attended.astype(jnp.bfloat16).reshape(slot_count, group_count * per_group * head_dim)
    by_slot = jnp.dot(
        lax.all_gather(heads, "yz", axis=0, tiled=True),
        head_output,
        preferred_element_type=jnp.float32,
    )
    by_request = jnp.take(by_slot, jnp.argsort(assign), axis=0)
    hidden_out = (first_out.astype(jnp.float32) + to_rows(by_request)).astype(jnp.bfloat16)
    return (hidden_out, ssm_new, conv_new, fresh_kv)


def solution(mesh):
    placed = (
        P(("groups", "gx"), "yz"),
        P("yz"),
        P(None, "gx", "yz"),
        P(None, ("gx", "yz")),
        P(("gx", "yz")),
        P(("gx", "yz"), None, "groups"),
        P(("gx", "yz"), None, "groups"),
        P("groups"),
        P(("gx", "yz"), None),
        P(None, ("gx", "yz")),
        P(("gx", "yz")),
        P(None, ("gx", "yz")),
        P(("gx", "yz")),
        P("gx", "yz"),
        P("yz"),
        P("yz", "gx", None),
        P("gx", "yz"),
        P(("groups", "yz"), None, "gx", None),
        P(("groups", "yz")),
        P("groups"),
    )
    return jax.shard_map(
        on_device,
        mesh=mesh,
        in_specs=placed,
        out_specs=(
            P(("groups", "gx"), "yz"),
            P(("gx", "yz"), None, "groups"),
            P(("gx", "yz"), None, "groups"),
            P(("groups", "yz"), "gx", None),
        ),
        check_vma=False,
    )
```

profile of v0, /device:TPU:0, one launch (start us, length us, event | category | flops | bytes accessed | tf_op | source)
XLA Modules:
  0.0 404.5 jit_solution(747982498712659782)
XLA Ops:
  7.2 1.0 fusion.13
  8.2 18.1 %psum.21 = f32[32]{0:T(128)S(1)} all-reduce(f32[32]{0:T(128)S(1)} %fusion.13), channel_id=1, replica_groups=mesh['groups'=1,'gx'=4,'yz'=8] {'yz'}, use_global_device_ids=true, to_apply=%region_2.0 | all-reduce | flops 32 | bytes 256 | tf_op jit(solution)/shard_map/psum | solution.py:11
  26.3 0.9 fusion.15
  27.2 9.0 %all_gather.15 = bf16[128,1024]{1,0:T(8,128)(2,1)S(1)} all-gather(bf16[32,1024]{1,0:T(8,128)(2,1)S(1)} %fusion.15), channel_id=1, replica_groups=mesh['groups'=1,'gx'=4,'yz'=8] {'gx'}, dimensions={0}, use_global_device_ids=true | all-gather | bytes 327680 | tf_op jit(solution)/shard_map/all_gather | solution.py:18
  36.3 12.7 %fusion = bf16[4096,2,128]{0,2,1:T(8,128)(2,1)} fusion(bf16[2,4096,1024]{2,1,0:T(8,128)(2,1)} %param.22, bf16[128,1024]{1,0:T(8,128)(2,1)S(1)} %all_gather.15), kind=kOutput, calls=%fused_computation.3 | convolution fusion | flops 2148532224 | bytes 19136512 | tf_op jit(solution)/shard_map/rfz,uz->fru/dot_general | solution.py:63
  49.2 1.1 broadcast_select_fusion
  50.3 32.0 %reduce-scatter.5.cloned.1.call-done = bf16[512,2,128]{0,2,1:T(8,128)(2,1)} async-done(((bf16[4096,2,128]{0,2,1:T(8,128)(2,1)}), bf16[512,2,128]{0,2,1:T(8,128)(2,1)}) %reduce-scatter.5.cloned.1.call-update) | async-done | bytes 262160 | tf_op jit(solution)/shard_map/reduce_scatter | solution.py:22
  83.4 1.0 multiply_reduce_fusion.1
  84.4 1.1 copy.39
  86.3 1.0 convolution_bitcast_fusion
  88.2 1.7 copy.42
  89.9 122.4 %all-reduce.2.cloned.1.call-done = f32[544,128]{1,0:T(8,128)} async-done(((f32[544,128]{1,0:T(8,128)}), f32[544,128]{1,0:T(8,128)}) %all-reduce.2.cloned.1.call-update) | async-done | bytes 278544 | tf_op jit(solution)/shard_map/psum | solution.py:84
  212.4 2.2 compare_select_fusion
  214.6 1.8 copy.40
  217.1 5.8 %fusion.1 = (bf16[512,16,128]{2,1,0:T(8,128)(2,1)}, f32[512,128]{1,0:T(8,128)}) fusion(bf16[512,16,128]{2,1,0:T(8,128)(2,1)S(1)} %copy-done.2, f32[512,128]{1,0:T(8,128)} %copy.42, f32[16,128]{1,0:T(8,128)S(1)} %get-tuple-element.12, f32[512,16]{1,0:T(8,128)} %copy.41, f32[512,128]{1,0:T(8,128)} %copy.40, pred[128]{0:T(512)(128)(4,1)S(1)} %fusion.28, ...), kind=kLoop, calls=%fused_computation.7 | loop fusion | flops 10420224 | bytes 5030016 | tf_op jit(solution)/shard_map/convert_element_type | solution.py:101
  222.8 1.1 copy.43
  223.9 1.7 fusion.12
  225.7 23.2 %all-gather.2.cloned.1.call-done = bf16[4096,128]{0,1:T(8,128)(2,1)} async-done(((bf16[512,128]{0,1:T(8,128)(2,1)}), bf16[4096,128]{0,1:T(8,128)(2,1)}) %all-gather.2.cloned.1.call-update) | async-done | bytes 1048592 | tf_op jit(solution)/shard_map/all_gather | solution.py:106
  249.0 5.7 %convolution_convert_fusion.2 = bf16[128,1024]{1,0:T(8,128)(2,1)} fusion(bf16[4096,128]{0,1:T(8,128)(2,1)} %all-gather.2.cloned.1.call-done, bf16[4096,1024]{1,0:T(8,128)(2,1)} %param.33), kind=kOutput, calls=%fused_computation.8 | convolution fusion | flops 1073872896 | bytes 9699328 | tf_op jit(solution)/shard_map/dot_general | solution.py:105
  254.7 5.8 %copy.50 = bf16[128,8,2,1280]{3,1,2,0:T(8,128)(2,1)} copy(bf16[128,8,2,1280]{3,2,1,0:T(2,128)(2,1)} %bitcast.43) | data formatting | bytes 10485760
  260.5 18.0 %reduce-scatter.7.cloned.1.call-done = bf16[32,1024]{1,0:T(8,128)(2,1)} async-done(((bf16[128,1024]{1,0:T(8,128)(2,1)}), bf16[32,1024]{1,0:T(8,128)(2,1)}) %reduce-scatter.7.cloned.1.call-update) | async-done | bytes 65552 | tf_op jit(solution)/shard_map/reduce_scatter | solution.py:31
  278.5 1.0 fusion.17
  279.5 15.9 %psum.23 = f32[32]{0:T(128)S(1)} all-reduce(f32[32]{0:T(128)S(1)} %fusion.17), channel_id=1, replica_groups=mesh['groups'=1,'gx'=4,'yz'=8] {'yz'}, use_global_device_ids=true, to_apply=%region_10.11 | all-reduce | flops 32 | bytes 256 | tf_op jit(solution)/shard_map/psum | solution.py:11
  296.3 9.1 %all_gather.17 = bf16[128,1024]{1,0:T(8,128)(2,1)S(1)} all-gather(bf16[32,1024]{1,0:T(8,128)(2,1)S(1)} %fusion.19), channel_id=1, replica_groups=mesh['groups'=1,'gx'=4,'yz'=8] {'gx'}, dimensions={0}, use_global_device_ids=true | all-gather | bytes 327680 | tf_op jit(solution)/shard_map/all_gather | solution.py:18
  305.4 4.2 %convolution_convert_fusion.1 = bf16[128,2560]{1,0:T(8,128)(2,1)} fusion(bf16[128,1024]{1,0:T(8,128)(2,1)S(1)} %all_gather.17, bf16[1024,2560]{1,0:T(8,128)(2,1)} %bitcast.42), kind=kOutput, calls=%fused_computation.6 | convolution fusion | flops 671416320 | bytes 6160384 | tf_op jit(solution)/shard_map/dot_general | solution.py:125
  309.7 2.5 sort.17
  312.4 2.1 fusion.32
  314.5 23.8 %reduce-scatter.9.cloned.1.call-done = bf16[16,2560]{1,0:T(8,128)(2,1)} async-done(((bf16[128,2560]{1,0:T(8,128)(2,1)}), bf16[16,2560]{1,0:T(8,128)(2,1)}) %reduce-scatter.9.cloned.1.call-update) | async-done | bytes 81936 | tf_op jit(solution)/shard_map/reduce_scatter | solution.py:22
  338.3 15.6 %all_gather.18 = bf16[128,2560]{1,0:T(8,128)(2,1)S(1)} all-gather(bf16[16,2560]{1,0:T(8,128)(2,1)} %reduce-scatter.9.cloned.1.call-done), channel_id=1, replica_groups=mesh['groups'=1,'gx'=4,'yz'=8] {'yz'}, dimensions={0}, use_global_device_ids=true | all-gather | bytes 737280 | tf_op jit(solution)/shard_map/all_gather | solution.py:128
  356.1 15.0 %all_gather.19 = bf16[128,2048]{1,0:T(8,128)(2,1)S(1)} all-gather(bf16[16,2048]{1,0:T(8,128)(2,1)S(1)} %bitcast.44), channel_id=1, replica_groups=mesh['groups'=1,'gx'=4,'yz'=8] {'yz'}, dimensions={0}, use_global_device_ids=true | all-gather | bytes 589824 | tf_op jit(solution)/shard_map/all_gather | solution.py:165
  374.9 21.3 %reduce-scatter.11.cloned.1.call-done = bf16[32,1024]{1,0:T(8,128)(2,1)} async-done(((bf16[128,1024]{1,0:T(8,128)(2,1)}), bf16[32,1024]{1,0:T(8,128)(2,1)}) %reduce-scatter.11.cloned.1.call-update) | async-done | bytes 65552 | tf_op jit(solution)/shard_map/reduce_scatter | solution.py:31
  396.2 1.5 fusion.20
  (77 shorter events, 10.9 us)
Async XLA Ops:
  7.2 79.1 %copy-start = (bf16[512,544]{0,1:T(8,128)(2,1)S(1)}, bf16[512,544]{0,1:T(8,128)(2,1)}, u32[]{:S(2)}) copy-start(bf16[512,544]{0,1:T(8,128)(2,1)} %param.28) | copy-start | bytes 1671172
  7.2 75.1 %reduce-scatter.5.cloned.1.call-start = ((), (), s32[]{:S(2)}) async-start(), calls=%async_computation.4 | async-start | bytes 2359296 | tf_op jit(solution)/shard_map/reduce_scatter | solution.py:22
  36.2 12.8 %copy-start.14 = (s32[16]{0:T(128)S(1)}, s32[16]{0:T(128)}, u32[]{:S(2)}) copy-start(s32[16]{0:T(128)} %param.27) | copy-start | bytes 196
  36.3 47.1 %copy-start.7 = (f32[4,512]{1,0:T(4,128)S(1)}, f32[4,512]{1,0:T(4,128)}, u32[]{:S(2)}) copy-start(f32[4,512]{1,0:T(4,128)} %param.23) | copy-start | bytes 24580
  49.0 36.5 %copy-start.8 = (f32[512]{0:T(512)S(1)}, f32[512]{0:T(512)}, u32[]{:S(2)}) copy-start(f32[512]{0:T(512)} %param.24) | copy-start | bytes 6148
  49.0 38.4 %copy-start.6 = (f32[16,512]{1,0:T(8,128)S(1)}, f32[16,512]{1,0:T(8,128)}, u32[]{:S(2)}) copy-start(f32[16,512]{1,0:T(8,128)} %param.31) | copy-start | bytes 98308
  49.0 163.4 %copy-start.10 = (f32[512]{0:T(512)S(1)}, f32[512]{0:T(512)}, u32[]{:S(2)}) copy-start(f32[512]{0:T(512)} %param.30) | copy-start | bytes 6148
  49.0 168.1 %copy-start.2 = (bf16[512,16,128]{2,1,0:T(8,128)(2,1)S(1)}, bf16[512,16,128]{2,1,0:T(8,128)(2,1)}, u32[]{:S(2)}) copy-start(bf16[512,16,128]{2,1,0:T(8,128)(2,1)} %param.26) | copy-start | bytes 6291460
  49.0 163.3 %all-reduce.2.cloned.1.call-start = ((), (), s32[]{:S(2)}) async-start(), calls=%async_computation.5 | async-start | bytes 557056 | tf_op jit(solution)/shard_map/psum | solution.py:84
  85.6 0.7 copy-start.4
  87.3 136.6 %copy-start.11 = (f32[512]{0:T(512)S(1)}, f32[512]{0:T(512)}, u32[]{:S(2)}) copy-start(f32[512]{0:T(512)} %param.32) | copy-start | bytes 6148
  87.3 161.7 %all-gather.2.cloned.1.call-start = ((), (), s32[]{:S(2)}) async-start(), calls=%async_computation.6 | async-start | bytes 1179648 | tf_op jit(solution)/shard_map/all_gather | solution.py:106
  225.7 52.9 %reduce-scatter.7.cloned.1.call-start = ((), (), s32[]{:S(2)}) async-start(), calls=%async_computation.7 | async-start | bytes 327680 | tf_op jit(solution)/shard_map/reduce_scatter | solution.py:31
  254.7 83.7 %reduce-scatter.9.cloned.1.call-start = ((), (), s32[]{:S(2)}) async-start(), calls=%async_computation.8 | async-start | bytes 737280 | tf_op jit(solution)/shard_map/reduce_scatter | solution.py:22
  254.7 23.8 %copy-start.3 = (bf16[32,1024]{1,0:T(8,128)(2,1)S(1)}, bf16[32,1024]{1,0:T(8,128)(2,1)}, u32[]{:S(2)}) copy-start(bf16[32,1024]{1,0:T(8,128)(2,1)} %param.20) | copy-start | bytes 196612
  254.7 40.7 %copy-start.9 = (f32[1024]{0:T(1024)S(1)}, f32[1024]{0:T(1024)}, u32[]{:S(2)}) copy-start(f32[1024]{0:T(1024)} %param.34) | copy-start | bytes 12292
  260.5 49.2 %copy-start.13 = (s32[128]{0:T(128)S(1)}, s32[128]{0:T(128)}, u32[]{:S(2)}) copy-start(s32[128]{0:T(128)} %param.39) | copy-start | bytes 1540
  260.5 51.9 %copy-start.12 = (s32[16]{0:T(128)S(1)}, s32[16]{0:T(128)}, u32[]{:S(2)}) copy-start(s32[16]{0:T(128)} %param.38) | copy-start | bytes 196
  309.6 86.6 %reduce-scatter.11.cloned.1.call-start = ((), (), s32[]{:S(2)}) async-start(), calls=%async_computation.9 | async-start | bytes 327680 | tf_op jit(solution)/shard_map/reduce_scatter | solution.py:31
  354.9 16.2 %copy-start.1 = (bf16[2048,1024]{1,0:T(8,128)(2,1)S(1)}, bf16[2048,1024]{1,0:T(8,128)(2,1)}, u32[]{:S(2)}) copy-start(bf16[2048,1024]{1,0:T(8,128)(2,1)} %param.36) | copy-start | bytes 12582916
  371.1 25.1 %copy-start.5 = (bf16[32,1024]{1,0:T(8,128)(2,1)S(1)}, bf16[32,1024]{1,0:T(8,128)(2,1)}, u32[]{:S(2)}) copy-start(bf16[32,1024]{1,0:T(8,128)(2,1)} %reduce-scatter.7.cloned.1.call-done) | copy-start | bytes 196612
Sparse Core Ops, SparseCore 0:
  49.1 33.1 reduce-scatter.4
  88.3 124.0 all-reduce.1
  225.8 23.1 all-gather.1
  254.8 23.7 reduce-scatter.6
  309.7 28.5 reduce-scatter.8
  373.7 22.4 reduce-scatter.10
where the time goes:
time: 405 us
  waiting for transfers between devices  241 us (60%)
  blocking collectives  82.6 us (20%)
  matrix products  27.5 us (7%)
  other arithmetic  19.9 us (5%)
  local copies, waits for them, and re-layouts  19 us (5%)
  between operations  14.4 us (4%)
    psum x1, waiting for transfers between devices, on_device(): proj = lax.psum(partial_value, ('gx', 'yz'))  122 us
    reduce_scatter x2, waiting for transfers between devices, owner_sum(): lax.psum_scatter(term_fn(jnp.int32(0), owned_rows * lax.axis_size('yz'))....  55.8 us
    reduce_scatter x2, waiting for transfers between devices, to_rows(): lax.psum_scatter(partial_value.astype(jnp.bfloat16), 'gx', scatter_dimens...  39.3 us
    psum x2, blocking collectives, normalize(): squares = lax.psum(jnp.sum(wide * wide, axis=1), 'yz')  33.9 us
    all_gather x1, waiting for transfers between devices, on_device(): lax.all_gather(gated, 'yz', axis=0, tiled=True)  23.2 us
    all_gather x2, blocking collectives, spread(): return lax.all_gather(values, 'gx', axis=0, tiled=True)  18.1 us
    all_gather x1, blocking collectives, on_device(): every_row = lax.all_gather(block_rows, 'yz', axis=0, tiled=True)  15.6 us
    all_gather x1, blocking collectives, on_device(): lax.all_gather(heads, 'yz', axis=0, tiled=True)  15 us
  transfers between devices with their start and end apart: 6, of which 6 were waited for; matrix products, arithmetic and copies ran while one was open for 4% of the time, Pallas kernels for 0%

commit v1 on v0

v1 whole, which is shorter than its diff:
```python
import math

import jax
import jax.numpy as jnp
from jax import lax
from jax.sharding import PartitionSpec as P

F32 = jnp.float32
BF16 = jnp.bfloat16


def swap(value, axis, bits):
    size = lax.axis_size(axis)
    return lax.ppermute(value, axis, [(i, i ^ bits) for i in range(size)])


def pick(stack, index):
    return lax.dynamic_index_in_dim(stack, index, 0, keepdims=False)


def gather_gx(value):
    size = lax.axis_size("gx")
    me = lax.axis_index("gx")
    got = jnp.stack([value] + [swap(value, "gx", k) for k in range(1, size)])
    return jnp.take(got, me ^ jnp.arange(size), axis=0)


def scatter_gx(pieces):
    size = lax.axis_size("gx")
    me = lax.axis_index("gx")
    wire = pieces.astype(BF16)
    got = [swap(pick(wire, me ^ k), "gx", k) for k in range(1, size)]
    total = pick(wire, me).astype(F32)
    for term in got:
        total = total + term.astype(F32)
    return total


def scatter_yz(pieces):
    size = lax.axis_size("yz")
    chips = size // 2
    me = lax.axis_index("yz")
    core, chip = me % 2, me // 2
    pairs = pieces.reshape((chips, 2) + pieces.shape[1:])
    keep = lax.dynamic_index_in_dim(pairs, core, 1, keepdims=False)
    give = lax.dynamic_index_in_dim(pairs, 1 - core, 1, keepdims=False)
    summed = keep.astype(F32) + swap(give.astype(BF16), "yz", 1).astype(F32)
    wire = summed.astype(BF16)
    got = [swap(pick(wire, chip ^ k), "yz", 2 * k) for k in range(1, chips)]
    total = pick(summed, chip)
    for term in got:
        total = total + term.astype(F32)
    return total


def gather_yz(value):
    size = lax.axis_size("yz")
    chips = size // 2
    me = lax.axis_index("yz")
    mine = [value] + [swap(value, "yz", 2 * k) for k in range(1, chips)]
    other = [swap(v, "yz", 1) for v in mine]
    got = jnp.stack([v for pair in zip(mine, other) for v in pair])
    return jnp.take(got, me ^ jnp.arange(size), axis=0)


def sum_all(value):
    rows = value.shape[0]
    core = lax.axis_index("yz") % 2
    halves = value.reshape(2, rows // 2, value.shape[1])
    half = pick(halves, core) + swap(pick(halves, 1 - core).astype(BF16), "yz", 1).astype(F32)
    wire = half.astype(BF16)
    for k in range(1, lax.axis_size("gx")):
        half = half + swap(wire, "gx", k).astype(F32)
    wire = half.astype(BF16)
    for k in range(1, lax.axis_size("yz") // 2):
        half = half + swap(wire, "yz", 2 * k).astype(F32)
    wire = half.astype(BF16)
    other = swap(wire, "yz", 1)
    pair = jnp.stack([wire, other])
    return jnp.concatenate([pick(pair, core), pick(pair, 1 - core)], axis=0).astype(F32)


def on_device(
    hidden_in,
    norm_gain_a,
    mixer_projection,
    conv_weight,
    conv_bias,
    conv_state,
    ssm_state,
    reset_ids,
    x_proj,
    dt_proj,
    dt_bias,
    a_log,
    d_skip,
    mixer_output,
    norm_gain_b,
    attention_projection,
    head_output,
    kv_cache,
    lengths,
    assign,
):
    batch = assign.shape[0]
    yz = lax.axis_size("yz")
    gx = lax.axis_size("gx")
    width = hidden_in.shape[1]
    whole_width = width * yz

    rows_in = gather_gx(hidden_in).reshape(batch, width).astype(F32)
    squares = jnp.sum(rows_in * rows_in, axis=1)
    gained = (rows_in * norm_gain_a[None, :]).astype(BF16)
    channels = mixer_projection.shape[1]
    own = channels // yz

    def project(part):
        return lax.dot_general(
            mixer_projection[part], gained, (((1,), (1,)), ((), ())), preferred_element_type=F32
        ).reshape(yz, own, batch)

    extra = jnp.broadcast_to(squares[None, None, :], (yz, 16, batch))
    xsum = scatter_yz(jnp.concatenate([project(0), extra], axis=1))
    scale = lax.rsqrt(xsum[own] / whole_width + 1e-05)
    xval = (xsum[:own] * scale[None, :]).astype(BF16)
    zval = (scatter_yz(project(1)) * scale[None, :]).astype(BF16)

    reset = jnp.any(reset_ids[:, None] == jnp.arange(batch, dtype=jnp.int32)[None, :], axis=0)
    conv_old = jnp.where(reset[None, None, :], jnp.zeros_like(conv_state), conv_state)
    window = jnp.concatenate([conv_old, xval[:, None, :]], axis=1)
    conv_new = window[:, 1:, :]
    mixed_conv = (
        jnp.sum(jnp.transpose(conv_weight)[:, :, None] * window.astype(F32), axis=1)
        + conv_bias[:, None]
    )
    activated = jax.nn.silu(mixed_conv).astype(BF16)
    proj = sum_all(
        lax.dot_general(
            x_proj, activated, (((0,), (0,)), ((), ())), preferred_element_type=F32
        )
    )
    rank = dt_proj.shape[0]
    nstate = a_log.shape[0]
    dt_low = proj[:rank].astype(BF16)
    bmat = proj[rank : rank + nstate]
    cmat = proj[rank + nstate :]
    step_pre = lax.dot_general(
        dt_proj, dt_low, (((0,), (0,)), ((), ())), preferred_element_type=F32
    )
    step = jax.nn.softplus(step_pre + dt_bias[:, None])
    rates = -jnp.exp(jnp.transpose(a_log))
    old = jnp.where(reset[None, None, :], jnp.zeros((), F32), ssm_state.astype(F32))
    act_wide = activated.astype(F32)
    state = (
        jnp.exp(step[:, None, :] * rates[:, :, None]) * old
        + step[:, None, :] * bmat[None, :, :] * act_wide[:, None, :]
    )
    ssm_new = state.astype(BF16)
    yval = jnp.sum(state * cmat[None, :, :], axis=1) + d_skip[:, None] * act_wide
    gated = (yval * jax.nn.silu(zval.astype(F32))).astype(BF16)

    mixed = lax.dot_general(
        gather_yz(gated).reshape(channels, batch),
        mixer_output,
        (((0,), (0,)), ((), ())),
        preferred_element_type=F32,
    )
    first_out = (
        hidden_in.astype(F32) + scatter_gx(mixed.reshape(gx, batch // gx, width))
    ).astype(BF16)

    first_all = gather_gx(first_out).reshape(batch, width)
    chosen = assign[:, None] == jnp.arange(batch, dtype=jnp.int32)[None, :]
    by_slot = jnp.dot(chosen.astype(BF16), first_all, preferred_element_type=F32)
    squares = jnp.sum(by_slot * by_slot, axis=1)
    gained = (by_slot * norm_gain_b[None, :]).astype(BF16)
    group_count = attention_projection.shape[1]
    group_cols = attention_projection.shape[2]
    flattened = attention_projection.reshape(width, group_count * group_cols)
    slot_count = kv_cache.shape[0]
    entries = jnp.dot(gained, flattened, preferred_element_type=F32)
    extra = jnp.broadcast_to(squares[:, None], (batch, 128))
    entries = jnp.concatenate([entries, extra], axis=1).reshape(yz, slot_count, -1)
    entries = scatter_yz(entries)
    scale = lax.rsqrt(entries[:, -1:] / whole_width + 1e-05)
    newest_entry = (entries[:, :-128] * scale).astype(BF16)
    newest_entry = newest_entry.reshape(slot_count, group_count, group_cols)
    head_dim = kv_cache.shape[3] // 2
    per_group = group_cols // head_dim - 2
    fresh_kv = newest_entry[:, :, per_group * head_dim :]
    query_vector = newest_entry[:, :, : per_group * head_dim].reshape(
        slot_count, group_count, per_group, head_dim
    )
    key_new = newest_entry[:, :, per_group * head_dim : (per_group + 1) * head_dim]
    value_new = newest_entry[:, :, (per_group + 1) * head_dim :]
    keys = kv_cache[..., :head_dim]
    values = kv_cache[..., head_dim:]
    factor = 1.0 / math.sqrt(head_dim)
    scores = (
        jnp.einsum("sghd,stgd->sght", query_vector, keys, preferred_element_type=F32) * factor
    )
    own_score = (
        jnp.einsum("sghd,sgd->sgh", query_vector, key_new, preferred_element_type=F32) * factor
    )
    positions = jnp.arange(kv_cache.shape[1], dtype=jnp.int32)
    valid = (positions[None, :] < lengths[:, None])[:, None, None, :]
    top = jnp.maximum(jnp.max(jnp.where(valid, scores, -1e30), axis=-1), own_score)
    expo = jnp.where(valid, jnp.exp(scores - top[..., None]), 0.0)
    expo_own = jnp.exp(own_score - top)
    total = jnp.sum(expo, axis=-1) + expo_own
    weights = (expo / total[..., None]).astype(BF16)
    weight_own = (expo_own / total).astype(BF16)
    attended = jnp.einsum("sght,stgd->sghd", weights, values, preferred_element_type=F32)
    attended = (
        attended + weight_own.astype(F32)[..., None] * value_new.astype(F32)[:, :, None, :]
    )
    heads = attended.astype(BF16).reshape(slot_count, group_count * per_group * head_dim)
    heads_all = gather_yz(heads).reshape(batch, -1)
    by_request = lax.dot_general(
        chosen.astype(BF16), heads_all, (((0,), (0,)), ((), ())), preferred_element_type=F32
    ).astype(BF16)
    second = jnp.dot(by_request, head_output, preferred_element_type=F32)
    hidden_out = (
        first_out.astype(F32) + scatter_gx(second.reshape(gx, batch // gx, width))
    ).astype(BF16)
    return (hidden_out, ssm_new, conv_new, fresh_kv)


def solution(mesh):
    placed = (
        P(("groups", "gx"), "yz"),
        P("yz"),
        P(None, "gx", "yz"),
        P(None, ("gx", "yz")),
        P(("gx", "yz")),
        P(("gx", "yz"), None, "groups"),
        P(("gx", "yz"), None, "groups"),
        P("groups"),
        P(("gx", "yz"), None),
        P(None, ("gx", "yz")),
        P(("gx", "yz")),
        P(None, ("gx", "yz")),
        P(("gx", "yz")),
        P("gx", "yz"),
        P("yz"),
        P("yz", "gx", None),
        P("gx", "yz"),
        P(("groups", "yz"), None, "gx", None),
        P(("groups", "yz")),
        P("groups"),
    )
    return jax.shard_map(
        on_device,
        mesh=mesh,
        in_specs=placed,
        out_specs=(
            P(("groups", "gx"), "yz"),
            P(("gx", "yz"), None, "groups"),
            P(("gx", "yz"), None, "groups"),
            P(("groups", "yz"), "gx", None),
        ),
        check_vma=False,
    )
```

time: 405 us -> 178 us (0.44)
  waiting for transfers between devices: 241 us -> 41.2 us
  blocking collectives: 82.6 us -> 0 us
  starting transfers between devices: 0.25 us -> 48.8 us
  local copies, waits for them, and re-layouts: 19 us -> 36.4 us
  between operations: 14.4 us -> 1.42 us
    psum x1 -> x0, waiting for transfers between devices: 122 us -> none  [on_device(): proj = lax.psum(partial_value, ('gx', 'yz'))]
    reduce_scatter x4 -> x0, waiting for transfers between devices: 95.1 us -> none  [the longest x2 55.8 us: owner_sum(): lax.psum_scatter(term_fn(jnp.int32(0), owned_rows * lax.axis_size('yz'))....]
    ppermute x0 -> x46, starting transfers between devices: none -> 48.8 us  [swap(): return lax.ppermute(value, axis, [(i, i ^ bits) for i in range(size)])]
    all_gather x4 -> x0, blocking collectives: 48.7 us -> none  [the longest x2 18.1 us: spread(): return lax.all_gather(values, 'gx', axis=0, tiled=True)]
    ppermute x0 -> x46, waiting for transfers between devices: none -> 41.2 us  [swap(): return lax.ppermute(value, axis, [(i, i ^ bits) for i in range(size)])]
    psum x2 -> x0, blocking collectives: 33.9 us -> none  [normalize(): squares = lax.psum(jnp.sum(wide * wide, axis=1), 'yz')]
    all_gather x1 -> x0, waiting for transfers between devices: 23.2 us -> none  [on_device(): lax.all_gather(gated, 'yz', axis=0, tiled=True)]
    dynamic_slice x0 -> x3, local copies, waits for them, and re-layouts: none -> 6.41 us  [the longest x2 4.38 us: scatter_yz(): keep = lax.dynamic_index_in_dim(pairs, core, 1, keepdims=False)]
  transfers between devices with their start and end apart: 6 -> 46, of which waited for: 6 -> 20; matrix products, arithmetic and copies ran while one was open for 4% -> 23% of each run, Pallas kernels for 0% -> 0%
where the time goes in v1:
time: 178 us; the launch traced here: 177 us
  starting transfers between devices  48.8 us (27%)
  waiting for transfers between devices  41.2 us (23%)
  local copies, waits for them, and re-layouts  36.4 us (20%)
  matrix products  27 us (15%)
  other arithmetic  22.4 us (13%)
    ppermute x46, starting transfers between devices, swap(): return lax.ppermute(value, axis, [(i, i ^ bits) for i in range(size)])  48.8 us
    ppermute x46, waiting for transfers between devices, swap(): return lax.ppermute(value, axis, [(i, i ^ bits) for i in range(size)])  41.2 us
    dot_general x2, matrix products, project(): lax.dot_general(mixer_projection[part], gained, (((1,), (1,)), ((), ())),...  13.8 us
    unnamed x58, local copies, waits for them, and re-layouts  12.7 us
    concatenate x2, local copies, waits for them, and re-layouts, on_device(): xsum = scatter_yz(jnp.concatenate([project(0), extra], axis=1))  5.71 us
    convert_element_type x1, other arithmetic, on_device(): ssm_new = state.astype(BF16)  5.04 us
    dot_general x1, matrix products, on_device(): lax.dot_general(gather_yz(gated).reshape(channels, batch), mixer_output,...  4.67 us
    dynamic_slice x2, local copies, waits for them, and re-layouts, scatter_yz(): keep = lax.dynamic_index_in_dim(pairs, core, 1, keepdims=False)  4.38 us
  transfers between devices with their start and end apart: 46, of which 20 were waited for; matrix products, arithmetic and copies ran while one was open for 23% of the time, Pallas kernels for 0%

profile of v1, /device:TPU:0, one launch (start us, length us, event | category | flops | bytes accessed | tf_op | source)
XLA Modules:
  0.0 177.1 jit_solution(8718679322732871822)
XLA Ops:
  0.6 3.0 %collective-permute-start = (bf16[32,1024]{1,0:T(8,128)(2,1)}, bf16[32,1024]{1,0:T(8,128)(2,1)S(1)}, u32[]{:S(2)}, u32[]{:S(2)}) collective-permute-start(bf16[32,1024]{1,0:T(8,128)(2,1)} %param.22), channel_id=1, source_target_pairs={{0,8},{8,0},{16,24},{24,16},{1,9},{9,1},{17,25},{25,17},{2,10},{10... | collective-permute-start | bytes 196616 | tf_op jit(solution)/shard_map/ppermute | solution.py:14
  8.1 2.4 %collective-permute-done.2 = bf16[32,1024]{1,0:T(8,128)(2,1)S(1)} collective-permute-done((bf16[32,1024]{1,0:T(8,128)(2,1)}, bf16[32,1024]{1,0:T(8,128)(2,1)S(1)}, u32[]{:S(2)}, u32[]{:S(2)}) %collective-permute-start.2) | collective-permute-done | bytes 65568 | tf_op jit(solution)/shard_map/ppermute | solution.py:14
  13.6 6.2 %fusion.8 = f32[4096,128]{0,1:T(8,128)S(1)} fusion(bf16[128,1024]{1,0:T(8,128)(2,1)S(1)} %bitcast.224, bf16[2,4096,1024]{2,1,0:T(8,128)(2,1)} %param.24), kind=kOutput, calls=%fused_computation.12 | convolution fusion | flops 1073741824 | bytes 10747904 | tf_op jit(solution)/shard_map/dot_general | solution.py:118
  19.9 3.0 %concatenate.15 = f32[4,2,512,128]{2,1,0,3:T(2,128)} reshape(f32[4096,128]{0,1:T(8,128)S(1)} %fusion.8) | data formatting | bytes 4194304 | tf_op jit(solution)/shard_map/concatenate | solution.py:123
  22.9 2.8 %copy.71 = f32[4,2,512,128]{3,2,0,1:T(8,128)S(1)} copy(f32[4,2,512,128]{2,1,0,3:T(2,128)} %concatenate.15) | data formatting | bytes 4194304 | tf_op jit(solution)/shard_map/concatenate | solution.py:123
  31.3 2.6 %collective-permute-start.5 = (bf16[528,128]{1,0:T(8,128)(2,1)}, bf16[528,128]{1,0:T(8,128)(2,1)S(1)}, u32[]{:S(2)}, u32[]{:S(2)}) collective-permute-start(bf16[528,128]{1,0:T(8,128)(2,1)} %get-tuple-element.23), channel_id=1, source_target_pairs={{0,4},{1,5},{2,6},{3,7},{4,0},{5,1},{6,2},{7,3},{8,12},{9,13},{10,... | collective-permute-start | bytes 405512 | tf_op jit(solution)/shard_map/ppermute | solution.py:14
  34.1 7.6 %fusion.11 = f32[4096,128]{0,1:T(8,128)} fusion(bf16[128,1024]{1,0:T(8,128)(2,1)S(1)} %bitcast.225, bf16[2,4096,1024]{2,1,0:T(8,128)(2,1)} %param.24), kind=kOutput, calls=%fused_computation.13 | convolution fusion | flops 1073741824 | bytes 10747904 | tf_op jit(solution)/shard_map/dot_general | solution.py:118
  41.7 3.1 %reshape_reshape.6 = f32[4,2,512,128]{2,1,0,3:T(2,128)S(1)} reshape(f32[4096,128]{0,1:T(8,128)} %fusion.11) | data formatting | bytes 4194304 | tf_op jit(solution)/shard_map/reshape;reshape | solution.py:44
  50.1 2.0 %constant_dynamic-slice_fusion = bf16[4,1,512,128]{2,1,0,3:T(2,128)(2,1)} fusion(f32[4,2,512,128]{2,1,0,3:T(2,128)S(1)} %reshape_reshape.6, s32[]{:T(128)S(6)} %select_n.139), kind=kLoop, calls=%fused_computation.168 | loop fusion | bytes 1048580 | tf_op jit(solution)/shard_map/jit(dynamic_index_in_dim)/dynamic_slice | solution.py:46
  52.2 2.4 %copy.81 = bf16[4,1,512,128]{3,2,0,1:T(8,128)(2,1)S(1)} copy(bf16[4,1,512,128]{2,1,0,3:T(2,128)(2,1)} %constant_dynamic-slice_fusion) | data formatting | bytes 1048576
  59.3 2.0 %constant_dynamic-slice_fusion.1 = f32[4,1,512,128]{2,1,0,3:T(1,128)} fusion(f32[4,2,512,128]{2,1,0,3:T(2,128)S(1)} %reshape_reshape.6, s32[]{:T(128)S(6)} %select_n.138), kind=kLoop, calls=%fused_computation.169 | loop fusion | bytes 2097156 | tf_op jit(solution)/shard_map/jit(dynamic_index_in_dim)/dynamic_slice | solution.py:45
  61.3 2.3 %copy.74 = f32[4,1,512,128]{3,2,0,1:T(8,128)S(1)} copy(f32[4,1,512,128]{2,1,0,3:T(1,128)} %constant_dynamic-slice_fusion.1) | data formatting | bytes 2097152 | tf_op jit(solution)/shard_map/jit(dynamic_index_in_dim)/dynamic_slice | solution.py:45
  66.4 2.5 %collective-permute-start.12 = (bf16[272,128]{1,0:T(8,128)(2,1)S(1)}, bf16[272,128]{1,0:T(8,128)(2,1)S(1)}, u32[]{:S(2)}, u32[]{:S(2)}) collective-permute-start(bf16[272,128]{1,0:T(8,128)(2,1)S(1)} %get-tuple-element.13), channel_id=1, source_target_pairs={{0,4},{1,5},{2,6},{3,7},{4,0},{5,1},{6,2},{7,3},{8,12},{9,13},{10,... | collective-permute-start | bytes 208904 | tf_op jit(solution)/shard_map/ppermute | solution.py:14
  69.2 2.2 %fusion.94 = (bf16[4,512,128]{2,1,0:T(8,128)(2,1)S(1)}, f32[4,512,128]{2,1,0:T(8,128)}) fusion(bf16[4,512,128]{2,1,0:T(8,128)(2,1)} %collective-permute-done.15, f32[4,1,512,128]{3,2,0,1:T(8,128)S(1)} %copy.74), kind=kLoop, calls=%fused_computation.197 | loop fusion | flops 786432 | bytes 3145728 | tf_op jit(solution)/shard_map/convert_element_type | solution.py:48
  71.4 1.9 %collective-permute-done.12 = bf16[272,128]{1,0:T(8,128)(2,1)S(1)} collective-permute-done((bf16[272,128]{1,0:T(8,128)(2,1)S(1)}, bf16[272,128]{1,0:T(8,128)(2,1)S(1)}, u32[]{:S(2)}, u32[]{:S(2)}) %collective-permute-start.12) | collective-permute-done | bytes 69664 | tf_op jit(solution)/shard_map/ppermute | solution.py:14
  76.0 2.0 %collective-permute-start.17 = (bf16[512,128]{1,0:T(8,128)(2,1)}, bf16[512,128]{1,0:T(8,128)(2,1)}, u32[]{:S(2)}, u32[]{:S(2)}) collective-permute-start(bf16[512,128]{1,0:T(8,128)(2,1)} %get-tuple-element.26), channel_id=1, source_target_pairs={{0,4},{1,5},{2,6},{3,7},{4,0},{5,1},{6,2},{7,3},{8,12},{9,13},{10,... | collective-permute-start | bytes 393224 | tf_op jit(solution)/shard_map/ppermute | solution.py:14
  78.0 2.4 %collective-permute-start.18 = (bf16[512,128]{1,0:T(8,128)(2,1)}, bf16[512,128]{1,0:T(8,128)(2,1)}, u32[]{:S(2)}, u32[]{:S(2)}) collective-permute-start(bf16[512,128]{1,0:T(8,128)(2,1)} %get-tuple-element.25), channel_id=1, source_target_pairs={{0,6},{1,7},{2,4},{3,5},{4,2},{5,3},{6,0},{7,1},{8,14},{9,15},{10,... | collective-permute-start | bytes 393224 | tf_op jit(solution)/shard_map/ppermute | solution.py:14
  81.1 5.0 %fusion.14 = (bf16[512,16,128]{2,1,0:T(8,128)(2,1)}, f32[512,128]{1,0:T(8,128)S(1)}) fusion(bf16[512,16,128]{2,1,0:T(8,128)(2,1)S(1)} %copy-done.2, f32[512,128]{1,0:T(8,128)} %get-tuple-element.11, f32[16,128]{1,0:T(8,128)S(1)} %get-tuple-element.30, f32[512,16]{1,0:T(8,128)} %copy.73, f32[512,128]{1,0:T(8,128)S(1)} %copy.72, pred[128]{0:T(512)(128)(4,1)S(1)} %fusion.83, ...), kind=kLoop, calls=%fused_computation.16 | loop fusion | flops 10420224 | bytes 5030016 | tf_op jit(solution)/shard_map/convert_element_type | solution.py:158
  86.1 3.1 %collective-permute-done.17 = bf16[512,128]{1,0:T(8,128)(2,1)} collective-permute-done((bf16[512,128]{1,0:T(8,128)(2,1)}, bf16[512,128]{1,0:T(8,128)(2,1)}, u32[]{:S(2)}, u32[]{:S(2)}) %collective-permute-start.17) | collective-permute-done | bytes 131104 | tf_op jit(solution)/shard_map/ppermute | solution.py:14
  90.6 3.0 %collective-permute-start.20 = (bf16[512,128]{1,0:T(8,128)(2,1)S(1)}, bf16[512,128]{1,0:T(8,128)(2,1)S(1)}, u32[]{:S(2)}, u32[]{:S(2)}) collective-permute-start(bf16[512,128]{1,0:T(8,128)(2,1)S(1)} %get-tuple-element.8), channel_id=1, source_target_pairs={{0,2},{1,3},{2,0},{3,1},{4,6},{5,7},{6,4},{7,5},{8,10},{9,11},{10,... | collective-permute-start | bytes 393224 | tf_op jit(solution)/shard_map/ppermute | solution.py:14
  96.1 3.8 %collective-permute-done.20 = bf16[512,128]{1,0:T(8,128)(2,1)S(1)} collective-permute-done((bf16[512,128]{1,0:T(8,128)(2,1)S(1)}, bf16[512,128]{1,0:T(8,128)(2,1)S(1)}, u32[]{:S(2)}, u32[]{:S(2)}) %collective-permute-start.20) | collective-permute-done | bytes 131104 | tf_op jit(solution)/shard_map/ppermute | solution.py:14
  99.9 6.6 %collective-permute-done.22 = bf16[512,128]{1,0:T(8,128)(2,1)S(1)} collective-permute-done((bf16[512,128]{1,0:T(8,128)(2,1)S(1)}, bf16[512,128]{1,0:T(8,128)(2,1)S(1)}, u32[]{:S(2)}, u32[]{:S(2)}) %collective-permute-start.22) | collective-permute-done | bytes 131104 | tf_op jit(solution)/shard_map/ppermute | solution.py:14
  108.8 2.4 %bitcast_select_fusion = bf16[4096,128]{1,0:T(8,128)(2,1)S(1)} fusion(bf16[8,512,128]{2,1,0:T(8,128)(2,1)S(1)} %gather_fusion, pred[4096]{0:T(1024)(128)(4,1)S(1)} %bitcast.241), kind=kLoop, calls=%fused_computation.36 | loop fusion | flops 524288 | bytes 2101248 | tf_op jit(solution)/shard_map/jit(_take)/select_n | solution.py:63
  111.8 4.7 %fusion.16 = bf16[4,32,1024]{2,1,0:T(8,128)(2,1)S(1)} fusion(bf16[4,32,4096]{2,1,0:T(8,128)(2,1)S(1)} %bitcast.211, bf16[4096,1024]{1,0:T(8,128)(2,1)} %param.35), kind=kOutput, calls=%fused_computation.24 | convolution fusion | flops 1073872896 | bytes 9699328 | tf_op jit(solution)/shard_map/dot_general | solution.py:162
  117.6 2.5 %collective-permute-start.28 = (bf16[32,1024]{1,0:T(8,128)(2,1)S(1)}, bf16[32,1024]{1,0:T(8,128)(2,1)S(1)}, u32[]{:S(2)}, u32[]{:S(2)}) collective-permute-start(bf16[32,1024]{1,0:T(8,128)(2,1)S(1)} %get-tuple-element.38), channel_id=1, source_target_pairs={{0,24},{8,16},{16,8},{24,0},{1,25},{9,17},{17,9},{25,1},{2,26},{10... | collective-permute-start | bytes 196616 | tf_op jit(solution)/shard_map/ppermute | solution.py:14
  126.3 5.8 %copy.85 = bf16[128,8,2,1280]{3,1,2,0:T(8,128)(2,1)} copy(bf16[128,8,2,1280]{3,2,1,0:T(2,128)(2,1)} %bitcast.210) | data formatting | bytes 10485760
  133.2 3.3 %fusion.40 = f32[128,2560]{1,0:T(8,128)S(1)} fusion(bf16[1024,2560]{1,0:T(8,128)(2,1)} %bitcast.209, f32[128,1024]{1,0:T(8,128)S(1)} %get-tuple-element.47, f32[1024]{0:T(1024)S(1)} %copy-done.13), kind=kOutput, calls=%fused_computation.68 | convolution fusion | flops 671350784 | bytes 7081984 | tf_op jit(solution)/shard_map/dot_general | solution.py:181
  139.0 2.5 %collective-permute-start.33 = (bf16[16,2688]{1,0:T(8,128)(2,1)S(1)}, bf16[16,2688]{1,0:T(8,128)(2,1)S(1)}, u32[]{:S(2)}, u32[]{:S(2)}) collective-permute-start(bf16[16,2688]{1,0:T(8,128)(2,1)S(1)} %get-tuple-element.27), channel_id=1, source_target_pairs={{0,2},{1,3},{2,0},{3,1},{4,6},{5,7},{6,4},{7,5},{8,10},{9,11},{10,... | collective-permute-start | bytes 258056 | tf_op jit(solution)/shard_map/ppermute | solution.py:14
  144.4 6.5 %collective-permute-done.34 = bf16[16,2688]{1,0:T(8,128)(2,1)S(1)} collective-permute-done((bf16[16,2688]{1,0:T(8,128)(2,1)S(1)}, bf16[16,2688]{1,0:T(8,128)(2,1)S(1)}, u32[]{:S(2)}, u32[]{:S(2)}) %collective-permute-start.34) | collective-permute-done | bytes 86048 | tf_op jit(solution)/shard_map/ppermute | solution.py:14
  157.4 5.4 %collective-permute-done.39 = bf16[16,2048]{1,0:T(8,128)(2,1)S(1)} collective-permute-done((bf16[16,2048]{1,0:T(8,128)(2,1)S(1)}, bf16[16,2048]{1,0:T(8,128)(2,1)S(1)}, u32[]{:S(2)}, u32[]{:S(2)}) %collective-permute-start.39) | collective-permute-done | bytes 65568 | tf_op jit(solution)/shard_map/ppermute | solution.py:14
  165.0 3.2 %fusion.19 = bf16[128,1024]{1,0:T(8,128)(2,1)S(1)} fusion(bf16[2048,1024]{1,0:T(8,128)(2,1)} %param.38, bf16[128,2048]{1,0:T(8,128)(2,1)S(1)} %bitcast_select_fusion.1, s32[128]{0:T(128)S(1)} %copy-done.16), kind=kOutput, calls=%fused_computation.25 | convolution fusion | flops 604389376 | bytes 4981248 | tf_op jit(solution)/shard_map/dot_general | solution.py:222
  174.0 2.4 %collective-permute-done.45 = bf16[32,1024]{1,0:T(8,128)(2,1)S(1)} collective-permute-done((bf16[32,1024]{1,0:T(8,128)(2,1)S(1)}, bf16[32,1024]{1,0:T(8,128)(2,1)S(1)}, u32[]{:S(2)}, u32[]{:S(2)}) %collective-permute-start.45) | collective-permute-done | bytes 65568 | tf_op jit(solution)/shard_map/ppermute | solution.py:14
  (206 shorter events, 65.1 us)
Async XLA Ops:
  0.6 6.9 %collective-permute-start = (bf16[32,1024]{1,0:T(8,128)(2,1)}, bf16[32,1024]{1,0:T(8,128)(2,1)S(1)}, u32[]{:S(2)}, u32[]{:S(2)}) collective-permute-start(bf16[32,1024]{1,0:T(8,128)(2,1)} %param.22), channel_id=1, source_target_pairs={{0,8},{8,0},{16,24},{24,16},{1,9},{9,1},{17,25},{25,17},{2,10},{10... | collective-permute-start | bytes 196616 | tf_op jit(solution)/shard_map/ppermute | solution.py:14
  5.2 5.4 %collective-permute-start.2 = (bf16[32,1024]{1,0:T(8,128)(2,1)}, bf16[32,1024]{1,0:T(8,128)(2,1)S(1)}, u32[]{:S(2)}, u32[]{:S(2)}) collective-permute-start(bf16[32,1024]{1,0:T(8,128)(2,1)} %param.22), channel_id=1, source_target_pairs={{0,24},{8,16},{16,8},{24,0},{1,25},{9,17},{17,9},{25,1},{2,26},{10... | collective-permute-start | bytes 196616 | tf_op jit(solution)/shard_map/ppermute | solution.py:14
  29.8 15.0 %collective-permute-start.4 = (bf16[528,128]{1,0:T(8,128)(2,1)}, bf16[528,128]{1,0:T(8,128)(2,1)S(1)}, u32[]{:S(2)}, u32[]{:S(2)}) collective-permute-start(bf16[528,128]{1,0:T(8,128)(2,1)} %get-tuple-element.21), channel_id=1, source_target_pairs={{0,2},{1,3},{2,0},{3,1},{4,6},{5,7},{6,4},{7,5},{8,10},{9,11},{10,... | collective-permute-start | bytes 405512 | tf_op jit(solution)/shard_map/ppermute | solution.py:14
  31.3 13.5 %collective-permute-start.5 = (bf16[528,128]{1,0:T(8,128)(2,1)}, bf16[528,128]{1,0:T(8,128)(2,1)S(1)}, u32[]{:S(2)}, u32[]{:S(2)}) collective-permute-start(bf16[528,128]{1,0:T(8,128)(2,1)} %get-tuple-element.23), channel_id=1, source_target_pairs={{0,4},{1,5},{2,6},{3,7},{4,0},{5,1},{6,2},{7,3},{8,12},{9,13},{10,... | collective-permute-start | bytes 405512 | tf_op jit(solution)/shard_map/ppermute | solution.py:14
  33.9 10.9 %collective-permute-start.6 = (bf16[528,128]{1,0:T(8,128)(2,1)}, bf16[528,128]{1,0:T(8,128)(2,1)S(1)}, u32[]{:S(2)}, u32[]{:S(2)}) collective-permute-start(bf16[528,128]{1,0:T(8,128)(2,1)} %get-tuple-element.22), channel_id=1, source_target_pairs={{0,6},{1,7},{2,4},{3,5},{4,2},{5,3},{6,0},{7,1},{8,14},{9,15},{10,... | collective-permute-start | bytes 405512 | tf_op jit(solution)/shard_map/ppermute | solution.py:14
  54.6 14.6 %collective-permute-start.15 = (bf16[4,512,128]{2,1,0:T(8,128)(2,1)S(1)}, bf16[4,512,128]{2,1,0:T(8,128)(2,1)}, u32[]{:S(2)}, u32[]{:S(2)}) collective-permute-start(bf16[4,512,128]{2,1,0:T(8,128)(2,1)S(1)} %bitcast.222), channel_id=1, source_target_pairs={{0,1},{1,0},{2,3},{3,2},{4,5},{5,4},{6,7},{7,6},{8,9},{9,8},{10,11... | collective-permute-start | bytes 1572872 | tf_op jit(solution)/shard_map/ppermute | solution.py:14
  55.8 7.9 %collective-permute-start.10 = (bf16[272,128]{1,0:T(8,128)(2,1)}, bf16[272,128]{1,0:T(8,128)(2,1)}, u32[]{:S(2)}, u32[]{:S(2)}) collective-permute-start(bf16[272,128]{1,0:T(8,128)(2,1)} %fusion.64), channel_id=1, source_target_pairs={{0,24},{8,16},{16,8},{24,0},{1,25},{9,17},{17,9},{25,1},{2,26},{10... | collective-permute-start | bytes 208904 | tf_op jit(solution)/shard_map/ppermute | solution.py:14
  56.2 7.5 %collective-permute-start.8 = (bf16[272,128]{1,0:T(8,128)(2,1)}, bf16[272,128]{1,0:T(8,128)(2,1)}, u32[]{:S(2)}, u32[]{:S(2)}) collective-permute-start(bf16[272,128]{1,0:T(8,128)(2,1)} %fusion.64), channel_id=1, source_target_pairs={{0,8},{8,0},{16,24},{24,16},{1,9},{9,1},{17,25},{25,17},{2,10},{10... | collective-permute-start | bytes 208904 | tf_op jit(solution)/shard_map/ppermute | solution.py:14
  57.8 5.9 %collective-permute-start.9 = (bf16[272,128]{1,0:T(8,128)(2,1)}, bf16[272,128]{1,0:T(8,128)(2,1)}, u32[]{:S(2)}, u32[]{:S(2)}) collective-permute-start(bf16[272,128]{1,0:T(8,128)(2,1)} %fusion.64), channel_id=1, source_target_pairs={{0,16},{8,24},{16,0},{24,8},{1,17},{9,25},{17,1},{25,9},{2,18},{10... | collective-permute-start | bytes 208904 | tf_op jit(solution)/shard_map/ppermute | solution.py:14
  64.7 6.7 %collective-permute-start.11 = (bf16[272,128]{1,0:T(8,128)(2,1)S(1)}, bf16[272,128]{1,0:T(8,128)(2,1)S(1)}, u32[]{:S(2)}, u32[]{:S(2)}) collective-permute-start(bf16[272,128]{1,0:T(8,128)(2,1)S(1)} %get-tuple-element.13), channel_id=1, source_target_pairs={{0,2},{1,3},{2,0},{3,1},{4,6},{5,7},{6,4},{7,5},{8,10},{9,11},{10,... | collective-permute-start | bytes 208904 | tf_op jit(solution)/shard_map/ppermute | solution.py:14
  66.4 6.9 %collective-permute-start.12 = (bf16[272,128]{1,0:T(8,128)(2,1)S(1)}, bf16[272,128]{1,0:T(8,128)(2,1)S(1)}, u32[]{:S(2)}, u32[]{:S(2)}) collective-permute-start(bf16[272,128]{1,0:T(8,128)(2,1)S(1)} %get-tuple-element.13), channel_id=1, source_target_pairs={{0,4},{1,5},{2,6},{3,7},{4,0},{5,1},{6,2},{7,3},{8,12},{9,13},{10,... | collective-permute-start | bytes 208904 | tf_op jit(solution)/shard_map/ppermute | solution.py:14
  69.0 6.1 %collective-permute-start.13 = (bf16[272,128]{1,0:T(8,128)(2,1)S(1)}, bf16[272,128]{1,0:T(8,128)(2,1)S(1)}, u32[]{:S(2)}, u32[]{:S(2)}) collective-permute-start(bf16[272,128]{1,0:T(8,128)(2,1)S(1)} %get-tuple-element.13), channel_id=1, source_target_pairs={{0,6},{1,7},{2,4},{3,5},{4,2},{5,3},{6,0},{7,1},{8,14},{9,15},{10,... | collective-permute-start | bytes 208904 | tf_op jit(solution)/shard_map/ppermute | solution.py:14
  75.1 5.3 %collective-permute-start.14 = (bf16[272,128]{1,0:T(8,128)(2,1)S(1)}, bf16[272,128]{1,0:T(8,128)(2,1)S(1)}, u32[]{:S(2)}, u32[]{:S(2)}) collective-permute-start(bf16[272,128]{1,0:T(8,128)(2,1)S(1)} %add_convert_fusion), channel_id=1, source_target_pairs={{0,1},{1,0},{2,3},{3,2},{4,5},{5,4},{6,7},{7,6},{8,9},{9,8},{10,11... | collective-permute-start | bytes 208904 | tf_op jit(solution)/shard_map/ppermute | solution.py:14
  76.0 10.1 %collective-permute-start.16 = (bf16[512,128]{1,0:T(8,128)(2,1)}, bf16[512,128]{1,0:T(8,128)(2,1)}, u32[]{:S(2)}, u32[]{:S(2)}) collective-permute-start(bf16[512,128]{1,0:T(8,128)(2,1)} %get-tuple-element.24), channel_id=1, source_target_pairs={{0,2},{1,3},{2,0},{3,1},{4,6},{5,7},{6,4},{7,5},{8,10},{9,11},{10,... | collective-permute-start | bytes 393224 | tf_op jit(solution)/shard_map/ppermute | solution.py:14
  76.0 13.2 %collective-permute-start.17 = (bf16[512,128]{1,0:T(8,128)(2,1)}, bf16[512,128]{1,0:T(8,128)(2,1)}, u32[]{:S(2)}, u32[]{:S(2)}) collective-permute-start(bf16[512,128]{1,0:T(8,128)(2,1)} %get-tuple-element.26), channel_id=1, source_target_pairs={{0,4},{1,5},{2,6},{3,7},{4,0},{5,1},{6,2},{7,3},{8,12},{9,13},{10,... | collective-permute-start | bytes 393224 | tf_op jit(solution)/shard_map/ppermute | solution.py:14
  78.0 11.2 %collective-permute-start.18 = (bf16[512,128]{1,0:T(8,128)(2,1)}, bf16[512,128]{1,0:T(8,128)(2,1)}, u32[]{:S(2)}, u32[]{:S(2)}) collective-permute-start(bf16[512,128]{1,0:T(8,128)(2,1)} %get-tuple-element.25), channel_id=1, source_target_pairs={{0,6},{1,7},{2,4},{3,5},{4,2},{5,3},{6,0},{7,1},{8,14},{9,15},{10,... | collective-permute-start | bytes 393224 | tf_op jit(solution)/shard_map/ppermute | solution.py:14
  90.5 16.5 %collective-permute-start.19 = (bf16[512,128]{1,0:T(8,128)(2,1)S(1)}, bf16[512,128]{1,0:T(8,128)(2,1)S(1)}, u32[]{:S(2)}, u32[]{:S(2)}) collective-permute-start(bf16[512,128]{1,0:T(8,128)(2,1)S(1)} %get-tuple-element.8), channel_id=1, source_target_pairs={{0,1},{1,0},{2,3},{3,2},{4,5},{5,4},{6,7},{7,6},{8,9},{9,8},{10,11... | collective-permute-start | bytes 393224 | tf_op jit(solution)/shard_map/ppermute | solution.py:14
  90.6 9.3 %collective-permute-start.20 = (bf16[512,128]{1,0:T(8,128)(2,1)S(1)}, bf16[512,128]{1,0:T(8,128)(2,1)S(1)}, u32[]{:S(2)}, u32[]{:S(2)}) collective-permute-start(bf16[512,128]{1,0:T(8,128)(2,1)S(1)} %get-tuple-element.8), channel_id=1, source_target_pairs={{0,2},{1,3},{2,0},{3,1},{4,6},{5,7},{6,4},{7,5},{8,10},{9,11},{10,... | collective-permute-start | bytes 393224 | tf_op jit(solution)/shard_map/ppermute | solution.py:14
  93.6 12.9 %collective-permute-start.22 = (bf16[512,128]{1,0:T(8,128)(2,1)S(1)}, bf16[512,128]{1,0:T(8,128)(2,1)S(1)}, u32[]{:S(2)}, u32[]{:S(2)}) collective-permute-start(bf16[512,128]{1,0:T(8,128)(2,1)S(1)} %get-tuple-element.8), channel_id=1, source_target_pairs={{0,4},{1,5},{2,6},{3,7},{4,0},{5,1},{6,2},{7,3},{8,12},{9,13},{10,... | collective-permute-start | bytes 393224 | tf_op jit(solution)/shard_map/ppermute | solution.py:14
  94.7 11.8 %collective-permute-start.24 = (bf16[512,128]{1,0:T(8,128)(2,1)S(1)}, bf16[512,128]{1,0:T(8,128)(2,1)S(1)}, u32[]{:S(2)}, u32[]{:S(2)}) collective-permute-start(bf16[512,128]{1,0:T(8,128)(2,1)S(1)} %get-tuple-element.8), channel_id=1, source_target_pairs={{0,6},{1,7},{2,4},{3,5},{4,2},{5,3},{6,0},{7,1},{8,14},{9,15},{10,... | collective-permute-start | bytes 393224 | tf_op jit(solution)/shard_map/ppermute | solution.py:14
  99.9 7.2 %collective-permute-start.21 = (bf16[512,128]{1,0:T(8,128)(2,1)S(1)}, bf16[512,128]{1,0:T(8,128)(2,1)S(1)}, u32[]{:S(2)}, u32[]{:S(2)}) collective-permute-start(bf16[512,128]{1,0:T(8,128)(2,1)S(1)} %collective-permute-done.20), channel_id=1, source_target_pairs={{0,1},{1,0},{2,3},{3,2},{4,5},{5,4},{6,7},{7,6},{8,9},{9,8},{10,11... | collective-permute-start | bytes 393224 | tf_op jit(solution)/shard_map/ppermute | solution.py:14
  117.6 5.2 %collective-permute-start.28 = (bf16[32,1024]{1,0:T(8,128)(2,1)S(1)}, bf16[32,1024]{1,0:T(8,128)(2,1)S(1)}, u32[]{:S(2)}, u32[]{:S(2)}) collective-permute-start(bf16[32,1024]{1,0:T(8,128)(2,1)S(1)} %get-tuple-element.38), channel_id=1, source_target_pairs={{0,24},{8,16},{16,8},{24,0},{1,25},{9,17},{17,9},{25,1},{2,26},{10... | collective-permute-start | bytes 196616 | tf_op jit(solution)/shard_map/ppermute | solution.py:14
  122.8 9.3 %collective-permute-start.29 = (bf16[32,1024]{1,0:T(8,128)(2,1)S(1)}, bf16[32,1024]{1,0:T(8,128)(2,1)S(1)}, u32[]{:S(2)}, u32[]{:S(2)}) collective-permute-start(bf16[32,1024]{1,0:T(8,128)(2,1)S(1)} %fusion.62), channel_id=1, source_target_pairs={{0,8},{8,0},{16,24},{24,16},{1,9},{9,1},{17,25},{25,17},{2,10},{10... | collective-permute-start | bytes 196616 | tf_op jit(solution)/shard_map/ppermute | solution.py:14
  124.4 7.8 %collective-permute-start.30 = (bf16[32,1024]{1,0:T(8,128)(2,1)S(1)}, bf16[32,1024]{1,0:T(8,128)(2,1)S(1)}, u32[]{:S(2)}, u32[]{:S(2)}) collective-permute-start(bf16[32,1024]{1,0:T(8,128)(2,1)S(1)} %fusion.62), channel_id=1, source_target_pairs={{0,16},{8,24},{16,0},{24,8},{1,17},{9,25},{17,1},{25,9},{2,18},{10... | collective-permute-start | bytes 196616 | tf_op jit(solution)/shard_map/ppermute | solution.py:14
  125.9 6.3 %collective-permute-start.31 = (bf16[32,1024]{1,0:T(8,128)(2,1)S(1)}, bf16[32,1024]{1,0:T(8,128)(2,1)S(1)}, u32[]{:S(2)}, u32[]{:S(2)}) collective-permute-start(bf16[32,1024]{1,0:T(8,128)(2,1)S(1)} %fusion.62), channel_id=1, source_target_pairs={{0,24},{8,16},{16,8},{24,0},{1,25},{9,17},{17,9},{25,1},{2,26},{10... | collective-permute-start | bytes 196616 | tf_op jit(solution)/shard_map/ppermute | solution.py:14
  139.0 5.4 %collective-permute-start.33 = (bf16[16,2688]{1,0:T(8,128)(2,1)S(1)}, bf16[16,2688]{1,0:T(8,128)(2,1)S(1)}, u32[]{:S(2)}, u32[]{:S(2)}) collective-permute-start(bf16[16,2688]{1,0:T(8,128)(2,1)S(1)} %get-tuple-element.27), channel_id=1, source_target_pairs={{0,2},{1,3},{2,0},{3,1},{4,6},{5,7},{6,4},{7,5},{8,10},{9,11},{10,... | collective-permute-start | bytes 258056 | tf_op jit(solution)/shard_map/ppermute | solution.py:14
  141.5 9.4 %collective-permute-start.34 = (bf16[16,2688]{1,0:T(8,128)(2,1)S(1)}, bf16[16,2688]{1,0:T(8,128)(2,1)S(1)}, u32[]{:S(2)}, u32[]{:S(2)}) collective-permute-start(bf16[16,2688]{1,0:T(8,128)(2,1)S(1)} %get-tuple-element.29), channel_id=1, source_target_pairs={{0,4},{1,5},{2,6},{3,7},{4,0},{5,1},{6,2},{7,3},{8,12},{9,13},{10,... | collective-permute-start | bytes 258056 | tf_op jit(solution)/shard_map/ppermute | solution.py:14
  142.6 8.4 %collective-permute-start.35 = (bf16[16,2688]{1,0:T(8,128)(2,1)S(1)}, bf16[16,2688]{1,0:T(8,128)(2,1)S(1)}, u32[]{:S(2)}, u32[]{:S(2)}) collective-permute-start(bf16[16,2688]{1,0:T(8,128)(2,1)S(1)} %get-tuple-element.28), channel_id=1, source_target_pairs={{0,6},{1,7},{2,4},{3,5},{4,2},{5,3},{6,0},{7,1},{8,14},{9,15},{10,... | collective-permute-start | bytes 258056 | tf_op jit(solution)/shard_map/ppermute | solution.py:14
  154.4 8.4 %collective-permute-start.39 = (bf16[16,2048]{1,0:T(8,128)(2,1)S(1)}, bf16[16,2048]{1,0:T(8,128)(2,1)S(1)}, u32[]{:S(2)}, u32[]{:S(2)}) collective-permute-start(bf16[16,2048]{1,0:T(8,128)(2,1)S(1)} %bitcast.233), channel_id=1, source_target_pairs={{0,4},{1,5},{2,6},{3,7},{4,0},{5,1},{6,2},{7,3},{8,12},{9,13},{10,... | collective-permute-start | bytes 196616 | tf_op jit(solution)/shard_map/ppermute | solution.py:14
  155.7 7.1 %collective-permute-start.41 = (bf16[16,2048]{1,0:T(8,128)(2,1)S(1)}, bf16[16,2048]{1,0:T(8,128)(2,1)S(1)}, u32[]{:S(2)}, u32[]{:S(2)}) collective-permute-start(bf16[16,2048]{1,0:T(8,128)(2,1)S(1)} %bitcast.234), channel_id=1, source_target_pairs={{0,6},{1,7},{2,4},{3,5},{4,2},{5,3},{6,0},{7,1},{8,14},{9,15},{10,... | collective-permute-start | bytes 196616 | tf_op jit(solution)/shard_map/ppermute | solution.py:14
  157.4 6.0 %collective-permute-start.38 = (bf16[16,2048]{1,0:T(8,128)(2,1)S(1)}, bf16[16,2048]{1,0:T(8,128)(2,1)S(1)}, u32[]{:S(2)}, u32[]{:S(2)}) collective-permute-start(bf16[16,2048]{1,0:T(8,128)(2,1)S(1)} %collective-permute-done.37), channel_id=1, source_target_pairs={{0,1},{1,0},{2,3},{3,2},{4,5},{5,4},{6,7},{7,6},{8,9},{9,8},{10,11... | collective-permute-start | bytes 196616 | tf_op jit(solution)/shard_map/ppermute | solution.py:14
  171.2 5.2 %collective-permute-start.45 = (bf16[32,1024]{1,0:T(8,128)(2,1)S(1)}, bf16[32,1024]{1,0:T(8,128)(2,1)S(1)}, u32[]{:S(2)}, u32[]{:S(2)}) collective-permute-start(bf16[32,1024]{1,0:T(8,128)(2,1)S(1)} %get-tuple-element.35), channel_id=1, source_target_pairs={{0,24},{8,16},{16,8},{24,0},{1,25},{9,17},{17,9},{25,1},{2,26},{10... | collective-permute-start | bytes 196616 | tf_op jit(solution)/shard_map/ppermute | solution.py:14
  (34 other events, 214.8 us)

commit v2 on v0

v2 whole, which is shorter than its diff:
```python
import math

import jax
import jax.numpy as jnp
from jax import lax
from jax.experimental import pallas as pl
from jax.experimental.pallas import tpu as pltpu
from jax.sharding import PartitionSpec as P

F32 = jnp.float32
BF16 = jnp.bfloat16
MIB = 1 << 20


def swap(value, axis, bits):
    size = lax.axis_size(axis)
    return lax.ppermute(value, axis, [(i, i ^ bits) for i in range(size)])


def swaps_gx(values):
    return [swap(v, "gx", k + 1) for k, v in enumerate(values)]


def swaps_chip(values):
    return [swap(v, "yz", 2 * (k + 1)) for k, v in enumerate(values)]


def gather_yz(value, *staged):
    chips = lax.axis_size("yz") // 2
    got = swaps_chip([value] * (chips - 1))
    *got[1:], staged = lax.optimization_barrier((*got[1:], staged))
    mine = [value] + got
    other = [swap(v, "yz", 1) for v in mine]
    return [v for pair in zip(mine, other) for v in pair], staged


def dot(a, b, dims=((1,), (0,)), **kw):
    return lax.dot_general(a, b, (dims, ((), ())), preferred_element_type=F32, **kw)


def in_hbm(array):
    held = pltpu.with_memory_space_constraint(array, pltpu.HBM)
    return held, pl.BlockSpec(memory_space=pltpu.HBM)


def in_vmem(array):
    held = pltpu.with_memory_space_constraint(array, pltpu.VMEM)
    return held, pl.BlockSpec(memory_space=pltpu.VMEM)


def anywhere(array):
    return array, pl.BlockSpec(memory_space=pl.ANY)


def shape(dims, dtype):
    return pltpu.VMEM(tuple(dims), dtype)


def call(kernel, place, inputs, outs, scratch=(), limit=4, cost=None, name=None):
    pairs = [a if isinstance(a, tuple) else in_vmem(a) for a in inputs]
    return pl.pallas_call(
        kernel,
        grid_spec=pltpu.PrefetchScalarGridSpec(
            num_scalar_prefetch=1,
            grid=(),
            in_specs=[spec for _, spec in pairs],
            out_specs=[pl.BlockSpec(memory_space=pltpu.VMEM)] * len(outs),
            scratch_shapes=list(scratch),
        ),
        out_shape=outs,
        compiler_params=pltpu.CompilerParams(vmem_limit_bytes=limit * MIB),
        cost_estimate=cost and pl.CostEstimate(flops=0, bytes_accessed=cost, transcendentals=0),
        name=name,
    )(place, *[array for array, _ in pairs])


def fetch(pairs, sems):
    copies = [
        pltpu.make_async_copy(source, target, sems.at[k])
        for k, (source, target) in enumerate(pairs)
    ]
    for copy in copies:
        copy.start()
    return copies


def owner_rows(w_ref, half, place_ref, own, target, count):
    return [
        (
            w_ref.at[half, pl.ds(pl.multiple_of(place_ref[k] * own, own), own), :],
            target.at[k],
        )
        for k in range(count)
    ]


def stage_first(place, weights, hidden, gain, own, chips):
    width = weights.shape[2]

    def kernel(place_ref, w_ref, hidden_ref, gain_ref, held, hidden_to, gain_to, sems):
        pairs = owner_rows(w_ref, 0, place_ref, own, held, 2 * chips)
        for copy in fetch(pairs + [(hidden_ref, hidden_to), (gain_ref, gain_to)], sems):
            copy.wait()

    return call(
        kernel,
        place,
        [in_hbm(weights), in_hbm(hidden), in_hbm(gain)],
        [
            shape((2 * chips, own, width), BF16),
            shape(hidden.shape, BF16),
            shape(gain.shape, F32),
        ],
        scratch=[pltpu.SemaphoreType.DMA((2 * chips + 2,))],
        limit=4,
        cost=2 * chips * own * width * 2,
        name="stage_first",
    )


def stage_rows(place, weights, count, earlier, ordered, chips, name):
    rows, width = weights.shape
    block = rows // count

    def kernel(place_ref, w_ref, earlier_ref, held, sems):
        pairs = []
        for k in range(count):
            at = place_ref[2 * chips + 1] ^ k if ordered else k
            pairs.append(
                (w_ref.at[pl.ds(pl.multiple_of(at * block, block), block), :], held.at[k])
            )
        for copy in fetch(pairs, sems):
            copy.wait()

    return call(
        kernel,
        place,
        [in_hbm(weights), anywhere(earlier)],
        [shape((count, block, width), BF16)],
        scratch=[pltpu.SemaphoreType.DMA((count,))],
        limit=4,
        cost=rows * width * 2,
        name=name,
    )[0]


def add_pairs(keep, received, parts, place, name):
    rows = keep.shape[0] // parts
    width = keep.shape[1]

    def kernel(place_ref, keep_ref, received_ref, own_ref, *wire_refs):
        for k in range(parts):
            block = pl.ds(k * rows, rows)
            total = keep_ref[block, :].astype(F32) + received_ref[block, :].astype(F32)
            if k == 0:
                own_ref[...] = total
            else:
                wire_refs[k - 1][...] = total.astype(BF16)

    own, *wires = call(
        kernel,
        place,
        [keep, received],
        [shape((rows, width), F32)] + [shape((rows, width), BF16)] * (parts - 1),
        name=name,
    )
    return own, wires


def add_both(place, part, received, keep, z_received, parts):
    half, batch = part.shape
    own = keep.shape[0] // parts

    def kernel(place_ref, part_ref, received_ref, keep_ref, z_ref, sum_ref, zown_ref, *refs):
        total = part_ref[...] + received_ref[...].astype(F32)
        sum_ref[...] = total
        for k in range(parts):
            block = pl.ds(k * own, own)
            z = keep_ref[block, :].astype(F32) + z_ref[block, :].astype(F32)
            if k == 0:
                zown_ref[...] = z
                continue
            refs[k - 1][:half, :] = total.astype(BF16)
            if k < parts - 1:
                refs[k - 1][half:, :] = z.astype(BF16)
            else:
                refs[k][...] = z.astype(BF16)

    total, zown, *wires = call(
        kernel,
        place,
        [part, received, keep, z_received],
        [shape((half, batch), F32), shape((own, batch), F32)]
        + [shape((half + own, batch), BF16)] * (parts - 2)
        + [shape((half, batch), BF16), shape((own, batch), BF16)],
        name="add_both",
    )
    return total, zown, wires[:-1], wires[-1]


def project_first(place, pieces, gain, weights, batch, chips):
    own, width = weights.shape[1:]
    rows = pieces[0].shape[0]
    count = len(pieces)

    def kernel(place_ref, *refs):
        piece_refs = refs[:count]
        gain_ref, w_ref, out_ref, gained_ref, squares_ref, wide = refs[count:]
        me = place_ref[2 * chips]
        for k in range(count):
            start = pl.multiple_of((me ^ k) * rows, rows)
            wide[pl.ds(start, rows), :] = piece_refs[k][...].astype(F32)
        value = wide[...]
        squares = jnp.sum(value * value, axis=1, keepdims=True)
        squares = jnp.transpose(jnp.broadcast_to(squares, (batch, 128)))[:16, :]
        squares_ref[...] = squares
        gained_ref[...] = jnp.transpose(value * gain_ref[...]).astype(BF16)
        for k in range(chips):
            out_ref[k, :own, :] = dot(w_ref[k], gained_ref[...]).astype(BF16)
            out_ref[k, own:, :] = squares.astype(BF16)

    return call(
        kernel,
        place,
        list(pieces) + [gain, weights],
        [
            shape((chips, own + 16, batch), BF16),
            shape((width, batch), BF16),
            shape((16, batch), F32),
        ],
        scratch=[pltpu.VMEM((batch, width), F32)],
        limit=8,
        name="project_first",
    )


def project_keep(place, weights, gained, squares, chips):
    own = weights.shape[1]
    batch = gained.shape[1]

    def kernel(place_ref, w_ref, gained_ref, squares_ref, out_ref):
        for k in range(chips):
            out_ref[k, :own, :] = dot(w_ref[chips + k], gained_ref[...]).astype(BF16)
            out_ref[k, own:, :] = squares_ref[...].astype(BF16)

    return call(
        kernel,
        place,
        [weights, gained, squares],
        [shape((chips, own + 16, batch), BF16)],
        name="project_keep",
    )[0]


def project_gate(place, weights, gained, conv_rows, x_cols, own, chips, earlier):
    width, batch = gained.shape
    count = 2 * chips

    def kernel(
        place_ref, w_ref, gained_ref, conv_ref, cols_ref, earlier_ref,
        give_ref, keep_ref, conv_to, cols_to, held, sems,
    ):
        pairs = owner_rows(w_ref, 1, place_ref, own, held, count)
        copies = fetch(pairs + [(conv_ref, conv_to), (cols_ref, cols_to)], sems)
        for out_ref, base in ((give_ref, 0), (keep_ref, chips)):
            for k in range(chips):
                copies[base + k].wait()
            for k in range(chips):
                out_ref[k] = dot(held[base + k], gained_ref[...]).astype(BF16)
        copies[count].wait()
        copies[count + 1].wait()

    return call(
        kernel,
        place,
        [in_hbm(weights), gained, in_hbm(conv_rows), in_hbm(x_cols), anywhere(earlier)],
        [shape((chips, own, batch), BF16)] * 2
        + [shape(conv_rows.shape, BF16), shape(x_cols.shape, BF16)],
        scratch=[
            pltpu.VMEM((count, own, width), BF16),
            pltpu.SemaphoreType.DMA((count + 2,)),
        ],
        limit=12,
        cost=count * own * width * 2,
        name="project_gate",
    )


def convolve(place, own_sum, received, conv_state, params, alive, x_cols, own, whole_width):
    taps, _, batch = conv_state.shape
    half = x_cols.shape[0] // 2
    count = len(received)

    def kernel(place_ref, own_ref, *refs):
        got = refs[:count]
        (
            state_ref,
            params_ref,
            alive_ref,
            cols_ref,
            new_ref,
            xa_ref,
            give_ref,
            keep_ref,
            scale_ref,
        ) = refs[count:]
        total = own_ref[...]
        for ref in got:
            total = total + ref[...].astype(F32)
        scale = lax.rsqrt(total[own : own + 8, :] / whole_width + 1e-05)
        scale_ref[...] = scale
        value = (total[:own] * scale[:1]).astype(BF16)
        held = alive_ref[:1, :] > 0
        mixed = params_ref[:, taps : taps + 1] * value.astype(F32)
        for k in range(taps):
            old = jnp.where(held, state_ref[k].astype(F32), 0.0)
            mixed = mixed + params_ref[:, k : k + 1] * old
            if k:
                new_ref[k - 1] = old.astype(BF16)
        new_ref[taps - 1] = value
        mixed = mixed + params_ref[:, taps + 1 : taps + 2]
        active = (mixed / (1.0 + jnp.exp(-mixed))).astype(BF16)
        xa_ref[...] = active
        core = place_ref[place_ref.shape[0] - 1]
        there = pl.multiple_of((1 - core) * half, half)
        here = pl.multiple_of(core * half, half)
        give_ref[...] = dot(cols_ref[pl.ds(there, half), :], active).astype(BF16)
        keep_ref[...] = dot(cols_ref[pl.ds(here, half), :], active)

    return call(
        kernel,
        place,
        [own_sum]
        + list(received)
        + [
            conv_state,
            params,
            alive,
            x_cols,
        ],
        [
            shape(conv_state.shape, BF16),
            shape((own, batch), BF16),
            shape((half, batch), BF16),
            shape((half, batch), F32),
            shape((8, batch), F32),
        ],
        limit=8,
        name="convolve",
    )


def ready_state(place, state, alive, earlier):
    own, nstate, batch = state.shape
    block = 128
    steps, lanes = own // block, batch // 128

    def kernel(place_ref, state_ref, alive_ref, earlier_ref, out_ref, held, wide, sems):
        copies = fetch(
            [(state_ref.at[pl.ds(i * block, block)], held.at[i]) for i in range(steps)], sems
        )
        for i in range(steps):
            copies[i].wait()
            old = held[i].reshape(block * nstate, batch).astype(F32)
            old = jnp.where(alive_ref[:1, :] > 0, old, 0.0)
            for c in range(lanes):
                wide[i % 2, c] = old[:, c * 128 : (c + 1) * 128]
                for n in range(nstate):
                    out_ref[n, i * block : (i + 1) * block, c * 128 : (c + 1) * 128] = wide[
                        i % 2, c, pl.ds(n, block, stride=nstate), :
                    ]

    return call(
        kernel,
        place,
        [in_hbm(state), alive, anywhere(earlier)],
        [shape((nstate, own, batch), F32)],
        scratch=[
            pltpu.VMEM((steps, block, nstate, batch), BF16),
            pltpu.VMEM((2, lanes, block * nstate, 128), F32),
            pltpu.SemaphoreType.DMA((steps,)),
        ],
        limit=16,
        cost=own * nstate * batch * 6,
        name="ready_state",
    )[0]


def scan(place, mine, other, dt_rows, params, state, xa, zown, zgot, scale, taps):
    nstate, own, batch = state.shape
    rank = dt_rows.shape[1]
    half = mine.shape[0]
    block = 128
    steps, lanes = own // block, batch // 128
    count = len(zgot)

    def kernel(place_ref, mine_ref, other_ref, dtw_ref, params_ref, state_ref, *refs):
        xa_ref, zown_ref = refs[:2]
        zrefs = refs[2 : 2 + count]
        scale_ref, new_ref, gated_ref, low, behind, packed, sems = refs[2 + count :]
        core = place_ref[place_ref.shape[0] - 1]
        first = jnp.broadcast_to(core, mine_ref.shape) == 0
        low[:half] = jnp.where(first, mine_ref[...], other_ref[...])
        low[half:] = jnp.where(first, other_ref[...], mine_ref[...])
        copies = []
        for i in range(steps):
            here = slice(i * block, (i + 1) * block)
            pre = dot(dtw_ref[here, :], low[:rank, :]) + params_ref[here, taps + 2 : taps + 3]
            step = jnp.maximum(pre, 0.0) + jnp.log1p(jnp.exp(-jnp.abs(pre)))
            wide = xa_ref[here, :].astype(F32)
            drive = step * wide
            value = params_ref[here, taps + 3 : taps + 4] * wide
            for n in range(nstate):
                rate = params_ref[here, taps + 4 + n : taps + 5 + n]
                bm = low[rank + n : rank + n + 1, :].astype(F32)
                cm = low[rank + nstate + n : rank + nstate + n + 1, :].astype(F32)
                fresh = jnp.exp(-step * rate) * state_ref[n, here, :] + drive * bm
                for c in range(lanes):
                    behind[i % 2, c, pl.ds(n, block, stride=nstate), :] = fresh[
                        :, c * 128 : (c + 1) * 128
                    ]
                value = value + fresh * cm
            for c in range(lanes):
                packed[i, :, :, c * 128 : (c + 1) * 128] = (
                    behind[i % 2, c].reshape(block, nstate, 128).astype(BF16)
                )
            copy = pltpu.make_async_copy(packed.at[i], new_ref.at[pl.ds(i * block, block)], sems.at[i])
            copy.start()
            copies.append(copy)
            ztotal = zown_ref[here, :]
            for ref in zrefs:
                start = ref.shape[0] - own + i * block
                ztotal = ztotal + ref[start : start + block, :].astype(F32)
            gate = (ztotal * scale_ref[:1, :]).astype(BF16).astype(F32)
            value = value * (gate / (1.0 + jnp.exp(-gate)))
            gated_ref[:, here] = jnp.transpose(value).astype(BF16)
        for copy in copies:
            copy.wait()

    pairs = [in_vmem(a) for a in (mine, other, dt_rows, params, state, xa, zown, *zgot, scale)]
    return pl.pallas_call(
        kernel,
        grid_spec=pltpu.PrefetchScalarGridSpec(
            num_scalar_prefetch=1,
            grid=(),
            in_specs=[spec for _, spec in pairs],
            out_specs=[
                pl.BlockSpec(memory_space=pltpu.HBM),
                pl.BlockSpec(memory_space=pltpu.VMEM),
            ],
            scratch_shapes=[
                pltpu.VMEM((2 * half, batch), BF16),
                pltpu.VMEM((2, lanes, block * nstate, 128), F32),
                pltpu.VMEM((steps, block, nstate, batch), BF16),
                pltpu.SemaphoreType.DMA((steps,)),
            ],
        ),
        out_shape=[
            pltpu.HBM((own, nstate, batch), BF16),
            pltpu.VMEM((batch, own), BF16),
        ],
        compiler_params=pltpu.CompilerParams(vmem_limit_bytes=18 * MIB),
        name="scan",
    )(place, *[array for array, _ in pairs])


def mix_out(place, pieces, weights, parts, chips):
    batch, own = pieces[0].shape
    width = weights.shape[2]
    count = len(pieces)
    rows = batch // parts

    def kernel(place_ref, *refs):
        piece_refs = refs[:count]
        w_ref, own_ref = refs[count : count + 2]
        wire_refs = refs[count + 2 : -1]
        total = refs[-1]
        for j in range(count):
            term = dot(piece_refs[j][...], w_ref[j])
            total[...] = term if j == 0 else total[...] + term
        me = place_ref[2 * chips]
        for k in range(parts):
            start = pl.multiple_of((me ^ k) * rows, rows)
            value = total[pl.ds(start, rows), :]
            if k == 0:
                own_ref[...] = value
            else:
                wire_refs[k - 1][...] = value.astype(BF16)

    own_rows, *wires = call(
        kernel,
        place,
        list(pieces) + [weights],
        [shape((rows, width), F32)] + [shape((rows, width), BF16)] * (parts - 1),
        scratch=[pltpu.VMEM((batch, width), F32)],
        limit=8,
        name="mix_out",
    )
    return own_rows, wires


def held_by(assign_ref):
    batch = assign_ref.shape[1]
    requests = lax.broadcasted_iota(jnp.int32, (batch, batch), 0)
    return jnp.where(assign_ref[...] == requests, 1.0, 0.0).astype(BF16)


def query(place, pieces, assign, gain, weights, chips):
    rows, width = pieces[0].shape
    batch = rows * len(pieces)
    count = len(pieces)
    columns = weights.shape[1]
    steps = 5
    block = columns // steps
    half = batch // 2
    slots = half // chips

    def kernel(place_ref, *refs):
        piece_refs = refs[:count]
        assign_ref, gain_ref, w_ref, give_ref, keep_ref, stacked, ordered = refs[count:]
        me = place_ref[2 * chips]
        for k in range(count):
            start = pl.multiple_of((me ^ k) * rows, rows)
            stacked[pl.ds(start, rows), :] = piece_refs[k][...]
        chosen = held_by(assign_ref)
        stacked[...] = dot(chosen, stacked[...], ((0,), (0,))).astype(BF16)
        for k in range(2 * chips):
            start = pl.multiple_of(place_ref[k] * slots, slots)
            ordered[k * slots : (k + 1) * slots, :] = stacked[pl.ds(start, slots), :]
        value = ordered[...].astype(F32)
        squares = jnp.sum(value * value, axis=1, keepdims=True)
        squares = jnp.broadcast_to(squares, (batch, 128)).astype(BF16)
        give_ref[:, columns:] = squares[:half]
        keep_ref[:, columns:] = squares[half:]
        gained = (value * gain_ref[...]).astype(BF16)
        for j in range(steps):
            out = dot(gained, w_ref[:, j * block : (j + 1) * block]).astype(BF16)
            give_ref[:, j * block : (j + 1) * block] = out[:half]
            keep_ref[:, j * block : (j + 1) * block] = out[half:]

    return call(
        kernel,
        place,
        list(pieces) + [assign, gain, weights],
        [shape((half, columns + 128), BF16)] * 2,
        scratch=[pltpu.VMEM((batch, width), BF16)] * 2,
        limit=8,
        name="query",
    )


def head_out(place, pieces, assign, weights, parts, chips):
    slots, depth = pieces[0].shape
    count = len(pieces)
    batch = slots * count
    steps, block, width = weights.shape
    rows = batch // parts

    def kernel(place_ref, *refs):
        piece_refs = refs[:count]
        assign_ref, w_ref, own_ref = refs[count : count + 3]
        wire_refs = refs[count + 3 : -2]
        stacked, total = refs[-2:]
        mine = place_ref[2 * chips + 1]
        for j in range(count):
            start = pl.multiple_of((mine ^ j) * slots, slots)
            stacked[pl.ds(start, slots), :] = piece_refs[j][...]
        chosen = held_by(assign_ref)
        for j in range(steps):
            taken = dot(chosen, stacked[:, j * block : (j + 1) * block]).astype(BF16)
            term = dot(taken, w_ref[j])
            total[...] = term if j == 0 else total[...] + term
        me = place_ref[2 * chips]
        for k in range(parts):
            start = pl.multiple_of((me ^ k) * rows, rows)
            value = total[pl.ds(start, rows), :]
            if k == 0:
                own_ref[...] = value
            else:
                wire_refs[k - 1][...] = value.astype(BF16)

    own_rows, *wires = call(
        kernel,
        place,
        list(pieces) + [assign, weights],
        [shape((rows, width), F32)] + [shape((rows, width), BF16)] * (parts - 1),
        scratch=[pltpu.VMEM((batch, depth), BF16), pltpu.VMEM((batch, width), F32)],
        limit=8,
        name="head_out",
    )
    return own_rows, wires


def total_of(own, received):
    total = own
    for value in received:
        total = total + value.astype(F32)
    return total


def on_device(
    hidden_in,
    norm_gain_a,
    mixer_projection,
    conv_weight,
    conv_bias,
    conv_state,
    ssm_state,
    reset_ids,
    x_proj,
    dt_proj,
    dt_bias,
    a_log,
    d_skip,
    mixer_output,
    norm_gain_b,
    attention_projection,
    head_output,
    kv_cache,
    lengths,
    assign,
):
    batch = assign.shape[0]
    yz, gx = lax.axis_size("yz"), lax.axis_size("gx")
    chips = yz // 2
    me_yz, me_gx = lax.axis_index("yz"), lax.axis_index("gx")
    core = me_yz % 2
    width = hidden_in.shape[1]
    whole_width = width * yz
    own = mixer_projection.shape[1] // yz
    taps = conv_state.shape[1]

    owners = jnp.concatenate(
        [(me_yz ^ 1) ^ (2 * jnp.arange(chips)), me_yz ^ (2 * jnp.arange(chips))]
    ).astype(jnp.int32)
    place = jnp.concatenate([owners, jnp.stack([me_gx, me_yz, core]).astype(jnp.int32)])
    requests = jnp.arange(batch, dtype=jnp.int32)
    x_cols = jnp.transpose(x_proj)
    conv_rows = jnp.transpose(conv_state, (1, 0, 2))
    group_count, group_cols = attention_projection.shape[1:]
    slot_count = kv_cache.shape[0]

    got = swaps_gx([hidden_in] * (gx - 1))
    weights, hidden_here, gain = stage_first(
        place, mixer_projection, hidden_in, norm_gain_a[None, :], own, chips
    )
    got, weights = lax.optimization_barrier((got, weights))
    give, gained, squares = project_first(
        place, [hidden_here] + got, gain, weights, batch, chips
    )
    tall = chips * (own + 16)
    received = swap(give.reshape(tall, batch), "yz", 1)
    keep = project_keep(place, weights, gained, squares, chips)
    xown, wires = add_pairs(keep.reshape(tall, batch), received, chips, place, "add_x")
    xgot = swaps_chip(wires)
    give, keep, conv_rows, x_cols = project_gate(
        place, mixer_projection, gained, conv_rows, x_cols, own, chips, wires[0]
    )
    (conv_weight, a_log, reset_ids, dt_proj), wires = lax.optimization_barrier(
        ((conv_weight, a_log, reset_ids, dt_proj), wires)
    )
    alive = jnp.where(jnp.any(reset_ids[:, None] == requests[None, :], axis=0), 0.0, 1.0)
    alive = jnp.broadcast_to(alive[None, :].astype(F32), (8, batch))
    params = jnp.transpose(
        jnp.concatenate(
            [conv_weight, conv_bias[None], dt_bias[None], d_skip[None], jnp.exp(a_log)], axis=0
        )
    )
    dt_rows = jnp.transpose(dt_proj)
    xgot, give, keep, conv_rows, x_cols, params, alive, dt_rows = lax.optimization_barrier(
        (xgot, give, keep, conv_rows, x_cols, params, alive, dt_rows)
    )
    z_received = swap(give.reshape(chips * own, batch), "yz", 1)
    conv_new, xa, give, part, scale = convolve(
        place, xown, xgot, conv_rows, params, alive, x_cols, own, whole_width
    )
    part, zown, wires, z_last = add_both(
        place, part, swap(give, "yz", 1), keep.reshape(chips * own, batch), z_received, chips
    )
    got = swaps_chip(wires)
    half = part.shape[0]
    part = total_of(part, [g[:half] for g in got])
    z_got = got[:-1] + [swap(z_last, "yz", 2 * (chips - 1))]
    wire = part.astype(BF16)
    got = swaps_gx([wire] * (gx - 1))
    old = ready_state(place, ssm_state, alive, wire)
    got, z_got, old = lax.optimization_barrier((got, z_got, old))
    part = total_of(part, got).astype(BF16)
    ssm_new, gated = scan(
        place, part, swap(part, "yz", 1), dt_rows, params, old, xa, zown, z_got, scale, taps
    )

    gated, attention_projection = lax.optimization_barrier((gated, attention_projection))
    flattened = attention_projection.reshape(width, group_count * group_cols)
    weights = stage_rows(place, mixer_output, yz, gated, True, chips, "stage_mix")
    pieces, (flattened, weights) = gather_yz(gated, flattened, weights)
    own_rows, wires = mix_out(place, pieces, weights, gx, chips)
    first_out = (hidden_in.astype(F32) + total_of(own_rows, swaps_gx(wires))).astype(BF16)

    pieces = [first_out] + swaps_gx([first_out] * (gx - 1))
    give, keep = query(place, pieces, assign[None, :], norm_gain_b[None, :], flattened, chips)
    entries, wires = add_pairs(keep, swap(give, "yz", 1), chips, place, "add_query")
    entries = total_of(entries, swaps_chip(wires))
    scale = lax.rsqrt(entries[:, -1:] / whole_width + 1e-05)
    newest_entry = (entries[:, :-128] * scale).astype(BF16)
    newest_entry = newest_entry.reshape(slot_count, group_count, group_cols)
    head_dim = kv_cache.shape[3] // 2
    per_group = group_cols // head_dim - 2
    fresh_kv = newest_entry[:, :, per_group * head_dim :]
    query_vector = newest_entry[:, :, : per_group * head_dim].reshape(
        slot_count, group_count, per_group, head_dim
    )
    key_new = newest_entry[:, :, per_group * head_dim : (per_group + 1) * head_dim]
    value_new = newest_entry[:, :, (per_group + 1) * head_dim :]
    keys = kv_cache[..., :head_dim]
    values = kv_cache[..., head_dim:]
    factor = 1.0 / math.sqrt(head_dim)
    scores = (
        jnp.einsum("sghd,stgd->sght", query_vector, keys, preferred_element_type=F32) * factor
    )
    own_score = (
        jnp.einsum("sghd,sgd->sgh", query_vector, key_new, preferred_element_type=F32) * factor
    )
    positions = jnp.arange(kv_cache.shape[1], dtype=jnp.int32)
    valid = (positions[None, :] < lengths[:, None])[:, None, None, :]
    top = jnp.maximum(jnp.max(jnp.where(valid, scores, -1e30), axis=-1), own_score)
    expo = jnp.where(valid, jnp.exp(scores - top[..., None]), 0.0)
    expo_own = jnp.exp(own_score - top)
    total = jnp.sum(expo, axis=-1) + expo_own
    weights = (expo / total[..., None]).astype(BF16)
    weight_own = (expo_own / total).astype(BF16)
    attended = jnp.einsum("sght,stgd->sghd", weights, values, preferred_element_type=F32)
    attended = (
        attended + weight_own.astype(F32)[..., None] * value_new.astype(F32)[:, :, None, :]
    )
    heads = attended.astype(BF16).reshape(slot_count, group_count * per_group * head_dim)
    head_weights = stage_rows(place, head_output, 4, heads, False, chips, "stage_head")
    pieces, (head_weights,) = gather_yz(heads, head_weights)
    own_rows, wires = head_out(place, pieces, assign[None, :], head_weights, gx, chips)
    hidden_out = (first_out.astype(F32) + total_of(own_rows, swaps_gx(wires))).astype(BF16)
    return (hidden_out, ssm_new, jnp.transpose(conv_new, (1, 0, 2)), fresh_kv)


def solution(mesh):
    placed = (
        P(("groups", "gx"), "yz"),
        P("yz"),
        P(None, "gx", "yz"),
        P(None, ("gx", "yz")),
        P(("gx", "yz")),
        P(("gx", "yz"), None, "groups"),
        P(("gx", "yz"), None, "groups"),
        P("groups"),
        P(("gx", "yz"), None),
        P(None, ("gx", "yz")),
        P(("gx", "yz")),
        P(None, ("gx", "yz")),
        P(("gx", "yz")),
        P("gx", "yz"),
        P("yz"),
        P("yz", "gx", None),
        P("gx", "yz"),
        P(("groups", "yz"), None, "gx", None),
        P(("groups", "yz")),
        P("groups"),
    )
    return jax.shard_map(
        on_device,
        mesh=mesh,
        in_specs=placed,
        out_specs=(
            P(("groups", "gx"), "yz"),
            P(("gx", "yz"), None, "groups"),
            P(("gx", "yz"), None, "groups"),
            P(("groups", "yz"), "gx", None),
        ),
        check_vma=False,
    )
```

time: 405 us -> 135 us (0.33)
  waiting for transfers between devices: 241 us -> 41.3 us
  blocking collectives: 82.6 us -> 0 us
  starting transfers between devices: 0.25 us -> 48.2 us
  Pallas kernels: 0 us -> 36.7 us
  matrix products: 27.5 us -> 0.95 us
  other arithmetic: 19.9 us -> 1.61 us
  local copies, waits for them, and re-layouts: 19 us -> 4.42 us
  between operations: 14.4 us -> 1.18 us
    psum x1 -> x0, waiting for transfers between devices: 122 us -> none  [on_device(): proj = lax.psum(partial_value, ('gx', 'yz'))]
    reduce_scatter x4 -> x0, waiting for transfers between devices: 95.1 us -> none  [the longest x2 55.8 us: owner_sum(): lax.psum_scatter(term_fn(jnp.int32(0), owned_rows * lax.axis_size('yz'))....]
    all_gather x4 -> x0, blocking collectives: 48.7 us -> none  [the longest x2 18.1 us: spread(): return lax.all_gather(values, 'gx', axis=0, tiled=True)]
    ppermute x0 -> x44, starting transfers between devices: none -> 48.2 us  [swap(): return lax.ppermute(value, axis, [(i, i ^ bits) for i in range(size)])]
    ppermute x0 -> x44, waiting for transfers between devices: none -> 41.3 us  [swap(): return lax.ppermute(value, axis, [(i, i ^ bits) for i in range(size)])]
    pallas_call x0 -> x15, Pallas kernels: none -> 36.7 us  [the longest x14 32.2 us: call(): pl.pallas_call(kernel, grid_spec=pltpu.PrefetchScalarGridSpec(num_scalar_...]
    psum x2 -> x0, blocking collectives: 33.9 us -> none  [normalize(): squares = lax.psum(jnp.sum(wide * wide, axis=1), 'yz')]
    dot_general x7 -> x1, matrix products: 26.9 us -> 0.32 us  [on_device(): jnp.einsum('sght,stgd->sghd', weights, values, preferred_element_type=F32)]
  transfers between devices with their start and end apart: 6 -> 44, of which waited for: 6 -> 28; matrix products, arithmetic and copies ran while one was open for 4% -> 3% of each run, Pallas kernels for 0% -> 17%
where the time goes in v2:
time: 135 us; the launch traced here: 134 us
  starting transfers between devices  48.2 us (36%)
  waiting for transfers between devices  41.3 us (31%)
  Pallas kernels  36.7 us (27%)
  local copies, waits for them, and re-layouts  4.42 us (3%)
  other arithmetic  1.61 us (1%)
    ppermute x44, starting transfers between devices, swap(): return lax.ppermute(value, axis, [(i, i ^ bits) for i in range(size)])  48.2 us
    ppermute x44, waiting for transfers between devices, swap(): return lax.ppermute(value, axis, [(i, i ^ bits) for i in range(size)])  41.3 us
    pallas_call x14, Pallas kernels, call(): pl.pallas_call(kernel, grid_spec=pltpu.PrefetchScalarGridSpec(num_scalar_...  32.2 us
    pallas_call x1, Pallas kernels, scan(): pl.pallas_call(kernel, grid_spec=pltpu.PrefetchScalarGridSpec(num_scalar_...  4.53 us
  transfers between devices with their start and end apart: 44, of which 28 were waited for; matrix products, arithmetic and copies ran while one was open for 3% of the time, Pallas kernels for 17%

profile of v2, /device:TPU:0, one launch (start us, length us, event | category | flops | bytes accessed | tf_op | source)
XLA Modules:
  0.0 134.4 jit_solution(8705173230077987964)
XLA Ops:
  0.6 3.0 %collective-permute-start = (bf16[32,1024]{1,0:T(8,128)(2,1)}, bf16[32,1024]{1,0:T(8,128)(2,1)S(1)}, u32[]{:S(2)}, u32[]{:S(2)}) collective-permute-start(bf16[32,1024]{1,0:T(8,128)(2,1)} %hidden_ref.1), channel_id=1, source_target_pairs={{0,8},{8,0},{16,24},{24,16},{1,9},{9,1},{17,25},{25,17},{2,10},{10... | collective-permute-start | bytes 196616 | tf_op jit(solution)/shard_map/ppermute | solution.py:17
  5.3 4.0 %stage_first.1 = (bf16[8,512,1024]{2,1,0:T(8,128)(2,1)S(1)}, bf16[32,1024]{1,0:T(8,128)(2,1)S(1)}, f32[1,1024]{1,0:T(1,128)S(1)}) custom-call(s32[11]{0:T(128)S(1)} %concatenate.6.place_ref, bf16[2,4096,1024]{2,1,0:T(8,128)(2,1)} %w_ref.5, bf16[32,1024]{1,0:T(8,128)(2,1)} %hidden_ref.1, f32[1,1024]{1,0:T(1,128)} %bitcast.57), custom_call_target="tpu_custom_call" | custom-call | bytes 8388608 | tf_op jit(solution)/shard_map/stage_first/pallas_call | solution.py:61
  10.5 2.0 %project_first.1 = (bf16[4,528,128]{2,1,0:T(8,128)(2,1)S(1)}, bf16[1024,128]{1,0:T(8,128)(2,1)S(1)}, f32[16,128]{1,0:T(8,128)S(1)}) custom-call(s32[11]{0:T(128)S(1)} %concatenate.6.place_ref, bf16[32,1024]{1,0:T(8,128)(2,1)S(1)} %get-tuple-element.81.refs_0_, bf16[32,1024]{1,0:T(8,128)(2,1)S(1)} %collective-permute-done.refs_1_, ...), custom_call_target="tpu_custom_call" | custom-call | tf_op jit(solution)/shard_map/project_first/pallas_call | solution.py:61
  12.7 1.8 %project_keep.1 = bf16[4,528,128]{2,1,0:T(8,128)(2,1)S(1)} custom-call(s32[11]{0:T(128)S(1)} %concatenate.6.place_ref, bf16[8,512,1024]{2,1,0:T(8,128)(2,1)S(1)} %get-tuple-element.80.refs_5_.w_ref, bf16[1024,128]{1,0:T(8,128)(2,1)S(1)} %get-tuple-element.86.gained_ref, f32[16,128]{1,0:T(8,128)S(1)} %get-tuple-element.87.squares_ref), custom_call_target="tpu_custom_call" | custom-call | tf_op jit(solution)/shard_map/project_keep/pallas_call | solution.py:61
  15.2 1.6 %collective-permute-start.4 = (bf16[528,128]{1,0:T(8,128)(2,1)S(1)}, bf16[528,128]{1,0:T(8,128)(2,1)S(1)}, u32[]{:S(2)}, u32[]{:S(2)}) collective-permute-start(bf16[528,128]{1,0:T(8,128)(2,1)S(1)} %get-tuple-element.90.earlier_ref), channel_id=1, source_target_pairs={{0,2},{1,3},{2,0},{3,1},{4,6},{5,7},{6,4},{7,5},{8,10},{9,11},{10,... | collective-permute-start | bytes 405512 | tf_op jit(solution)/shard_map/ppermute | solution.py:17
  16.8 2.6 %collective-permute-start.5 = (bf16[528,128]{1,0:T(8,128)(2,1)S(1)}, bf16[528,128]{1,0:T(8,128)(2,1)S(1)}, u32[]{:S(2)}, u32[]{:S(2)}) collective-permute-start(bf16[528,128]{1,0:T(8,128)(2,1)S(1)} %get-tuple-element.91), channel_id=1, source_target_pairs={{0,4},{1,5},{2,6},{3,7},{4,0},{5,1},{6,2},{7,3},{8,12},{9,13},{10,... | collective-permute-start | bytes 405512 | tf_op jit(solution)/shard_map/ppermute | solution.py:17
  20.5 5.3 %project_gate.1 = (bf16[4,512,128]{2,1,0:T(8,128)(2,1)S(1)}, bf16[4,512,128]{2,1,0:T(8,128)(2,1)S(1)}, bf16[3,512,128]{2,1,0:T(8,128)(2,1)S(1)}, bf16[544,512]{1,0:T(8,128)(2,1)S(1)}) custom-call(s32[11]{0:T(128)S(1)} %concatenate.6.place_ref, bf16[2,4096,1024]{2,1,0:T(8,128)(2,1)} %w_ref.5, bf16[1024,128]{1,0:T(8,128)(2,1)S(1)} %get-tuple-element.86.gained_ref, ...), custom_call_target="tpu_custom_call" | custom-call | bytes 8388608 | tf_op jit(solution)/shard_map/project_gate/pallas_call | solution.py:61
  25.8 4.1 %collective-permute-done.5.refs_1_ = bf16[528,128]{1,0:T(8,128)(2,1)S(1)} collective-permute-done((bf16[528,128]{1,0:T(8,128)(2,1)S(1)}, bf16[528,128]{1,0:T(8,128)(2,1)S(1)}, u32[]{:S(2)}, u32[]{:S(2)}) %collective-permute-start.5) | collective-permute-done | bytes 135200 | tf_op jit(solution)/shard_map/ppermute | solution.py:17
  33.5 3.7 %collective-permute-start.10 = (bf16[784,128]{1,0:T(8,128)(2,1)S(1)}, bf16[784,128]{1,0:T(8,128)(2,1)S(1)}, u32[]{:S(2)}, u32[]{:S(2)}) collective-permute-start(bf16[784,128]{1,0:T(8,128)(2,1)S(1)} %get-tuple-element.114), channel_id=1, source_target_pairs={{0,4},{1,5},{2,6},{3,7},{4,0},{5,1},{6,2},{7,3},{8,12},{9,13},{10,... | collective-permute-start | bytes 602120 | tf_op jit(solution)/shard_map/ppermute | solution.py:17
  38.7 2.3 %collective-permute-start.15 = (bf16[512,128]{1,0:T(8,128)(2,1)S(1)}, bf16[512,128]{1,0:T(8,128)(2,1)S(1)}, u32[]{:S(2)}, u32[]{:S(2)}) collective-permute-start(bf16[512,128]{1,0:T(8,128)(2,1)S(1)} %get-tuple-element.116), channel_id=1, source_target_pairs={{0,6},{1,7},{2,4},{3,5},{4,2},{5,3},{6,0},{7,1},{8,14},{9,15},{10,... | collective-permute-start | bytes 393224 | tf_op jit(solution)/shard_map/ppermute | solution.py:17
  41.0 9.2 %collective-permute-done.11 = bf16[272,128]{1,0:T(8,128)(2,1)S(1)} collective-permute-done((bf16[272,128]{1,0:T(8,128)(2,1)S(1)}, bf16[272,128]{1,0:T(8,128)(2,1)S(1)}, u32[]{:S(2)}, u32[]{:S(2)}) %collective-permute-start.11) | collective-permute-done | bytes 69664 | tf_op jit(solution)/shard_map/ppermute | solution.py:17
  53.9 3.5 %ready_state.1.state_ref = f32[16,512,128]{2,1,0:T(8,128)S(1)} custom-call(s32[11]{0:T(128)S(1)} %concatenate.6.place_ref, bf16[512,16,128]{2,1,0:T(8,128)(2,1)} %state_ref.1, f32[8,128]{1,0:T(8,128)S(1)} %broadcast_in_dim.66.refs_5_.alive_ref, bf16[272,128]{1,0:T(8,128)(2,1)S(1)} %fusion.20.earlier_ref), custom_call_target="tpu_custom_call" | custom-call | bytes 6291456 | tf_op jit(solution)/shard_map/ready_state/pallas_call | solution.py:61
  59.3 4.5 %scan.1 = (bf16[512,16,128]{2,1,0:T(8,128)(2,1)}, bf16[128,512]{1,0:T(8,128)(2,1)S(1)}) custom-call(s32[11]{0:T(128)S(1)} %concatenate.6.place_ref, bf16[272,128]{1,0:T(8,128)(2,1)S(1)} %add_convert_fusion.mine_ref, bf16[272,128]{1,0:T(8,128)(2,1)S(1)} %collective-permute-done.16.other_ref, bf16[512,512]{1,0:T(8,128)(2,1)S(1)} %bitcast.36, ...), custom_call_target="tpu_custom_call" | custom-call | tf_op jit(solution)/shard_map/scan/pallas_call | solution.py:441
  63.9 2.4 %collective-permute-start.20 = (bf16[128,512]{1,0:T(8,128)(2,1)S(1)}, bf16[128,512]{1,0:T(8,128)(2,1)S(1)}, u32[]{:S(2)}, u32[]{:S(2)}) collective-permute-start(bf16[128,512]{1,0:T(8,128)(2,1)S(1)} %get-tuple-element.129.earlier_ref.refs_0_), channel_id=1, source_target_pairs={{0,4},{1,5},{2,6},{3,7},{4,0},{5,1},{6,2},{7,3},{8,12},{9,13},{10,... | collective-permute-start | bytes 393224 | tf_op jit(solution)/shard_map/ppermute | solution.py:17
  66.2 3.5 %collective-permute-start.21 = (bf16[128,512]{1,0:T(8,128)(2,1)S(1)}, bf16[128,512]{1,0:T(8,128)(2,1)S(1)}, u32[]{:S(2)}, u32[]{:S(2)}) collective-permute-start(bf16[128,512]{1,0:T(8,128)(2,1)S(1)} %get-tuple-element.129.earlier_ref.refs_0_), channel_id=1, source_target_pairs={{0,6},{1,7},{2,4},{3,5},{4,2},{5,3},{6,0},{7,1},{8,14},{9,15},{10,... | collective-permute-start | bytes 393224 | tf_op jit(solution)/shard_map/ppermute | solution.py:17
  69.7 4.0 %stage_mix.1.refs_8_ = bf16[8,512,1024]{2,1,0:T(8,128)(2,1)S(1)} custom-call(s32[11]{0:T(128)S(1)} %concatenate.6.place_ref, bf16[4096,1024]{1,0:T(8,128)(2,1)} %w_ref.6, bf16[128,512]{1,0:T(8,128)(2,1)S(1)} %get-tuple-element.129.earlier_ref.refs_0_), custom_call_target="tpu_custom_call" | custom-call | bytes 8388608 | tf_op jit(solution)/shard_map/stage_mix/pallas_call | solution.py:61
  74.8 1.7 %collective-permute-done.20.refs_4_ = bf16[128,512]{1,0:T(8,128)(2,1)S(1)} collective-permute-done((bf16[128,512]{1,0:T(8,128)(2,1)S(1)}, bf16[128,512]{1,0:T(8,128)(2,1)S(1)}, u32[]{:S(2)}, u32[]{:S(2)}) %collective-permute-start.20) | collective-permute-done | bytes 131104 | tf_op jit(solution)/shard_map/ppermute | solution.py:17
  79.2 1.8 %mix_out.1 = (f32[32,1024]{1,0:T(8,128)S(1)}, bf16[32,1024]{1,0:T(8,128)(2,1)S(1)}, bf16[32,1024]{1,0:T(8,128)(2,1)S(1)}, bf16[32,1024]{1,0:T(8,128)(2,1)S(1)}) custom-call(s32[11]{0:T(128)S(1)} %concatenate.6.place_ref, bf16[128,512]{1,0:T(8,128)(2,1)S(1)} %get-tuple-element.129.earlier_ref.refs_0_, bf16[128,512]{1,0:T(8,128)(2,1)S(1)} %collective-permute-done.17.refs_1_, ...), custom_call_target="tpu_custom_call" | custom-call | tf_op jit(solution)/shard_map/mix_out/pallas_call | solution.py:61
  82.9 1.7 %collective-permute-start.26 = (bf16[32,1024]{1,0:T(8,128)(2,1)S(1)}, bf16[32,1024]{1,0:T(8,128)(2,1)S(1)}, u32[]{:S(2)}, u32[]{:S(2)}) collective-permute-start(bf16[32,1024]{1,0:T(8,128)(2,1)S(1)} %get-tuple-element.137), channel_id=1, source_target_pairs={{0,24},{8,16},{16,8},{24,0},{1,25},{9,17},{17,9},{25,1},{2,26},{10... | collective-permute-start | bytes 196616 | tf_op jit(solution)/shard_map/ppermute | solution.py:17
  85.9 2.2 %collective-permute-done.26 = bf16[32,1024]{1,0:T(8,128)(2,1)S(1)} collective-permute-done((bf16[32,1024]{1,0:T(8,128)(2,1)S(1)}, bf16[32,1024]{1,0:T(8,128)(2,1)S(1)}, u32[]{:S(2)}, u32[]{:S(2)}) %collective-permute-start.26) | collective-permute-done | bytes 65568 | tf_op jit(solution)/shard_map/ppermute | solution.py:17
  93.5 2.1 %collective-permute-done.29.refs_3_ = bf16[32,1024]{1,0:T(8,128)(2,1)S(1)} collective-permute-done((bf16[32,1024]{1,0:T(8,128)(2,1)S(1)}, bf16[32,1024]{1,0:T(8,128)(2,1)S(1)}, u32[]{:S(2)}, u32[]{:S(2)}) %collective-permute-start.29) | collective-permute-done | bytes 65568 | tf_op jit(solution)/shard_map/ppermute | solution.py:17
  95.6 1.9 %query.1 = (bf16[64,2688]{1,0:T(8,128)(2,1)S(1)}, bf16[64,2688]{1,0:T(8,128)(2,1)S(1)}) custom-call(s32[11]{0:T(128)S(1)} %concatenate.6.place_ref, bf16[32,1024]{1,0:T(8,128)(2,1)S(1)} %add_convert_fusion.2.refs_0_, bf16[32,1024]{1,0:T(8,128)(2,1)S(1)} %collective-permute-done.27.refs_1_, bf16[32,1024]{1,0:T(8,128)(2,1)S(1)} %collective-permute-done.28.refs_2_, ...), custom_call_target="tpu_custom_call" | custom-call | tf_op jit(solution)/shard_map/query/pallas_call | solution.py:61
  99.9 2.2 %collective-permute-start.31 = (bf16[16,2688]{1,0:T(8,128)(2,1)S(1)}, bf16[16,2688]{1,0:T(8,128)(2,1)S(1)}, u32[]{:S(2)}, u32[]{:S(2)}) collective-permute-start(bf16[16,2688]{1,0:T(8,128)(2,1)S(1)} %get-tuple-element.142), channel_id=1, source_target_pairs={{0,2},{1,3},{2,0},{3,1},{4,6},{5,7},{6,4},{7,5},{8,10},{9,11},{10,... | collective-permute-start | bytes 258056 | tf_op jit(solution)/shard_map/ppermute | solution.py:17
  102.0 1.8 %collective-permute-start.32 = (bf16[16,2688]{1,0:T(8,128)(2,1)S(1)}, bf16[16,2688]{1,0:T(8,128)(2,1)S(1)}, u32[]{:S(2)}, u32[]{:S(2)}) collective-permute-start(bf16[16,2688]{1,0:T(8,128)(2,1)S(1)} %get-tuple-element.143), channel_id=1, source_target_pairs={{0,4},{1,5},{2,6},{3,7},{4,0},{5,1},{6,2},{7,3},{8,12},{9,13},{10,... | collective-permute-start | bytes 258056 | tf_op jit(solution)/shard_map/ppermute | solution.py:17
  105.3 3.0 %collective-permute-done.32 = bf16[16,2688]{1,0:T(8,128)(2,1)S(1)} collective-permute-done((bf16[16,2688]{1,0:T(8,128)(2,1)S(1)}, bf16[16,2688]{1,0:T(8,128)(2,1)S(1)}, u32[]{:S(2)}, u32[]{:S(2)}) %collective-permute-start.32) | collective-permute-done | bytes 86048 | tf_op jit(solution)/shard_map/ppermute | solution.py:17
  108.4 3.2 %collective-permute-done.33 = bf16[16,2688]{1,0:T(8,128)(2,1)S(1)} collective-permute-done((bf16[16,2688]{1,0:T(8,128)(2,1)S(1)}, bf16[16,2688]{1,0:T(8,128)(2,1)S(1)}, u32[]{:S(2)}, u32[]{:S(2)}) %collective-permute-start.33) | collective-permute-done | bytes 86048 | tf_op jit(solution)/shard_map/ppermute | solution.py:17
  113.3 3.4 %collective-permute-start.37 = (bf16[16,2048]{1,0:T(8,128)(2,1)S(1)}, bf16[16,2048]{1,0:T(8,128)(2,1)S(1)}, u32[]{:S(2)}, u32[]{:S(2)}) collective-permute-start(bf16[16,2048]{1,0:T(8,128)(2,1)S(1)} %bitcast.37), channel_id=1, source_target_pairs={{0,4},{1,5},{2,6},{3,7},{4,0},{5,1},{6,2},{7,3},{8,12},{9,13},{10,... | collective-permute-start | bytes 196616 | tf_op jit(solution)/shard_map/ppermute | solution.py:17
  117.7 2.7 %stage_head.1.refs_9_ = bf16[4,512,1024]{2,1,0:T(8,128)(2,1)S(1)} custom-call(s32[11]{0:T(128)S(1)} %concatenate.6.place_ref, bf16[2048,1024]{1,0:T(8,128)(2,1)} %w_ref.7, bf16[16,2048]{1,0:T(8,128)(2,1)S(1)} %bitcast.41), custom_call_target="tpu_custom_call" | custom-call | bytes 4194304 | tf_op jit(solution)/shard_map/stage_head/pallas_call | solution.py:61
  120.7 2.3 %collective-permute-done.38.refs_6_ = bf16[16,2048]{1,0:T(8,128)(2,1)S(1)} collective-permute-done((bf16[16,2048]{1,0:T(8,128)(2,1)S(1)}, bf16[16,2048]{1,0:T(8,128)(2,1)S(1)}, u32[]{:S(2)}, u32[]{:S(2)}) %collective-permute-start.38) | collective-permute-done | bytes 65568 | tf_op jit(solution)/shard_map/ppermute | solution.py:17
  124.8 1.9 %head_out.1 = (f32[32,1024]{1,0:T(8,128)S(1)}, bf16[32,1024]{1,0:T(8,128)(2,1)S(1)}, bf16[32,1024]{1,0:T(8,128)(2,1)S(1)}, bf16[32,1024]{1,0:T(8,128)(2,1)S(1)}) custom-call(s32[11]{0:T(128)S(1)} %concatenate.6.place_ref, bf16[16,2048]{1,0:T(8,128)(2,1)S(1)} %bitcast.42, bf16[16,2048]{1,0:T(8,128)(2,1)S(1)} %collective-permute-done.34.refs_1_, ...), custom_call_target="tpu_custom_call" | custom-call | tf_op jit(solution)/shard_map/head_out/pallas_call | solution.py:61
  128.6 1.7 %collective-permute-start.43 = (bf16[32,1024]{1,0:T(8,128)(2,1)S(1)}, bf16[32,1024]{1,0:T(8,128)(2,1)S(1)}, u32[]{:S(2)}, u32[]{:S(2)}) collective-permute-start(bf16[32,1024]{1,0:T(8,128)(2,1)S(1)} %get-tuple-element.151), channel_id=1, source_target_pairs={{0,24},{8,16},{16,8},{24,0},{1,25},{9,17},{17,9},{25,1},{2,26},{10... | collective-permute-start | bytes 196616 | tf_op jit(solution)/shard_map/ppermute | solution.py:17
  131.6 2.1 %collective-permute-done.43 = bf16[32,1024]{1,0:T(8,128)(2,1)S(1)} collective-permute-done((bf16[32,1024]{1,0:T(8,128)(2,1)S(1)}, bf16[32,1024]{1,0:T(8,128)(2,1)S(1)}, u32[]{:S(2)}, u32[]{:S(2)}) %collective-permute-start.43) | collective-permute-done | bytes 65568 | tf_op jit(solution)/shard_map/ppermute | solution.py:17
  (132 shorter events, 39.8 us)
Async XLA Ops:
  0.6 8.7 %collective-permute-start = (bf16[32,1024]{1,0:T(8,128)(2,1)}, bf16[32,1024]{1,0:T(8,128)(2,1)S(1)}, u32[]{:S(2)}, u32[]{:S(2)}) collective-permute-start(bf16[32,1024]{1,0:T(8,128)(2,1)} %hidden_ref.1), channel_id=1, source_target_pairs={{0,8},{8,0},{16,24},{24,16},{1,9},{9,1},{17,25},{25,17},{2,10},{10... | collective-permute-start | bytes 196616 | tf_op jit(solution)/shard_map/ppermute | solution.py:17
  3.6 5.7 %collective-permute-start.1 = (bf16[32,1024]{1,0:T(8,128)(2,1)}, bf16[32,1024]{1,0:T(8,128)(2,1)S(1)}, u32[]{:S(2)}, u32[]{:S(2)}) collective-permute-start(bf16[32,1024]{1,0:T(8,128)(2,1)} %hidden_ref.1), channel_id=1, source_target_pairs={{0,16},{8,24},{16,0},{24,8},{1,17},{9,25},{17,1},{25,9},{2,18},{10... | collective-permute-start | bytes 196616 | tf_op jit(solution)/shard_map/ppermute | solution.py:17
  5.2 5.4 %collective-permute-start.2 = (bf16[32,1024]{1,0:T(8,128)(2,1)}, bf16[32,1024]{1,0:T(8,128)(2,1)S(1)}, u32[]{:S(2)}, u32[]{:S(2)}) collective-permute-start(bf16[32,1024]{1,0:T(8,128)(2,1)} %hidden_ref.1), channel_id=1, source_target_pairs={{0,24},{8,16},{16,8},{24,0},{1,25},{9,17},{17,9},{25,1},{2,26},{10... | collective-permute-start | bytes 196616 | tf_op jit(solution)/shard_map/ppermute | solution.py:17
  15.2 10.7 %collective-permute-start.4 = (bf16[528,128]{1,0:T(8,128)(2,1)S(1)}, bf16[528,128]{1,0:T(8,128)(2,1)S(1)}, u32[]{:S(2)}, u32[]{:S(2)}) collective-permute-start(bf16[528,128]{1,0:T(8,128)(2,1)S(1)} %get-tuple-element.90.earlier_ref), channel_id=1, source_target_pairs={{0,2},{1,3},{2,0},{3,1},{4,6},{5,7},{6,4},{7,5},{8,10},{9,11},{10,... | collective-permute-start | bytes 405512 | tf_op jit(solution)/shard_map/ppermute | solution.py:17
  16.8 13.2 %collective-permute-start.5 = (bf16[528,128]{1,0:T(8,128)(2,1)S(1)}, bf16[528,128]{1,0:T(8,128)(2,1)S(1)}, u32[]{:S(2)}, u32[]{:S(2)}) collective-permute-start(bf16[528,128]{1,0:T(8,128)(2,1)S(1)} %get-tuple-element.91), channel_id=1, source_target_pairs={{0,4},{1,5},{2,6},{3,7},{4,0},{5,1},{6,2},{7,3},{8,12},{9,13},{10,... | collective-permute-start | bytes 405512 | tf_op jit(solution)/shard_map/ppermute | solution.py:17
  19.4 10.6 %collective-permute-start.6 = (bf16[528,128]{1,0:T(8,128)(2,1)S(1)}, bf16[528,128]{1,0:T(8,128)(2,1)S(1)}, u32[]{:S(2)}, u32[]{:S(2)}) collective-permute-start(bf16[528,128]{1,0:T(8,128)(2,1)S(1)} %get-tuple-element.92), channel_id=1, source_target_pairs={{0,6},{1,7},{2,4},{3,5},{4,2},{5,3},{6,0},{7,1},{8,14},{9,15},{10,... | collective-permute-start | bytes 405512 | tf_op jit(solution)/shard_map/ppermute | solution.py:17
  33.5 16.8 %collective-permute-start.10 = (bf16[784,128]{1,0:T(8,128)(2,1)S(1)}, bf16[784,128]{1,0:T(8,128)(2,1)S(1)}, u32[]{:S(2)}, u32[]{:S(2)}) collective-permute-start(bf16[784,128]{1,0:T(8,128)(2,1)S(1)} %get-tuple-element.114), channel_id=1, source_target_pairs={{0,4},{1,5},{2,6},{3,7},{4,0},{5,1},{6,2},{7,3},{8,12},{9,13},{10,... | collective-permute-start | bytes 602120 | tf_op jit(solution)/shard_map/ppermute | solution.py:17
  37.2 13.1 %collective-permute-start.9 = (bf16[784,128]{1,0:T(8,128)(2,1)S(1)}, bf16[784,128]{1,0:T(8,128)(2,1)S(1)}, u32[]{:S(2)}, u32[]{:S(2)}) collective-permute-start(bf16[784,128]{1,0:T(8,128)(2,1)S(1)} %get-tuple-element.113), channel_id=1, source_target_pairs={{0,2},{1,3},{2,0},{3,1},{4,6},{5,7},{6,4},{7,5},{8,10},{9,11},{10,... | collective-permute-start | bytes 602120 | tf_op jit(solution)/shard_map/ppermute | solution.py:17
  37.2 13.1 %collective-permute-start.11 = (bf16[272,128]{1,0:T(8,128)(2,1)S(1)}, bf16[272,128]{1,0:T(8,128)(2,1)S(1)}, u32[]{:S(2)}, u32[]{:S(2)}) collective-permute-start(bf16[272,128]{1,0:T(8,128)(2,1)S(1)} %get-tuple-element.115), channel_id=1, source_target_pairs={{0,6},{1,7},{2,4},{3,5},{4,2},{5,3},{6,0},{7,1},{8,14},{9,15},{10,... | collective-permute-start | bytes 208904 | tf_op jit(solution)/shard_map/ppermute | solution.py:17
  38.7 18.6 %collective-permute-start.15 = (bf16[512,128]{1,0:T(8,128)(2,1)S(1)}, bf16[512,128]{1,0:T(8,128)(2,1)S(1)}, u32[]{:S(2)}, u32[]{:S(2)}) collective-permute-start(bf16[512,128]{1,0:T(8,128)(2,1)S(1)} %get-tuple-element.116), channel_id=1, source_target_pairs={{0,6},{1,7},{2,4},{3,5},{4,2},{5,3},{6,0},{7,1},{8,14},{9,15},{10,... | collective-permute-start | bytes 393224 | tf_op jit(solution)/shard_map/ppermute | solution.py:17
  50.3 7.0 %collective-permute-start.12 = (bf16[272,128]{1,0:T(8,128)(2,1)S(1)}, bf16[272,128]{1,0:T(8,128)(2,1)S(1)}, u32[]{:S(2)}, u32[]{:S(2)}) collective-permute-start(bf16[272,128]{1,0:T(8,128)(2,1)S(1)} %fusion.20.earlier_ref), channel_id=1, source_target_pairs={{0,8},{8,0},{16,24},{24,16},{1,9},{9,1},{17,25},{25,17},{2,10},{10... | collective-permute-start | bytes 208904 | tf_op jit(solution)/shard_map/ppermute | solution.py:17
  51.1 6.2 %collective-permute-start.13 = (bf16[272,128]{1,0:T(8,128)(2,1)S(1)}, bf16[272,128]{1,0:T(8,128)(2,1)S(1)}, u32[]{:S(2)}, u32[]{:S(2)}) collective-permute-start(bf16[272,128]{1,0:T(8,128)(2,1)S(1)} %fusion.20.earlier_ref), channel_id=1, source_target_pairs={{0,16},{8,24},{16,0},{24,8},{1,17},{9,25},{17,1},{25,9},{2,18},{10... | collective-permute-start | bytes 208904 | tf_op jit(solution)/shard_map/ppermute | solution.py:17
  52.7 5.2 %collective-permute-start.14 = (bf16[272,128]{1,0:T(8,128)(2,1)S(1)}, bf16[272,128]{1,0:T(8,128)(2,1)S(1)}, u32[]{:S(2)}, u32[]{:S(2)}) collective-permute-start(bf16[272,128]{1,0:T(8,128)(2,1)S(1)} %fusion.20.earlier_ref), channel_id=1, source_target_pairs={{0,24},{8,16},{16,8},{24,0},{1,25},{9,17},{17,9},{25,1},{2,26},{10... | collective-permute-start | bytes 208904 | tf_op jit(solution)/shard_map/ppermute | solution.py:17
  63.9 12.7 %collective-permute-start.20 = (bf16[128,512]{1,0:T(8,128)(2,1)S(1)}, bf16[128,512]{1,0:T(8,128)(2,1)S(1)}, u32[]{:S(2)}, u32[]{:S(2)}) collective-permute-start(bf16[128,512]{1,0:T(8,128)(2,1)S(1)} %get-tuple-element.129.earlier_ref.refs_0_), channel_id=1, source_target_pairs={{0,4},{1,5},{2,6},{3,7},{4,0},{5,1},{6,2},{7,3},{8,12},{9,13},{10,... | collective-permute-start | bytes 393224 | tf_op jit(solution)/shard_map/ppermute | solution.py:17
  66.2 10.7 %collective-permute-start.21 = (bf16[128,512]{1,0:T(8,128)(2,1)S(1)}, bf16[128,512]{1,0:T(8,128)(2,1)S(1)}, u32[]{:S(2)}, u32[]{:S(2)}) collective-permute-start(bf16[128,512]{1,0:T(8,128)(2,1)S(1)} %get-tuple-element.129.earlier_ref.refs_0_), channel_id=1, source_target_pairs={{0,6},{1,7},{2,4},{3,5},{4,2},{5,3},{6,0},{7,1},{8,14},{9,15},{10,... | collective-permute-start | bytes 393224 | tf_op jit(solution)/shard_map/ppermute | solution.py:17
  69.7 8.1 %collective-permute-start.18 = (bf16[128,512]{1,0:T(8,128)(2,1)S(1)}, bf16[128,512]{1,0:T(8,128)(2,1)S(1)}, u32[]{:S(2)}, u32[]{:S(2)}) collective-permute-start(bf16[128,512]{1,0:T(8,128)(2,1)S(1)} %get-tuple-element.129.earlier_ref.refs_0_), channel_id=1, source_target_pairs={{0,2},{1,3},{2,0},{3,1},{4,6},{5,7},{6,4},{7,5},{8,10},{9,11},{10,... | collective-permute-start | bytes 393224 | tf_op jit(solution)/shard_map/ppermute | solution.py:17
  69.7 8.1 %collective-permute-start.17 = (bf16[128,512]{1,0:T(8,128)(2,1)S(1)}, bf16[128,512]{1,0:T(8,128)(2,1)S(1)}, u32[]{:S(2)}, u32[]{:S(2)}) collective-permute-start(bf16[128,512]{1,0:T(8,128)(2,1)S(1)} %get-tuple-element.129.earlier_ref.refs_0_), channel_id=1, source_target_pairs={{0,1},{1,0},{2,3},{3,2},{4,5},{5,4},{6,7},{7,6},{8,9},{9,8},{10,11... | collective-permute-start | bytes 393224 | tf_op jit(solution)/shard_map/ppermute | solution.py:17
  81.0 4.5 %collective-permute-start.24 = (bf16[32,1024]{1,0:T(8,128)(2,1)S(1)}, bf16[32,1024]{1,0:T(8,128)(2,1)S(1)}, u32[]{:S(2)}, u32[]{:S(2)}) collective-permute-start(bf16[32,1024]{1,0:T(8,128)(2,1)S(1)} %get-tuple-element.135), channel_id=1, source_target_pairs={{0,8},{8,0},{16,24},{24,16},{1,9},{9,1},{17,25},{25,17},{2,10},{10... | collective-permute-start | bytes 196616 | tf_op jit(solution)/shard_map/ppermute | solution.py:17
  82.9 5.2 %collective-permute-start.26 = (bf16[32,1024]{1,0:T(8,128)(2,1)S(1)}, bf16[32,1024]{1,0:T(8,128)(2,1)S(1)}, u32[]{:S(2)}, u32[]{:S(2)}) collective-permute-start(bf16[32,1024]{1,0:T(8,128)(2,1)S(1)} %get-tuple-element.137), channel_id=1, source_target_pairs={{0,24},{8,16},{16,8},{24,0},{1,25},{9,17},{17,9},{25,1},{2,26},{10... | collective-permute-start | bytes 196616 | tf_op jit(solution)/shard_map/ppermute | solution.py:17
  88.1 4.3 %collective-permute-start.27 = (bf16[32,1024]{1,0:T(8,128)(2,1)S(1)}, bf16[32,1024]{1,0:T(8,128)(2,1)S(1)}, u32[]{:S(2)}, u32[]{:S(2)}) collective-permute-start(bf16[32,1024]{1,0:T(8,128)(2,1)S(1)} %add_convert_fusion.2.refs_0_), channel_id=1, source_target_pairs={{0,8},{8,0},{16,24},{24,16},{1,9},{9,1},{17,25},{25,17},{2,10},{10... | collective-permute-start | bytes 196616 | tf_op jit(solution)/shard_map/ppermute | solution.py:17
  88.9 4.6 %collective-permute-start.28 = (bf16[32,1024]{1,0:T(8,128)(2,1)S(1)}, bf16[32,1024]{1,0:T(8,128)(2,1)S(1)}, u32[]{:S(2)}, u32[]{:S(2)}) collective-permute-start(bf16[32,1024]{1,0:T(8,128)(2,1)S(1)} %add_convert_fusion.2.refs_0_), channel_id=1, source_target_pairs={{0,16},{8,24},{16,0},{24,8},{1,17},{9,25},{17,1},{25,9},{2,18},{10... | collective-permute-start | bytes 196616 | tf_op jit(solution)/shard_map/ppermute | solution.py:17
  90.4 5.2 %collective-permute-start.29 = (bf16[32,1024]{1,0:T(8,128)(2,1)S(1)}, bf16[32,1024]{1,0:T(8,128)(2,1)S(1)}, u32[]{:S(2)}, u32[]{:S(2)}) collective-permute-start(bf16[32,1024]{1,0:T(8,128)(2,1)S(1)} %add_convert_fusion.2.refs_0_), channel_id=1, source_target_pairs={{0,24},{8,16},{16,8},{24,0},{1,25},{9,17},{17,9},{25,1},{2,26},{10... | collective-permute-start | bytes 196616 | tf_op jit(solution)/shard_map/ppermute | solution.py:17
  99.9 5.5 %collective-permute-start.31 = (bf16[16,2688]{1,0:T(8,128)(2,1)S(1)}, bf16[16,2688]{1,0:T(8,128)(2,1)S(1)}, u32[]{:S(2)}, u32[]{:S(2)}) collective-permute-start(bf16[16,2688]{1,0:T(8,128)(2,1)S(1)} %get-tuple-element.142), channel_id=1, source_target_pairs={{0,2},{1,3},{2,0},{3,1},{4,6},{5,7},{6,4},{7,5},{8,10},{9,11},{10,... | collective-permute-start | bytes 258056 | tf_op jit(solution)/shard_map/ppermute | solution.py:17
  102.0 6.3 %collective-permute-start.32 = (bf16[16,2688]{1,0:T(8,128)(2,1)S(1)}, bf16[16,2688]{1,0:T(8,128)(2,1)S(1)}, u32[]{:S(2)}, u32[]{:S(2)}) collective-permute-start(bf16[16,2688]{1,0:T(8,128)(2,1)S(1)} %get-tuple-element.143), channel_id=1, source_target_pairs={{0,4},{1,5},{2,6},{3,7},{4,0},{5,1},{6,2},{7,3},{8,12},{9,13},{10,... | collective-permute-start | bytes 258056 | tf_op jit(solution)/shard_map/ppermute | solution.py:17
  103.9 7.7 %collective-permute-start.33 = (bf16[16,2688]{1,0:T(8,128)(2,1)S(1)}, bf16[16,2688]{1,0:T(8,128)(2,1)S(1)}, u32[]{:S(2)}, u32[]{:S(2)}) collective-permute-start(bf16[16,2688]{1,0:T(8,128)(2,1)S(1)} %get-tuple-element.144), channel_id=1, source_target_pairs={{0,6},{1,7},{2,4},{3,5},{4,2},{5,3},{6,0},{7,1},{8,14},{9,15},{10,... | collective-permute-start | bytes 258056 | tf_op jit(solution)/shard_map/ppermute | solution.py:17
  113.3 7.4 %collective-permute-start.37 = (bf16[16,2048]{1,0:T(8,128)(2,1)S(1)}, bf16[16,2048]{1,0:T(8,128)(2,1)S(1)}, u32[]{:S(2)}, u32[]{:S(2)}) collective-permute-start(bf16[16,2048]{1,0:T(8,128)(2,1)S(1)} %bitcast.37), channel_id=1, source_target_pairs={{0,4},{1,5},{2,6},{3,7},{4,0},{5,1},{6,2},{7,3},{8,12},{9,13},{10,... | collective-permute-start | bytes 196616 | tf_op jit(solution)/shard_map/ppermute | solution.py:17
  116.7 6.3 %collective-permute-start.38 = (bf16[16,2048]{1,0:T(8,128)(2,1)S(1)}, bf16[16,2048]{1,0:T(8,128)(2,1)S(1)}, u32[]{:S(2)}, u32[]{:S(2)}) collective-permute-start(bf16[16,2048]{1,0:T(8,128)(2,1)S(1)} %bitcast.38), channel_id=1, source_target_pairs={{0,6},{1,7},{2,4},{3,5},{4,2},{5,3},{6,0},{7,1},{8,14},{9,15},{10,... | collective-permute-start | bytes 196616 | tf_op jit(solution)/shard_map/ppermute | solution.py:17
  117.7 5.9 %collective-permute-start.35 = (bf16[16,2048]{1,0:T(8,128)(2,1)S(1)}, bf16[16,2048]{1,0:T(8,128)(2,1)S(1)}, u32[]{:S(2)}, u32[]{:S(2)}) collective-permute-start(bf16[16,2048]{1,0:T(8,128)(2,1)S(1)} %bitcast.39), channel_id=1, source_target_pairs={{0,2},{1,3},{2,0},{3,1},{4,6},{5,7},{6,4},{7,5},{8,10},{9,11},{10,... | collective-permute-start | bytes 196616 | tf_op jit(solution)/shard_map/ppermute | solution.py:17
  117.7 5.9 %collective-permute-start.34 = (bf16[16,2048]{1,0:T(8,128)(2,1)S(1)}, bf16[16,2048]{1,0:T(8,128)(2,1)S(1)}, u32[]{:S(2)}, u32[]{:S(2)}) collective-permute-start(bf16[16,2048]{1,0:T(8,128)(2,1)S(1)} %bitcast.40), channel_id=1, source_target_pairs={{0,1},{1,0},{2,3},{3,2},{4,5},{5,4},{6,7},{7,6},{8,9},{9,8},{10,11... | collective-permute-start | bytes 196616 | tf_op jit(solution)/shard_map/ppermute | solution.py:17
  126.7 4.9 %collective-permute-start.41 = (bf16[32,1024]{1,0:T(8,128)(2,1)S(1)}, bf16[32,1024]{1,0:T(8,128)(2,1)S(1)}, u32[]{:S(2)}, u32[]{:S(2)}) collective-permute-start(bf16[32,1024]{1,0:T(8,128)(2,1)S(1)} %get-tuple-element.149), channel_id=1, source_target_pairs={{0,8},{8,0},{16,24},{24,16},{1,9},{9,1},{17,25},{25,17},{2,10},{10... | collective-permute-start | bytes 196616 | tf_op jit(solution)/shard_map/ppermute | solution.py:17
  127.3 4.3 %collective-permute-start.42 = (bf16[32,1024]{1,0:T(8,128)(2,1)S(1)}, bf16[32,1024]{1,0:T(8,128)(2,1)S(1)}, u32[]{:S(2)}, u32[]{:S(2)}) collective-permute-start(bf16[32,1024]{1,0:T(8,128)(2,1)S(1)} %get-tuple-element.150), channel_id=1, source_target_pairs={{0,16},{8,24},{16,0},{24,8},{1,17},{9,25},{17,1},{25,9},{2,18},{10... | collective-permute-start | bytes 196616 | tf_op jit(solution)/shard_map/ppermute | solution.py:17
  128.6 5.2 %collective-permute-start.43 = (bf16[32,1024]{1,0:T(8,128)(2,1)S(1)}, bf16[32,1024]{1,0:T(8,128)(2,1)S(1)}, u32[]{:S(2)}, u32[]{:S(2)}) collective-permute-start(bf16[32,1024]{1,0:T(8,128)(2,1)S(1)} %get-tuple-element.151), channel_id=1, source_target_pairs={{0,24},{8,16},{16,8},{24,0},{1,25},{9,17},{17,9},{25,1},{2,26},{10... | collective-permute-start | bytes 196616 | tf_op jit(solution)/shard_map/ppermute | solution.py:17
  (26 other events, 188.7 us)

commit v3 on v2

--- a/solution.py
+++ b/solution.py
@@ -17,21 +17,28 @@
     return lax.ppermute(value, axis, [(i, i ^ bits) for i in range(size)])
 
 
-def swaps_gx(values):
-    return [swap(v, "gx", k + 1) for k, v in enumerate(values)]
-
-
-def swaps_chip(values):
-    return [swap(v, "yz", 2 * (k + 1)) for k, v in enumerate(values)]
-
-
-def gather_yz(value, *staged):
-    chips = lax.axis_size("yz") // 2
-    got = swaps_chip([value] * (chips - 1))
-    *got[1:], staged = lax.optimization_barrier((*got[1:], staged))
+def exchange(values, axis, step, order, depths):
+    count = len(values)
+    order = [k for k in order if k < count] + [k for k in range(count) if k not in order]
+    got = {k: swap(values[k], axis, (k + 1) * step) for k in order}
+    for k, depth in enumerate(depths[:count]):
+        for _ in range(depth):
+            got[k] = lax.optimization_barrier(got[k])
+    return [got[k] for k in range(count)]
+
+
+def swaps_gx(values, order=(2, 0, 1), depths=(1, 0, 2)):
+    return exchange(values, "gx", 1, order, depths)
+
+
+def swaps_chip(values, order=(2, 1, 0), depths=(0, 1, 2)):
+    return exchange(values, "yz", 2, order, depths)
+
+
+def gather_yz(value, got):
     mine = [value] + got
     other = [swap(v, "yz", 1) for v in mine]
-    return [v for pair in zip(mine, other) for v in pair], staged
+    return [v for pair in zip(mine, other) for v in pair]
 
 
 def dot(a, b, dims=((1,), (0,)), **kw):
@@ -640,7 +647,7 @@
     group_count, group_cols = attention_projection.shape[1:]
     slot_count = kv_cache.shape[0]
 
-    got = swaps_gx([hidden_in] * (gx - 1))
+    got = swaps_gx([hidden_in] * (gx - 1), (0, 1, 2), (1, 2, 0))
     weights, hidden_here, gain = stage_first(
         place, mixer_projection, hidden_in, norm_gain_a[None, :], own, chips
     )
@@ -652,7 +659,7 @@
     received = swap(give.reshape(tall, batch), "yz", 1)
     keep = project_keep(place, weights, gained, squares, chips)
     xown, wires = add_pairs(keep.reshape(tall, batch), received, chips, place, "add_x")
-    xgot = swaps_chip(wires)
+    xgot = swaps_chip(wires, (1, 2, 0), (2, 0, 0))
     give, keep, conv_rows, x_cols = project_gate(
         place, mixer_projection, gained, conv_rows, x_cols, own, chips, wires[0]
     )
@@ -679,12 +686,13 @@
     )
     got = swaps_chip(wires)
     half = part.shape[0]
+    old = ready_state(place, ssm_state, alive, part)
+    got, old, z_last = lax.optimization_barrier((got, old, z_last))
     part = total_of(part, [g[:half] for g in got])
     z_got = got[:-1] + [swap(z_last, "yz", 2 * (chips - 1))]
     wire = part.astype(BF16)
     got = swaps_gx([wire] * (gx - 1))
-    old = ready_state(place, ssm_state, alive, wire)
-    got, z_got, old = lax.optimization_barrier((got, z_got, old))
+    got, z_got = lax.optimization_barrier((got, z_got))
     part = total_of(part, got).astype(BF16)
     ssm_new, gated = scan(
         place, part, swap(part, "yz", 1), dt_rows, params, old, xa, zown, z_got, scale, taps
@@ -693,14 +701,16 @@
     gated, attention_projection = lax.optimization_barrier((gated, attention_projection))
     flattened = attention_projection.reshape(width, group_count * group_cols)
     weights = stage_rows(place, mixer_output, yz, gated, True, chips, "stage_mix")
-    pieces, (flattened, weights) = gather_yz(gated, flattened, weights)
+    got = swaps_chip([gated] * (chips - 1), (0, 1, 2), (0, 0, 0))
+    *got[1:], weights, flattened = lax.optimization_barrier((*got[1:], weights, flattened))
+    pieces = gather_yz(gated, got)
     own_rows, wires = mix_out(place, pieces, weights, gx, chips)
     first_out = (hidden_in.astype(F32) + total_of(own_rows, swaps_gx(wires))).astype(BF16)
 
     pieces = [first_out] + swaps_gx([first_out] * (gx - 1))
     give, keep = query(place, pieces, assign[None, :], norm_gain_b[None, :], flattened, chips)
     entries, wires = add_pairs(keep, swap(give, "yz", 1), chips, place, "add_query")
-    entries = total_of(entries, swaps_chip(wires))
+    entries = total_of(entries, swaps_chip(wires, (2, 1, 0), (2, 0, 1)))
     scale = lax.rsqrt(entries[:, -1:] / whole_width + 1e-05)
     newest_entry = (entries[:, :-128] * scale).astype(BF16)
     newest_entry = newest_entry.reshape(slot_count, group_count, group_cols)
@@ -735,7 +745,9 @@
     )
     heads = attended.astype(BF16).reshape(slot_count, group_count * per_group * head_dim)
     head_weights = stage_rows(place, head_output, 4, heads, False, chips, "stage_head")
-    pieces, (head_weights,) = gather_yz(heads, head_weights)
+    got = swaps_chip([heads] * (chips - 1), (0, 1, 2), (0, 0, 0))
+    got[-1], head_weights = lax.optimization_barrier((got[-1], head_weights))
+    pieces = gather_yz(heads, got)
     own_rows, wires = head_out(place, pieces, assign[None, :], head_weights, gx, chips)
     hidden_out = (first_out.astype(F32) + total_of(own_rows, swaps_gx(wires))).astype(BF16)
     return (hidden_out, ssm_new, jnp.transpose(conv_new, (1, 0, 2)), fresh_kv)

time: 135 us -> 130 us (0.963)
  waiting for transfers between devices: 41.3 us -> 38.3 us
  starting transfers between devices: 48.2 us -> 46.8 us
    ppermute x44, waiting for transfers between devices: 41.3 us -> 38.3 us  [swap(): return lax.ppermute(value, axis, [(i, i ^ bits) for i in range(size)])]
    ppermute x44, starting transfers between devices: 48.2 us -> 46.8 us  [swap(): return lax.ppermute(value, axis, [(i, i ^ bits) for i in range(size)])]
  transfers between devices with their start and end apart: 44 -> 44, of which waited for: 28 -> 29; matrix products, arithmetic and copies ran while one was open for 3% -> 3% of each run, Pallas kernels for 17% -> 17%
where the time goes in v3:
time: 130 us
  starting transfers between devices  46.8 us (36%)
  waiting for transfers between devices  38.3 us (29%)
  Pallas kernels  36.7 us (28%)
  local copies, waits for them, and re-layouts  4.42 us (3%)
  other arithmetic  1.6 us (1%)
    ppermute x44, starting transfers between devices, swap(): return lax.ppermute(value, axis, [(i, i ^ bits) for i in range(size)])  46.8 us
    ppermute x44, waiting for transfers between devices, swap(): return lax.ppermute(value, axis, [(i, i ^ bits) for i in range(size)])  38.3 us
    pallas_call x14, Pallas kernels, call(): pl.pallas_call(kernel, grid_spec=pltpu.PrefetchScalarGridSpec(num_scalar_...  32.2 us
    pallas_call x1, Pallas kernels, scan(): pl.pallas_call(kernel, grid_spec=pltpu.PrefetchScalarGridSpec(num_scalar_...  4.54 us
  transfers between devices with their start and end apart: 44, of which 29 were waited for; matrix products, arithmetic and copies ran while one was open for 3% of the time, Pallas kernels for 17%

profile of v3, /device:TPU:0, one launch (start us, length us, event | category | flops | bytes accessed | tf_op | source)
XLA Modules:
  0.0 129.9 jit_solution(16839555178374188750)
XLA Ops:
  0.6 4.0 %collective-permute-start.2 = (bf16[32,1024]{1,0:T(8,128)(2,1)}, bf16[32,1024]{1,0:T(8,128)(2,1)S(1)}, u32[]{:S(2)}, u32[]{:S(2)}) collective-permute-start(bf16[32,1024]{1,0:T(8,128)(2,1)} %hidden_ref.1), channel_id=1, source_target_pairs={{0,24},{8,16},{16,8},{24,0},{1,25},{9,17},{17,9},{25,1},{2,26},{10... | collective-permute-start | bytes 196616 | tf_op jit(solution)/shard_map/ppermute | solution.py:17
  5.3 4.0 %stage_first.1 = (bf16[8,512,1024]{2,1,0:T(8,128)(2,1)S(1)}, bf16[32,1024]{1,0:T(8,128)(2,1)S(1)}, f32[1,1024]{1,0:T(1,128)S(1)}) custom-call(s32[11]{0:T(128)S(1)} %concatenate.6.place_ref, bf16[2,4096,1024]{2,1,0:T(8,128)(2,1)} %w_ref.5, bf16[32,1024]{1,0:T(8,128)(2,1)} %hidden_ref.1, f32[1,1024]{1,0:T(1,128)} %bitcast.57), custom_call_target="tpu_custom_call" | custom-call | bytes 8388608 | tf_op jit(solution)/shard_map/stage_first/pallas_call | solution.py:68
  9.6 2.0 %project_first.1 = (bf16[4,528,128]{2,1,0:T(8,128)(2,1)S(1)}, bf16[1024,128]{1,0:T(8,128)(2,1)S(1)}, f32[16,128]{1,0:T(8,128)S(1)}) custom-call(s32[11]{0:T(128)S(1)} %concatenate.6.place_ref, bf16[32,1024]{1,0:T(8,128)(2,1)S(1)} %get-tuple-element.84.refs_0_, bf16[32,1024]{1,0:T(8,128)(2,1)S(1)} %collective-permute-done.refs_1_, ...), custom_call_target="tpu_custom_call" | custom-call | tf_op jit(solution)/shard_map/project_first/pallas_call | solution.py:68
  11.7 1.8 %project_keep.1 = bf16[4,528,128]{2,1,0:T(8,128)(2,1)S(1)} custom-call(s32[11]{0:T(128)S(1)} %concatenate.6.place_ref, bf16[8,512,1024]{2,1,0:T(8,128)(2,1)S(1)} %get-tuple-element.83.refs_5_.w_ref, bf16[1024,128]{1,0:T(8,128)(2,1)S(1)} %get-tuple-element.89.gained_ref, f32[16,128]{1,0:T(8,128)S(1)} %get-tuple-element.90.squares_ref), custom_call_target="tpu_custom_call" | custom-call | tf_op jit(solution)/shard_map/project_keep/pallas_call | solution.py:68
  14.2 2.8 %collective-permute-start.5 = (bf16[528,128]{1,0:T(8,128)(2,1)S(1)}, bf16[528,128]{1,0:T(8,128)(2,1)S(1)}, u32[]{:S(2)}, u32[]{:S(2)}) collective-permute-start(bf16[528,128]{1,0:T(8,128)(2,1)S(1)} %get-tuple-element.94), channel_id=1, source_target_pairs={{0,4},{1,5},{2,6},{3,7},{4,0},{5,1},{6,2},{7,3},{8,12},{9,13},{10,... | collective-permute-start | bytes 405512 | tf_op jit(solution)/shard_map/ppermute | solution.py:17
  19.6 5.3 %project_gate.1 = (bf16[4,512,128]{2,1,0:T(8,128)(2,1)S(1)}, bf16[4,512,128]{2,1,0:T(8,128)(2,1)S(1)}, bf16[3,512,128]{2,1,0:T(8,128)(2,1)S(1)}, bf16[544,512]{1,0:T(8,128)(2,1)S(1)}) custom-call(s32[11]{0:T(128)S(1)} %concatenate.6.place_ref, bf16[2,4096,1024]{2,1,0:T(8,128)(2,1)} %w_ref.5, bf16[1024,128]{1,0:T(8,128)(2,1)S(1)} %get-tuple-element.89.gained_ref, ...), custom_call_target="tpu_custom_call" | custom-call | bytes 8388608 | tf_op jit(solution)/shard_map/project_gate/pallas_call | solution.py:68
  24.9 3.5 %collective-permute-done.4.refs_0_ = bf16[528,128]{1,0:T(8,128)(2,1)S(1)} collective-permute-done((bf16[528,128]{1,0:T(8,128)(2,1)S(1)}, bf16[528,128]{1,0:T(8,128)(2,1)S(1)}, u32[]{:S(2)}, u32[]{:S(2)}) %collective-permute-start.4) | collective-permute-done | bytes 135200 | tf_op jit(solution)/shard_map/ppermute | solution.py:17
  32.0 4.2 %collective-permute-start.10 = (bf16[784,128]{1,0:T(8,128)(2,1)S(1)}, bf16[784,128]{1,0:T(8,128)(2,1)S(1)}, u32[]{:S(2)}, u32[]{:S(2)}) collective-permute-start(bf16[784,128]{1,0:T(8,128)(2,1)S(1)} %get-tuple-element.117), channel_id=1, source_target_pairs={{0,4},{1,5},{2,6},{3,7},{4,0},{5,1},{6,2},{7,3},{8,12},{9,13},{10,... | collective-permute-start | bytes 602120 | tf_op jit(solution)/shard_map/ppermute | solution.py:17
  36.2 1.5 %collective-permute-start.11 = (bf16[272,128]{1,0:T(8,128)(2,1)S(1)}, bf16[272,128]{1,0:T(8,128)(2,1)S(1)}, u32[]{:S(2)}, u32[]{:S(2)}) collective-permute-start(bf16[272,128]{1,0:T(8,128)(2,1)S(1)} %get-tuple-element.118), channel_id=1, source_target_pairs={{0,6},{1,7},{2,4},{3,5},{4,2},{5,3},{6,0},{7,1},{8,14},{9,15},{10,... | collective-permute-start | bytes 208904 | tf_op jit(solution)/shard_map/ppermute | solution.py:17
  37.7 3.5 %ready_state.1.state_ref = f32[16,512,128]{2,1,0:T(8,128)S(1)} custom-call(s32[11]{0:T(128)S(1)} %concatenate.6.place_ref, bf16[512,16,128]{2,1,0:T(8,128)(2,1)} %state_ref.1, f32[8,128]{1,0:T(8,128)S(1)} %broadcast_in_dim.66.refs_5_.alive_ref, f32[272,128]{1,0:T(8,128)S(1)} %get-tuple-element.115.earlier_ref), custom_call_target="tpu_custom_call" | custom-call | bytes 6291456 | tf_op jit(solution)/shard_map/ready_state/pallas_call | solution.py:68
  41.2 6.7 %collective-permute-done.11 = bf16[272,128]{1,0:T(8,128)(2,1)S(1)} collective-permute-done((bf16[272,128]{1,0:T(8,128)(2,1)S(1)}, bf16[272,128]{1,0:T(8,128)(2,1)S(1)}, u32[]{:S(2)}, u32[]{:S(2)}) %collective-permute-start.11) | collective-permute-done | bytes 69664 | tf_op jit(solution)/shard_map/ppermute | solution.py:17
  48.7 2.4 %collective-permute-start.15 = (bf16[512,128]{1,0:T(8,128)(2,1)S(1)}, bf16[512,128]{1,0:T(8,128)(2,1)S(1)}, u32[]{:S(2)}, u32[]{:S(2)}) collective-permute-start(bf16[512,128]{1,0:T(8,128)(2,1)S(1)} %get-tuple-element.123), channel_id=1, source_target_pairs={{0,6},{1,7},{2,4},{3,5},{4,2},{5,3},{6,0},{7,1},{8,14},{9,15},{10,... | collective-permute-start | bytes 393224 | tf_op jit(solution)/shard_map/ppermute | solution.py:17
  51.1 2.5 %collective-permute-start.14 = (bf16[272,128]{1,0:T(8,128)(2,1)S(1)}, bf16[272,128]{1,0:T(8,128)(2,1)S(1)}, u32[]{:S(2)}, u32[]{:S(2)}) collective-permute-start(bf16[272,128]{1,0:T(8,128)(2,1)S(1)} %fusion.20), channel_id=1, source_target_pairs={{0,24},{8,16},{16,8},{24,0},{1,25},{9,17},{17,9},{25,1},{2,26},{10... | collective-permute-start | bytes 208904 | tf_op jit(solution)/shard_map/ppermute | solution.py:17
  54.7 2.0 %collective-permute-done.14 = bf16[272,128]{1,0:T(8,128)(2,1)S(1)} collective-permute-done((bf16[272,128]{1,0:T(8,128)(2,1)S(1)}, bf16[272,128]{1,0:T(8,128)(2,1)S(1)}, u32[]{:S(2)}, u32[]{:S(2)}) %collective-permute-start.14) | collective-permute-done | bytes 69664 | tf_op jit(solution)/shard_map/ppermute | solution.py:17
  59.9 4.5 %scan.1 = (bf16[512,16,128]{2,1,0:T(8,128)(2,1)}, bf16[128,512]{1,0:T(8,128)(2,1)S(1)}) custom-call(s32[11]{0:T(128)S(1)} %concatenate.6.place_ref, bf16[272,128]{1,0:T(8,128)(2,1)S(1)} %add_convert_fusion.mine_ref, bf16[272,128]{1,0:T(8,128)(2,1)S(1)} %collective-permute-done.16.other_ref, bf16[512,512]{1,0:T(8,128)(2,1)S(1)} %bitcast.36, ...), custom_call_target="tpu_custom_call" | custom-call | tf_op jit(solution)/shard_map/scan/pallas_call | solution.py:448
  66.0 2.0 %collective-permute-start.18 = (bf16[128,512]{1,0:T(8,128)(2,1)S(1)}, bf16[128,512]{1,0:T(8,128)(2,1)S(1)}, u32[]{:S(2)}, u32[]{:S(2)}) collective-permute-start(bf16[128,512]{1,0:T(8,128)(2,1)S(1)} %get-tuple-element.136.earlier_ref.refs_0_), channel_id=1, source_target_pairs={{0,2},{1,3},{2,0},{3,1},{4,6},{5,7},{6,4},{7,5},{8,10},{9,11},{10,... | collective-permute-start | bytes 393224 | tf_op jit(solution)/shard_map/ppermute | solution.py:17
  68.0 4.0 %stage_mix.1.refs_8_ = bf16[8,512,1024]{2,1,0:T(8,128)(2,1)S(1)} custom-call(s32[11]{0:T(128)S(1)} %concatenate.6.place_ref, bf16[4096,1024]{1,0:T(8,128)(2,1)} %w_ref.6, bf16[128,512]{1,0:T(8,128)(2,1)S(1)} %get-tuple-element.136.earlier_ref.refs_0_), custom_call_target="tpu_custom_call" | custom-call | bytes 8388608 | tf_op jit(solution)/shard_map/stage_mix/pallas_call | solution.py:68
  73.1 2.4 %collective-permute-done.20.refs_4_ = bf16[128,512]{1,0:T(8,128)(2,1)S(1)} collective-permute-done((bf16[128,512]{1,0:T(8,128)(2,1)S(1)}, bf16[128,512]{1,0:T(8,128)(2,1)S(1)}, u32[]{:S(2)}, u32[]{:S(2)}) %collective-permute-start.20) | collective-permute-done | bytes 131104 | tf_op jit(solution)/shard_map/ppermute | solution.py:17
  78.2 1.8 %mix_out.1 = (f32[32,1024]{1,0:T(8,128)S(1)}, bf16[32,1024]{1,0:T(8,128)(2,1)S(1)}, bf16[32,1024]{1,0:T(8,128)(2,1)S(1)}, bf16[32,1024]{1,0:T(8,128)(2,1)S(1)}) custom-call(s32[11]{0:T(128)S(1)} %concatenate.6.place_ref, bf16[128,512]{1,0:T(8,128)(2,1)S(1)} %get-tuple-element.136.earlier_ref.refs_0_, bf16[128,512]{1,0:T(8,128)(2,1)S(1)} %collective-permute-done.17.refs_1_, ...), custom_call_target="tpu_custom_call" | custom-call | tf_op jit(solution)/shard_map/mix_out/pallas_call | solution.py:68
  80.1 2.2 %collective-permute-start.26 = (bf16[32,1024]{1,0:T(8,128)(2,1)S(1)}, bf16[32,1024]{1,0:T(8,128)(2,1)S(1)}, u32[]{:S(2)}, u32[]{:S(2)}) collective-permute-start(bf16[32,1024]{1,0:T(8,128)(2,1)S(1)} %get-tuple-element.144), channel_id=1, source_target_pairs={{0,24},{8,16},{16,8},{24,0},{1,25},{9,17},{17,9},{25,1},{2,26},{10... | collective-permute-start | bytes 196616 | tf_op jit(solution)/shard_map/ppermute | solution.py:17
  83.7 2.1 %collective-permute-done.26 = bf16[32,1024]{1,0:T(8,128)(2,1)S(1)} collective-permute-done((bf16[32,1024]{1,0:T(8,128)(2,1)S(1)}, bf16[32,1024]{1,0:T(8,128)(2,1)S(1)}, u32[]{:S(2)}, u32[]{:S(2)}) %collective-permute-start.26) | collective-permute-done | bytes 65568 | tf_op jit(solution)/shard_map/ppermute | solution.py:17
  87.2 1.8 %collective-permute-start.29 = (bf16[32,1024]{1,0:T(8,128)(2,1)S(1)}, bf16[32,1024]{1,0:T(8,128)(2,1)S(1)}, u32[]{:S(2)}, u32[]{:S(2)}) collective-permute-start(bf16[32,1024]{1,0:T(8,128)(2,1)S(1)} %add_convert_fusion.2.refs_0_), channel_id=1, source_target_pairs={{0,24},{8,16},{16,8},{24,0},{1,25},{9,17},{17,9},{25,1},{2,26},{10... | collective-permute-start | bytes 196616 | tf_op jit(solution)/shard_map/ppermute | solution.py:17
  90.7 1.9 %collective-permute-done.29.refs_3_ = bf16[32,1024]{1,0:T(8,128)(2,1)S(1)} collective-permute-done((bf16[32,1024]{1,0:T(8,128)(2,1)S(1)}, bf16[32,1024]{1,0:T(8,128)(2,1)S(1)}, u32[]{:S(2)}, u32[]{:S(2)}) %collective-permute-start.29) | collective-permute-done | bytes 65568 | tf_op jit(solution)/shard_map/ppermute | solution.py:17
  93.8 1.9 %query.1 = (bf16[64,2688]{1,0:T(8,128)(2,1)S(1)}, bf16[64,2688]{1,0:T(8,128)(2,1)S(1)}) custom-call(s32[11]{0:T(128)S(1)} %concatenate.6.place_ref, bf16[32,1024]{1,0:T(8,128)(2,1)S(1)} %add_convert_fusion.2.refs_0_, bf16[32,1024]{1,0:T(8,128)(2,1)S(1)} %collective-permute-done.27.refs_1_, bf16[32,1024]{1,0:T(8,128)(2,1)S(1)} %collective-permute-done.28.refs_2_, ...), custom_call_target="tpu_custom_call" | custom-call | tf_op jit(solution)/shard_map/query/pallas_call | solution.py:68
  98.0 3.4 %collective-permute-start.32 = (bf16[16,2688]{1,0:T(8,128)(2,1)S(1)}, bf16[16,2688]{1,0:T(8,128)(2,1)S(1)}, u32[]{:S(2)}, u32[]{:S(2)}) collective-permute-start(bf16[16,2688]{1,0:T(8,128)(2,1)S(1)} %get-tuple-element.150), channel_id=1, source_target_pairs={{0,4},{1,5},{2,6},{3,7},{4,0},{5,1},{6,2},{7,3},{8,12},{9,13},{10,... | collective-permute-start | bytes 258056 | tf_op jit(solution)/shard_map/ppermute | solution.py:17
  103.1 3.2 %collective-permute-done.31 = bf16[16,2688]{1,0:T(8,128)(2,1)S(1)} collective-permute-done((bf16[16,2688]{1,0:T(8,128)(2,1)S(1)}, bf16[16,2688]{1,0:T(8,128)(2,1)S(1)}, u32[]{:S(2)}, u32[]{:S(2)}) %collective-permute-start.31) | collective-permute-done | bytes 86048 | tf_op jit(solution)/shard_map/ppermute | solution.py:17
  106.3 3.0 %collective-permute-done.33 = bf16[16,2688]{1,0:T(8,128)(2,1)S(1)} collective-permute-done((bf16[16,2688]{1,0:T(8,128)(2,1)S(1)}, bf16[16,2688]{1,0:T(8,128)(2,1)S(1)}, u32[]{:S(2)}, u32[]{:S(2)}) %collective-permute-start.33) | collective-permute-done | bytes 86048 | tf_op jit(solution)/shard_map/ppermute | solution.py:17
  111.0 2.3 %collective-permute-start.39 = (bf16[16,2048]{1,0:T(8,128)(2,1)S(1)}, bf16[16,2048]{1,0:T(8,128)(2,1)S(1)}, u32[]{:S(2)}, u32[]{:S(2)}) collective-permute-start(bf16[16,2048]{1,0:T(8,128)(2,1)S(1)} %bitcast.37), channel_id=1, source_target_pairs={{0,6},{1,7},{2,4},{3,5},{4,2},{5,3},{6,0},{7,1},{8,14},{9,15},{10,... | collective-permute-start | bytes 196616 | tf_op jit(solution)/shard_map/ppermute | solution.py:17
  113.4 2.1 %collective-permute-start.37 = (bf16[16,2048]{1,0:T(8,128)(2,1)S(1)}, bf16[16,2048]{1,0:T(8,128)(2,1)S(1)}, u32[]{:S(2)}, u32[]{:S(2)}) collective-permute-start(bf16[16,2048]{1,0:T(8,128)(2,1)S(1)} %bitcast.39), channel_id=1, source_target_pairs={{0,4},{1,5},{2,6},{3,7},{4,0},{5,1},{6,2},{7,3},{8,12},{9,13},{10,... | collective-permute-start | bytes 196616 | tf_op jit(solution)/shard_map/ppermute | solution.py:17
  115.5 2.7 %stage_head.1.refs_9_ = bf16[4,512,1024]{2,1,0:T(8,128)(2,1)S(1)} custom-call(s32[11]{0:T(128)S(1)} %concatenate.6.place_ref, bf16[2048,1024]{1,0:T(8,128)(2,1)} %w_ref.7, bf16[16,2048]{1,0:T(8,128)(2,1)S(1)} %bitcast.41), custom_call_target="tpu_custom_call" | custom-call | bytes 4194304 | tf_op jit(solution)/shard_map/stage_head/pallas_call | solution.py:68
  120.3 1.9 %head_out.1 = (f32[32,1024]{1,0:T(8,128)S(1)}, bf16[32,1024]{1,0:T(8,128)(2,1)S(1)}, bf16[32,1024]{1,0:T(8,128)(2,1)S(1)}, bf16[32,1024]{1,0:T(8,128)(2,1)S(1)}) custom-call(s32[11]{0:T(128)S(1)} %concatenate.6.place_ref, bf16[16,2048]{1,0:T(8,128)(2,1)S(1)} %bitcast.42, bf16[16,2048]{1,0:T(8,128)(2,1)S(1)} %collective-permute-done.34.refs_1_, ...), custom_call_target="tpu_custom_call" | custom-call | tf_op jit(solution)/shard_map/head_out/pallas_call | solution.py:68
  122.2 2.3 %collective-permute-start.43 = (bf16[32,1024]{1,0:T(8,128)(2,1)S(1)}, bf16[32,1024]{1,0:T(8,128)(2,1)S(1)}, u32[]{:S(2)}, u32[]{:S(2)}) collective-permute-start(bf16[32,1024]{1,0:T(8,128)(2,1)S(1)} %get-tuple-element.157), channel_id=1, source_target_pairs={{0,24},{8,16},{16,8},{24,0},{1,25},{9,17},{17,9},{25,1},{2,26},{10... | collective-permute-start | bytes 196616 | tf_op jit(solution)/shard_map/ppermute | solution.py:17
  (132 shorter events, 36.9 us)
Async XLA Ops:
  0.6 9.0 %collective-permute-start.2 = (bf16[32,1024]{1,0:T(8,128)(2,1)}, bf16[32,1024]{1,0:T(8,128)(2,1)S(1)}, u32[]{:S(2)}, u32[]{:S(2)}) collective-permute-start(bf16[32,1024]{1,0:T(8,128)(2,1)} %hidden_ref.1), channel_id=1, source_target_pairs={{0,24},{8,16},{16,8},{24,0},{1,25},{9,17},{17,9},{25,1},{2,26},{10... | collective-permute-start | bytes 196616 | tf_op jit(solution)/shard_map/ppermute | solution.py:17
  4.6 5.0 %collective-permute-start = (bf16[32,1024]{1,0:T(8,128)(2,1)}, bf16[32,1024]{1,0:T(8,128)(2,1)S(1)}, u32[]{:S(2)}, u32[]{:S(2)}) collective-permute-start(bf16[32,1024]{1,0:T(8,128)(2,1)} %hidden_ref.1), channel_id=1, source_target_pairs={{0,8},{8,0},{16,24},{24,16},{1,9},{9,1},{17,25},{25,17},{2,10},{10... | collective-permute-start | bytes 196616 | tf_op jit(solution)/shard_map/ppermute | solution.py:17
  5.1 4.5 %collective-permute-start.1 = (bf16[32,1024]{1,0:T(8,128)(2,1)}, bf16[32,1024]{1,0:T(8,128)(2,1)S(1)}, u32[]{:S(2)}, u32[]{:S(2)}) collective-permute-start(bf16[32,1024]{1,0:T(8,128)(2,1)} %hidden_ref.1), channel_id=1, source_target_pairs={{0,16},{8,24},{16,0},{24,8},{1,17},{9,25},{17,1},{25,9},{2,18},{10... | collective-permute-start | bytes 196616 | tf_op jit(solution)/shard_map/ppermute | solution.py:17
  14.2 14.2 %collective-permute-start.5 = (bf16[528,128]{1,0:T(8,128)(2,1)S(1)}, bf16[528,128]{1,0:T(8,128)(2,1)S(1)}, u32[]{:S(2)}, u32[]{:S(2)}) collective-permute-start(bf16[528,128]{1,0:T(8,128)(2,1)S(1)} %get-tuple-element.94), channel_id=1, source_target_pairs={{0,4},{1,5},{2,6},{3,7},{4,0},{5,1},{6,2},{7,3},{8,12},{9,13},{10,... | collective-permute-start | bytes 405512 | tf_op jit(solution)/shard_map/ppermute | solution.py:17
  17.1 11.3 %collective-permute-start.6 = (bf16[528,128]{1,0:T(8,128)(2,1)S(1)}, bf16[528,128]{1,0:T(8,128)(2,1)S(1)}, u32[]{:S(2)}, u32[]{:S(2)}) collective-permute-start(bf16[528,128]{1,0:T(8,128)(2,1)S(1)} %get-tuple-element.95), channel_id=1, source_target_pairs={{0,6},{1,7},{2,4},{3,5},{4,2},{5,3},{6,0},{7,1},{8,14},{9,15},{10,... | collective-permute-start | bytes 405512 | tf_op jit(solution)/shard_map/ppermute | solution.py:17
  18.4 10.0 %collective-permute-start.4 = (bf16[528,128]{1,0:T(8,128)(2,1)S(1)}, bf16[528,128]{1,0:T(8,128)(2,1)S(1)}, u32[]{:S(2)}, u32[]{:S(2)}) collective-permute-start(bf16[528,128]{1,0:T(8,128)(2,1)S(1)} %get-tuple-element.93.earlier_ref), channel_id=1, source_target_pairs={{0,2},{1,3},{2,0},{3,1},{4,6},{5,7},{6,4},{7,5},{8,10},{9,11},{10,... | collective-permute-start | bytes 405512 | tf_op jit(solution)/shard_map/ppermute | solution.py:17
  32.0 15.9 %collective-permute-start.10 = (bf16[784,128]{1,0:T(8,128)(2,1)S(1)}, bf16[784,128]{1,0:T(8,128)(2,1)S(1)}, u32[]{:S(2)}, u32[]{:S(2)}) collective-permute-start(bf16[784,128]{1,0:T(8,128)(2,1)S(1)} %get-tuple-element.117), channel_id=1, source_target_pairs={{0,4},{1,5},{2,6},{3,7},{4,0},{5,1},{6,2},{7,3},{8,12},{9,13},{10,... | collective-permute-start | bytes 602120 | tf_op jit(solution)/shard_map/ppermute | solution.py:17
  36.2 12.5 %collective-permute-start.9 = (bf16[784,128]{1,0:T(8,128)(2,1)S(1)}, bf16[784,128]{1,0:T(8,128)(2,1)S(1)}, u32[]{:S(2)}, u32[]{:S(2)}) collective-permute-start(bf16[784,128]{1,0:T(8,128)(2,1)S(1)} %get-tuple-element.116), channel_id=1, source_target_pairs={{0,2},{1,3},{2,0},{3,1},{4,6},{5,7},{6,4},{7,5},{8,10},{9,11},{10,... | collective-permute-start | bytes 602120 | tf_op jit(solution)/shard_map/ppermute | solution.py:17
  36.2 11.7 %collective-permute-start.11 = (bf16[272,128]{1,0:T(8,128)(2,1)S(1)}, bf16[272,128]{1,0:T(8,128)(2,1)S(1)}, u32[]{:S(2)}, u32[]{:S(2)}) collective-permute-start(bf16[272,128]{1,0:T(8,128)(2,1)S(1)} %get-tuple-element.118), channel_id=1, source_target_pairs={{0,6},{1,7},{2,4},{3,5},{4,2},{5,3},{6,0},{7,1},{8,14},{9,15},{10,... | collective-permute-start | bytes 208904 | tf_op jit(solution)/shard_map/ppermute | solution.py:17
  48.7 9.8 %collective-permute-start.15 = (bf16[512,128]{1,0:T(8,128)(2,1)S(1)}, bf16[512,128]{1,0:T(8,128)(2,1)S(1)}, u32[]{:S(2)}, u32[]{:S(2)}) collective-permute-start(bf16[512,128]{1,0:T(8,128)(2,1)S(1)} %get-tuple-element.123), channel_id=1, source_target_pairs={{0,6},{1,7},{2,4},{3,5},{4,2},{5,3},{6,0},{7,1},{8,14},{9,15},{10,... | collective-permute-start | bytes 393224 | tf_op jit(solution)/shard_map/ppermute | solution.py:17
  51.1 5.6 %collective-permute-start.14 = (bf16[272,128]{1,0:T(8,128)(2,1)S(1)}, bf16[272,128]{1,0:T(8,128)(2,1)S(1)}, u32[]{:S(2)}, u32[]{:S(2)}) collective-permute-start(bf16[272,128]{1,0:T(8,128)(2,1)S(1)} %fusion.20), channel_id=1, source_target_pairs={{0,24},{8,16},{16,8},{24,0},{1,25},{9,17},{17,9},{25,1},{2,26},{10... | collective-permute-start | bytes 208904 | tf_op jit(solution)/shard_map/ppermute | solution.py:17
  53.6 4.3 %collective-permute-start.12 = (bf16[272,128]{1,0:T(8,128)(2,1)S(1)}, bf16[272,128]{1,0:T(8,128)(2,1)S(1)}, u32[]{:S(2)}, u32[]{:S(2)}) collective-permute-start(bf16[272,128]{1,0:T(8,128)(2,1)S(1)} %fusion.20), channel_id=1, source_target_pairs={{0,8},{8,0},{16,24},{24,16},{1,9},{9,1},{17,25},{25,17},{2,10},{10... | collective-permute-start | bytes 208904 | tf_op jit(solution)/shard_map/ppermute | solution.py:17
  54.2 4.3 %collective-permute-start.13 = (bf16[272,128]{1,0:T(8,128)(2,1)S(1)}, bf16[272,128]{1,0:T(8,128)(2,1)S(1)}, u32[]{:S(2)}, u32[]{:S(2)}) collective-permute-start(bf16[272,128]{1,0:T(8,128)(2,1)S(1)} %fusion.20), channel_id=1, source_target_pairs={{0,16},{8,24},{16,0},{24,8},{1,17},{9,25},{17,1},{25,9},{2,18},{10... | collective-permute-start | bytes 208904 | tf_op jit(solution)/shard_map/ppermute | solution.py:17
  64.4 11.0 %collective-permute-start.20 = (bf16[128,512]{1,0:T(8,128)(2,1)S(1)}, bf16[128,512]{1,0:T(8,128)(2,1)S(1)}, u32[]{:S(2)}, u32[]{:S(2)}) collective-permute-start(bf16[128,512]{1,0:T(8,128)(2,1)S(1)} %get-tuple-element.136.earlier_ref.refs_0_), channel_id=1, source_target_pairs={{0,4},{1,5},{2,6},{3,7},{4,0},{5,1},{6,2},{7,3},{8,12},{9,13},{10,... | collective-permute-start | bytes 393224 | tf_op jit(solution)/shard_map/ppermute | solution.py:17
  64.5 11.0 %collective-permute-start.21 = (bf16[128,512]{1,0:T(8,128)(2,1)S(1)}, bf16[128,512]{1,0:T(8,128)(2,1)S(1)}, u32[]{:S(2)}, u32[]{:S(2)}) collective-permute-start(bf16[128,512]{1,0:T(8,128)(2,1)S(1)} %get-tuple-element.136.earlier_ref.refs_0_), channel_id=1, source_target_pairs={{0,6},{1,7},{2,4},{3,5},{4,2},{5,3},{6,0},{7,1},{8,14},{9,15},{10,... | collective-permute-start | bytes 393224 | tf_op jit(solution)/shard_map/ppermute | solution.py:17
  66.0 10.8 %collective-permute-start.18 = (bf16[128,512]{1,0:T(8,128)(2,1)S(1)}, bf16[128,512]{1,0:T(8,128)(2,1)S(1)}, u32[]{:S(2)}, u32[]{:S(2)}) collective-permute-start(bf16[128,512]{1,0:T(8,128)(2,1)S(1)} %get-tuple-element.136.earlier_ref.refs_0_), channel_id=1, source_target_pairs={{0,2},{1,3},{2,0},{3,1},{4,6},{5,7},{6,4},{7,5},{8,10},{9,11},{10,... | collective-permute-start | bytes 393224 | tf_op jit(solution)/shard_map/ppermute | solution.py:17
  68.0 8.9 %collective-permute-start.17 = (bf16[128,512]{1,0:T(8,128)(2,1)S(1)}, bf16[128,512]{1,0:T(8,128)(2,1)S(1)}, u32[]{:S(2)}, u32[]{:S(2)}) collective-permute-start(bf16[128,512]{1,0:T(8,128)(2,1)S(1)} %get-tuple-element.136.earlier_ref.refs_0_), channel_id=1, source_target_pairs={{0,1},{1,0},{2,3},{3,2},{4,5},{5,4},{6,7},{7,6},{8,9},{9,8},{10,11... | collective-permute-start | bytes 393224 | tf_op jit(solution)/shard_map/ppermute | solution.py:17
  80.1 5.6 %collective-permute-start.26 = (bf16[32,1024]{1,0:T(8,128)(2,1)S(1)}, bf16[32,1024]{1,0:T(8,128)(2,1)S(1)}, u32[]{:S(2)}, u32[]{:S(2)}) collective-permute-start(bf16[32,1024]{1,0:T(8,128)(2,1)S(1)} %get-tuple-element.144), channel_id=1, source_target_pairs={{0,24},{8,16},{16,8},{24,0},{1,25},{9,17},{17,9},{25,1},{2,26},{10... | collective-permute-start | bytes 196616 | tf_op jit(solution)/shard_map/ppermute | solution.py:17
  82.3 4.3 %collective-permute-start.24 = (bf16[32,1024]{1,0:T(8,128)(2,1)S(1)}, bf16[32,1024]{1,0:T(8,128)(2,1)S(1)}, u32[]{:S(2)}, u32[]{:S(2)}) collective-permute-start(bf16[32,1024]{1,0:T(8,128)(2,1)S(1)} %get-tuple-element.142), channel_id=1, source_target_pairs={{0,8},{8,0},{16,24},{24,16},{1,9},{9,1},{17,25},{25,17},{2,10},{10... | collective-permute-start | bytes 196616 | tf_op jit(solution)/shard_map/ppermute | solution.py:17
  82.8 4.3 %collective-permute-start.25 = (bf16[32,1024]{1,0:T(8,128)(2,1)S(1)}, bf16[32,1024]{1,0:T(8,128)(2,1)S(1)}, u32[]{:S(2)}, u32[]{:S(2)}) collective-permute-start(bf16[32,1024]{1,0:T(8,128)(2,1)S(1)} %get-tuple-element.143), channel_id=1, source_target_pairs={{0,16},{8,24},{16,0},{24,8},{1,17},{9,25},{17,1},{25,9},{2,18},{10... | collective-permute-start | bytes 196616 | tf_op jit(solution)/shard_map/ppermute | solution.py:17
  87.2 5.4 %collective-permute-start.29 = (bf16[32,1024]{1,0:T(8,128)(2,1)S(1)}, bf16[32,1024]{1,0:T(8,128)(2,1)S(1)}, u32[]{:S(2)}, u32[]{:S(2)}) collective-permute-start(bf16[32,1024]{1,0:T(8,128)(2,1)S(1)} %add_convert_fusion.2.refs_0_), channel_id=1, source_target_pairs={{0,24},{8,16},{16,8},{24,0},{1,25},{9,17},{17,9},{25,1},{2,26},{10... | collective-permute-start | bytes 196616 | tf_op jit(solution)/shard_map/ppermute | solution.py:17
  89.0 4.3 %collective-permute-start.27 = (bf16[32,1024]{1,0:T(8,128)(2,1)S(1)}, bf16[32,1024]{1,0:T(8,128)(2,1)S(1)}, u32[]{:S(2)}, u32[]{:S(2)}) collective-permute-start(bf16[32,1024]{1,0:T(8,128)(2,1)S(1)} %add_convert_fusion.2.refs_0_), channel_id=1, source_target_pairs={{0,8},{8,0},{16,24},{24,16},{1,9},{9,1},{17,25},{25,17},{2,10},{10... | collective-permute-start | bytes 196616 | tf_op jit(solution)/shard_map/ppermute | solution.py:17
  89.5 4.3 %collective-permute-start.28 = (bf16[32,1024]{1,0:T(8,128)(2,1)S(1)}, bf16[32,1024]{1,0:T(8,128)(2,1)S(1)}, u32[]{:S(2)}, u32[]{:S(2)}) collective-permute-start(bf16[32,1024]{1,0:T(8,128)(2,1)S(1)} %add_convert_fusion.2.refs_0_), channel_id=1, source_target_pairs={{0,16},{8,24},{16,0},{24,8},{1,17},{9,25},{17,1},{25,9},{2,18},{10... | collective-permute-start | bytes 196616 | tf_op jit(solution)/shard_map/ppermute | solution.py:17
  98.0 11.2 %collective-permute-start.32 = (bf16[16,2688]{1,0:T(8,128)(2,1)S(1)}, bf16[16,2688]{1,0:T(8,128)(2,1)S(1)}, u32[]{:S(2)}, u32[]{:S(2)}) collective-permute-start(bf16[16,2688]{1,0:T(8,128)(2,1)S(1)} %get-tuple-element.150), channel_id=1, source_target_pairs={{0,4},{1,5},{2,6},{3,7},{4,0},{5,1},{6,2},{7,3},{8,12},{9,13},{10,... | collective-permute-start | bytes 258056 | tf_op jit(solution)/shard_map/ppermute | solution.py:17
  101.5 4.9 %collective-permute-start.31 = (bf16[16,2688]{1,0:T(8,128)(2,1)S(1)}, bf16[16,2688]{1,0:T(8,128)(2,1)S(1)}, u32[]{:S(2)}, u32[]{:S(2)}) collective-permute-start(bf16[16,2688]{1,0:T(8,128)(2,1)S(1)} %get-tuple-element.149), channel_id=1, source_target_pairs={{0,2},{1,3},{2,0},{3,1},{4,6},{5,7},{6,4},{7,5},{8,10},{9,11},{10,... | collective-permute-start | bytes 258056 | tf_op jit(solution)/shard_map/ppermute | solution.py:17
  101.5 7.8 %collective-permute-start.33 = (bf16[16,2688]{1,0:T(8,128)(2,1)S(1)}, bf16[16,2688]{1,0:T(8,128)(2,1)S(1)}, u32[]{:S(2)}, u32[]{:S(2)}) collective-permute-start(bf16[16,2688]{1,0:T(8,128)(2,1)S(1)} %get-tuple-element.151), channel_id=1, source_target_pairs={{0,6},{1,7},{2,4},{3,5},{4,2},{5,3},{6,0},{7,1},{8,14},{9,15},{10,... | collective-permute-start | bytes 258056 | tf_op jit(solution)/shard_map/ppermute | solution.py:17
  111.0 7.2 %collective-permute-start.39 = (bf16[16,2048]{1,0:T(8,128)(2,1)S(1)}, bf16[16,2048]{1,0:T(8,128)(2,1)S(1)}, u32[]{:S(2)}, u32[]{:S(2)}) collective-permute-start(bf16[16,2048]{1,0:T(8,128)(2,1)S(1)} %bitcast.37), channel_id=1, source_target_pairs={{0,6},{1,7},{2,4},{3,5},{4,2},{5,3},{6,0},{7,1},{8,14},{9,15},{10,... | collective-permute-start | bytes 196616 | tf_op jit(solution)/shard_map/ppermute | solution.py:17
  113.4 5.5 %collective-permute-start.35 = (bf16[16,2048]{1,0:T(8,128)(2,1)S(1)}, bf16[16,2048]{1,0:T(8,128)(2,1)S(1)}, u32[]{:S(2)}, u32[]{:S(2)}) collective-permute-start(bf16[16,2048]{1,0:T(8,128)(2,1)S(1)} %bitcast.38), channel_id=1, source_target_pairs={{0,2},{1,3},{2,0},{3,1},{4,6},{5,7},{6,4},{7,5},{8,10},{9,11},{10,... | collective-permute-start | bytes 196616 | tf_op jit(solution)/shard_map/ppermute | solution.py:17
  113.4 5.6 %collective-permute-start.37 = (bf16[16,2048]{1,0:T(8,128)(2,1)S(1)}, bf16[16,2048]{1,0:T(8,128)(2,1)S(1)}, u32[]{:S(2)}, u32[]{:S(2)}) collective-permute-start(bf16[16,2048]{1,0:T(8,128)(2,1)S(1)} %bitcast.39), channel_id=1, source_target_pairs={{0,4},{1,5},{2,6},{3,7},{4,0},{5,1},{6,2},{7,3},{8,12},{9,13},{10,... | collective-permute-start | bytes 196616 | tf_op jit(solution)/shard_map/ppermute | solution.py:17
  122.2 5.6 %collective-permute-start.43 = (bf16[32,1024]{1,0:T(8,128)(2,1)S(1)}, bf16[32,1024]{1,0:T(8,128)(2,1)S(1)}, u32[]{:S(2)}, u32[]{:S(2)}) collective-permute-start(bf16[32,1024]{1,0:T(8,128)(2,1)S(1)} %get-tuple-element.157), channel_id=1, source_target_pairs={{0,24},{8,16},{16,8},{24,0},{1,25},{9,17},{17,9},{25,1},{2,26},{10... | collective-permute-start | bytes 196616 | tf_op jit(solution)/shard_map/ppermute | solution.py:17
  124.4 4.3 %collective-permute-start.41 = (bf16[32,1024]{1,0:T(8,128)(2,1)S(1)}, bf16[32,1024]{1,0:T(8,128)(2,1)S(1)}, u32[]{:S(2)}, u32[]{:S(2)}) collective-permute-start(bf16[32,1024]{1,0:T(8,128)(2,1)S(1)} %get-tuple-element.155), channel_id=1, source_target_pairs={{0,8},{8,0},{16,24},{24,16},{1,9},{9,1},{17,25},{25,17},{2,10},{10... | collective-permute-start | bytes 196616 | tf_op jit(solution)/shard_map/ppermute | solution.py:17
  125.0 4.3 %collective-permute-start.42 = (bf16[32,1024]{1,0:T(8,128)(2,1)S(1)}, bf16[32,1024]{1,0:T(8,128)(2,1)S(1)}, u32[]{:S(2)}, u32[]{:S(2)}) collective-permute-start(bf16[32,1024]{1,0:T(8,128)(2,1)S(1)} %get-tuple-element.156), channel_id=1, source_target_pairs={{0,16},{8,24},{16,0},{24,8},{1,17},{9,25},{17,1},{25,9},{2,18},{10... | collective-permute-start | bytes 196616 | tf_op jit(solution)/shard_map/ppermute | solution.py:17
  (26 other events, 182.1 us)

commit v4 on v3

--- a/solution.py
+++ b/solution.py
@@ -177,32 +177,33 @@
 def add_both(place, part, received, keep, z_received, parts):
     half, batch = part.shape
     own = keep.shape[0] // parts
-
-    def kernel(place_ref, part_ref, received_ref, keep_ref, z_ref, sum_ref, zown_ref, *refs):
+    even = parts // 2 * own
+
+    def kernel(place_ref, part_ref, received_ref, keep_ref, z_ref, sum_ref, wire_ref, odd_ref, z_to):
         total = part_ref[...] + received_ref[...].astype(F32)
         sum_ref[...] = total
+        wire_ref[...] = total.astype(BF16)
         for k in range(parts):
             block = pl.ds(k * own, own)
             z = keep_ref[block, :].astype(F32) + z_ref[block, :].astype(F32)
-            if k == 0:
-                zown_ref[...] = z
-                continue
-            refs[k - 1][:half, :] = total.astype(BF16)
-            if k < parts - 1:
-                refs[k - 1][half:, :] = z.astype(BF16)
+            start = k // 2 * own
+            if k % 2:
+                odd_ref[start : start + own, :] = z.astype(BF16)
             else:
-                refs[k][...] = z.astype(BF16)
-
-    total, zown, *wires = call(
+                z_to[start : start + own, :] = z
+
+    return call(
         kernel,
         place,
         [part, received, keep, z_received],
-        [shape((half, batch), F32), shape((own, batch), F32)]
-        + [shape((half + own, batch), BF16)] * (parts - 2)
-        + [shape((half, batch), BF16), shape((own, batch), BF16)],
+        [
+            shape((half, batch), F32),
+            shape((half, batch), BF16),
+            shape((even, batch), BF16),
+            shape((even, batch), F32),
+        ],
         name="add_both",
     )
-    return total, zown, wires[:-1], wires[-1]
 
 
 def project_first(place, pieces, gain, weights, batch, chips):
@@ -393,18 +394,15 @@
     )[0]
 
 
-def scan(place, mine, other, dt_rows, params, state, xa, zown, zgot, scale, taps):
+def scan(place, mine, other, dt_rows, params, state, xa, taps):
     nstate, own, batch = state.shape
     rank = dt_rows.shape[1]
     half = mine.shape[0]
     block = 128
     steps, lanes = own // block, batch // 128
-    count = len(zgot)
 
     def kernel(place_ref, mine_ref, other_ref, dtw_ref, params_ref, state_ref, *refs):
-        xa_ref, zown_ref = refs[:2]
-        zrefs = refs[2 : 2 + count]
-        scale_ref, new_ref, gated_ref, low, behind, packed, sems = refs[2 + count :]
+        xa_ref, new_ref, value_ref, low, behind, packed, sems = refs
         core = place_ref[place_ref.shape[0] - 1]
         first = jnp.broadcast_to(core, mine_ref.shape) == 0
         low[:half] = jnp.where(first, mine_ref[...], other_ref[...])
@@ -434,17 +432,11 @@
             copy = pltpu.make_async_copy(packed.at[i], new_ref.at[pl.ds(i * block, block)], sems.at[i])
             copy.start()
             copies.append(copy)
-            ztotal = zown_ref[here, :]
-            for ref in zrefs:
-                start = ref.shape[0] - own + i * block
-                ztotal = ztotal + ref[start : start + block, :].astype(F32)
-            gate = (ztotal * scale_ref[:1, :]).astype(BF16).astype(F32)
-            value = value * (gate / (1.0 + jnp.exp(-gate)))
-            gated_ref[:, here] = jnp.transpose(value).astype(BF16)
+            value_ref[here, :] = value
         for copy in copies:
             copy.wait()
 
-    pairs = [in_vmem(a) for a in (mine, other, dt_rows, params, state, xa, zown, *zgot, scale)]
+    pairs = [in_vmem(a) for a in (mine, other, dt_rows, params, state, xa)]
     return pl.pallas_call(
         kernel,
         grid_spec=pltpu.PrefetchScalarGridSpec(
@@ -464,11 +456,34 @@
         ),
         out_shape=[
             pltpu.HBM((own, nstate, batch), BF16),
-            pltpu.VMEM((batch, own), BF16),
+            pltpu.VMEM((own, batch), F32),
         ],
         compiler_params=pltpu.CompilerParams(vmem_limit_bytes=18 * MIB),
+        cost_estimate=pl.CostEstimate(flops=0, bytes_accessed=1, transcendentals=0),
         name="scan",
     )(place, *[array for array, _ in pairs])
+
+
+def gate_rows(place, value, zown, zgot, scale):
+    own, batch = value.shape
+    count = len(zgot)
+
+    def kernel(place_ref, value_ref, zown_ref, *refs):
+        scale_ref, gated_ref = refs[count:]
+        total = zown_ref[...]
+        for ref in refs[:count]:
+            total = total + ref[...].astype(F32)
+        gate = (total * scale_ref[:1, :]).astype(BF16).astype(F32)
+        value = value_ref[...] * (gate / (1.0 + jnp.exp(-gate)))
+        gated_ref[...] = jnp.transpose(value).astype(BF16)
+
+    return call(
+        kernel,
+        place,
+        [value, zown, *zgot, scale],
+        [shape((batch, own), BF16)],
+        name="gate_rows",
+    )[0]
 
 
 def mix_out(place, pieces, weights, parts, chips):
@@ -681,22 +696,24 @@
     conv_new, xa, give, part, scale = convolve(
         place, xown, xgot, conv_rows, params, alive, x_cols, own, whole_width
     )
-    part, zown, wires, z_last = add_both(
+    part, wire, z_odd, z_even = add_both(
         place, part, swap(give, "yz", 1), keep.reshape(chips * own, batch), z_received, chips
     )
-    got = swaps_chip(wires)
-    half = part.shape[0]
+    got = swaps_chip([wire] * (chips - 1), (2, 1, 0), (2, 1, 0))
+    z_near = swap(z_odd, "yz", 2)
     old = ready_state(place, ssm_state, alive, part)
-    got, old, z_last = lax.optimization_barrier((got, old, z_last))
-    part = total_of(part, [g[:half] for g in got])
-    z_got = got[:-1] + [swap(z_last, "yz", 2 * (chips - 1))]
+    got, old = lax.optimization_barrier((got, old))
+    part = total_of(part, got)
     wire = part.astype(BF16)
-    got = swaps_gx([wire] * (gx - 1))
-    got, z_got = lax.optimization_barrier((got, z_got))
+    got = swaps_gx([wire] * (gx - 1), (0, 1, 2), (0, 0, 0))
+    z_even = z_even + z_near.astype(F32)
+    z_wires = [z_even[k * own : (k + 1) * own].astype(BF16) for k in range(1, chips // 2)]
+    z_got = [swap(w, "yz", 4 * (k + 1)) for k, w in enumerate(z_wires)]
     part = total_of(part, got).astype(BF16)
-    ssm_new, gated = scan(
-        place, part, swap(part, "yz", 1), dt_rows, params, old, xa, zown, z_got, scale, taps
-    )
+    ssm_new, value = scan(
+        place, part, swap(part, "yz", 1), dt_rows, params, old, xa, taps
+    )
+    gated = gate_rows(place, value, z_even[:own], z_got, scale)
 
     gated, attention_projection = lax.optimization_barrier((gated, attention_projection))
     flattened = attention_projection.reshape(width, group_count * group_cols)

time: 130 us -> 125 us (0.962)
  waiting for transfers between devices: 38.3 us -> 32.2 us
    ppermute x44 -> x45, waiting for transfers between devices: 38.3 us -> 32.2 us  [swap(): return lax.ppermute(value, axis, [(i, i ^ bits) for i in range(size)])]
    pallas_call x14 -> x15, Pallas kernels: 32.2 us -> 32.9 us  [call(): pl.pallas_call(kernel, grid_spec=pltpu.PrefetchScalarGridSpec(num_scalar_...]
    ppermute x44 -> x45, starting transfers between devices: 46.8 us -> 47.5 us  [swap(): return lax.ppermute(value, axis, [(i, i ^ bits) for i in range(size)])]
  transfers between devices with their start and end apart: 44 -> 45, of which waited for: 29 -> 27; matrix products, arithmetic and copies ran while one was open for 3% -> 3% of each run, Pallas kernels for 17% -> 22%
where the time goes in v4:
time: 125 us
  starting transfers between devices  47.5 us (38%)
  Pallas kernels  37.4 us (30%)
  waiting for transfers between devices  32.2 us (26%)
  local copies, waits for them, and re-layouts  4.09 us (3%)
  other arithmetic  1.67 us (1%)
    ppermute x45, starting transfers between devices, swap(): return lax.ppermute(value, axis, [(i, i ^ bits) for i in range(size)])  47.5 us
    pallas_call x15, Pallas kernels, call(): pl.pallas_call(kernel, grid_spec=pltpu.PrefetchScalarGridSpec(num_scalar_...  32.9 us
    ppermute x45, waiting for transfers between devices, swap(): return lax.ppermute(value, axis, [(i, i ^ bits) for i in range(size)])  32.2 us
    pallas_call x1, Pallas kernels, scan(): pl.pallas_call(kernel, grid_spec=pltpu.PrefetchScalarGridSpec(num_scalar_...  4.5 us
  transfers between devices with their start and end apart: 45, of which 27 were waited for; matrix products, arithmetic and copies ran while one was open for 3% of the time, Pallas kernels for 22%

profile of v4, /device:TPU:0, one launch (start us, length us, event | category | flops | bytes accessed | tf_op | source)
XLA Modules:
  0.0 124.9 jit_solution(14391116709867562660)
XLA Ops:
  0.6 4.0 %collective-permute-start.2 = (bf16[32,1024]{1,0:T(8,128)(2,1)}, bf16[32,1024]{1,0:T(8,128)(2,1)S(1)}, u32[]{:S(2)}, u32[]{:S(2)}) collective-permute-start(bf16[32,1024]{1,0:T(8,128)(2,1)} %hidden_ref.1), channel_id=1, source_target_pairs={{0,24},{8,16},{16,8},{24,0},{1,25},{9,17},{17,9},{25,1},{2,26},{10... | collective-permute-start | bytes 196616 | tf_op jit(solution)/shard_map/ppermute | solution.py:17
  5.3 4.0 %stage_first.1 = (bf16[8,512,1024]{2,1,0:T(8,128)(2,1)S(1)}, bf16[32,1024]{1,0:T(8,128)(2,1)S(1)}, f32[1,1024]{1,0:T(1,128)S(1)}) custom-call(s32[11]{0:T(128)S(1)} %concatenate.6.place_ref, bf16[2,4096,1024]{2,1,0:T(8,128)(2,1)} %w_ref.5, bf16[32,1024]{1,0:T(8,128)(2,1)} %hidden_ref.1, f32[1,1024]{1,0:T(1,128)} %bitcast.57), custom_call_target="tpu_custom_call" | custom-call | bytes 8388608 | tf_op jit(solution)/shard_map/stage_first/pallas_call | solution.py:68
  9.6 2.0 %project_first.1 = (bf16[4,528,128]{2,1,0:T(8,128)(2,1)S(1)}, bf16[1024,128]{1,0:T(8,128)(2,1)S(1)}, f32[16,128]{1,0:T(8,128)S(1)}) custom-call(s32[11]{0:T(128)S(1)} %concatenate.6.place_ref, bf16[32,1024]{1,0:T(8,128)(2,1)S(1)} %get-tuple-element.75.refs_0_, bf16[32,1024]{1,0:T(8,128)(2,1)S(1)} %collective-permute-done.refs_1_, ...), custom_call_target="tpu_custom_call" | custom-call | tf_op jit(solution)/shard_map/project_first/pallas_call | solution.py:68
  11.7 1.8 %project_keep.1 = bf16[4,528,128]{2,1,0:T(8,128)(2,1)S(1)} custom-call(s32[11]{0:T(128)S(1)} %concatenate.6.place_ref, bf16[8,512,1024]{2,1,0:T(8,128)(2,1)S(1)} %get-tuple-element.74.refs_5_.w_ref, bf16[1024,128]{1,0:T(8,128)(2,1)S(1)} %get-tuple-element.80.gained_ref, f32[16,128]{1,0:T(8,128)S(1)} %get-tuple-element.81.squares_ref), custom_call_target="tpu_custom_call" | custom-call | tf_op jit(solution)/shard_map/project_keep/pallas_call | solution.py:68
  14.2 2.8 %collective-permute-start.5 = (bf16[528,128]{1,0:T(8,128)(2,1)S(1)}, bf16[528,128]{1,0:T(8,128)(2,1)S(1)}, u32[]{:S(2)}, u32[]{:S(2)}) collective-permute-start(bf16[528,128]{1,0:T(8,128)(2,1)S(1)} %get-tuple-element.85), channel_id=1, source_target_pairs={{0,4},{1,5},{2,6},{3,7},{4,0},{5,1},{6,2},{7,3},{8,12},{9,13},{10,... | collective-permute-start | bytes 405512 | tf_op jit(solution)/shard_map/ppermute | solution.py:17
  19.6 5.3 %project_gate.1 = (bf16[4,512,128]{2,1,0:T(8,128)(2,1)S(1)}, bf16[4,512,128]{2,1,0:T(8,128)(2,1)S(1)}, bf16[3,512,128]{2,1,0:T(8,128)(2,1)S(1)}, bf16[544,512]{1,0:T(8,128)(2,1)S(1)}) custom-call(s32[11]{0:T(128)S(1)} %concatenate.6.place_ref, bf16[2,4096,1024]{2,1,0:T(8,128)(2,1)} %w_ref.5, bf16[1024,128]{1,0:T(8,128)(2,1)S(1)} %get-tuple-element.80.gained_ref, ...), custom_call_target="tpu_custom_call" | custom-call | bytes 8388608 | tf_op jit(solution)/shard_map/project_gate/pallas_call | solution.py:68
  24.9 3.5 %collective-permute-done.4.refs_0_ = bf16[528,128]{1,0:T(8,128)(2,1)S(1)} collective-permute-done((bf16[528,128]{1,0:T(8,128)(2,1)S(1)}, bf16[528,128]{1,0:T(8,128)(2,1)S(1)}, u32[]{:S(2)}, u32[]{:S(2)}) %collective-permute-start.4) | collective-permute-done | bytes 135200 | tf_op jit(solution)/shard_map/ppermute | solution.py:17
  32.0 2.3 %collective-permute-start.9 = (bf16[272,128]{1,0:T(8,128)(2,1)S(1)}, bf16[272,128]{1,0:T(8,128)(2,1)S(1)}, u32[]{:S(2)}, u32[]{:S(2)}) collective-permute-start(bf16[272,128]{1,0:T(8,128)(2,1)S(1)} %get-tuple-element.107), channel_id=1, source_target_pairs={{0,2},{1,3},{2,0},{3,1},{4,6},{5,7},{6,4},{7,5},{8,10},{9,11},{10,... | collective-permute-start | bytes 208904 | tf_op jit(solution)/shard_map/ppermute | solution.py:17
  34.3 2.0 %collective-permute-start.10 = (bf16[272,128]{1,0:T(8,128)(2,1)S(1)}, bf16[272,128]{1,0:T(8,128)(2,1)S(1)}, u32[]{:S(2)}, u32[]{:S(2)}) collective-permute-start(bf16[272,128]{1,0:T(8,128)(2,1)S(1)} %get-tuple-element.107), channel_id=1, source_target_pairs={{0,4},{1,5},{2,6},{3,7},{4,0},{5,1},{6,2},{7,3},{8,12},{9,13},{10,... | collective-permute-start | bytes 208904 | tf_op jit(solution)/shard_map/ppermute | solution.py:17
  38.2 3.5 %ready_state.1.state_ref = f32[16,512,128]{2,1,0:T(8,128)S(1)} custom-call(s32[11]{0:T(128)S(1)} %concatenate.6.place_ref, bf16[512,16,128]{2,1,0:T(8,128)(2,1)} %state_ref.1, f32[8,128]{1,0:T(8,128)S(1)} %broadcast_in_dim.66.refs_5_.alive_ref, f32[272,128]{1,0:T(8,128)S(1)} %get-tuple-element.106.earlier_ref), custom_call_target="tpu_custom_call" | custom-call | bytes 6291456 | tf_op jit(solution)/shard_map/ready_state/pallas_call | solution.py:68
  41.7 1.9 %collective-permute-done.11 = bf16[272,128]{1,0:T(8,128)(2,1)S(1)} collective-permute-done((bf16[272,128]{1,0:T(8,128)(2,1)S(1)}, bf16[272,128]{1,0:T(8,128)(2,1)S(1)}, u32[]{:S(2)}, u32[]{:S(2)}) %collective-permute-start.11) | collective-permute-done | bytes 69664 | tf_op jit(solution)/shard_map/ppermute | solution.py:17
  43.7 1.6 %collective-permute-start.12 = (bf16[272,128]{1,0:T(8,128)(2,1)S(1)}, bf16[272,128]{1,0:T(8,128)(2,1)S(1)}, u32[]{:S(2)}, u32[]{:S(2)}) collective-permute-start(bf16[272,128]{1,0:T(8,128)(2,1)S(1)} %fusion.11), channel_id=1, source_target_pairs={{0,8},{8,0},{16,24},{24,16},{1,9},{9,1},{17,25},{25,17},{2,10},{10... | collective-permute-start | bytes 208904 | tf_op jit(solution)/shard_map/ppermute | solution.py:17
  45.3 1.5 %collective-permute-start.13 = (bf16[272,128]{1,0:T(8,128)(2,1)S(1)}, bf16[272,128]{1,0:T(8,128)(2,1)S(1)}, u32[]{:S(2)}, u32[]{:S(2)}) collective-permute-start(bf16[272,128]{1,0:T(8,128)(2,1)S(1)} %fusion.11), channel_id=1, source_target_pairs={{0,16},{8,24},{16,0},{24,8},{1,17},{9,25},{17,1},{25,9},{2,18},{10... | collective-permute-start | bytes 208904 | tf_op jit(solution)/shard_map/ppermute | solution.py:17
  47.4 2.5 %collective-permute-start.17 = (bf16[512,128]{1,0:T(8,128)(2,1)S(1)}, bf16[512,128]{1,0:T(8,128)(2,1)S(1)}, u32[]{:S(2)}, u32[]{:S(2)}) collective-permute-start(bf16[512,128]{1,0:T(8,128)(2,1)S(1)} %slice.62), channel_id=1, source_target_pairs={{0,4},{1,5},{2,6},{3,7},{4,0},{5,1},{6,2},{7,3},{8,12},{9,13},{10,... | collective-permute-start | bytes 393224 | tf_op jit(solution)/shard_map/ppermute | solution.py:17
  50.2 1.8 %collective-permute-done.14 = bf16[272,128]{1,0:T(8,128)(2,1)S(1)} collective-permute-done((bf16[272,128]{1,0:T(8,128)(2,1)S(1)}, bf16[272,128]{1,0:T(8,128)(2,1)S(1)}, u32[]{:S(2)}, u32[]{:S(2)}) %collective-permute-start.14) | collective-permute-done | bytes 69664 | tf_op jit(solution)/shard_map/ppermute | solution.py:17
  53.4 4.5 %scan.1 = (bf16[512,16,128]{2,1,0:T(8,128)(2,1)}, f32[512,128]{1,0:T(8,128)S(1)}) custom-call(s32[11]{0:T(128)S(1)} %concatenate.6.place_ref, bf16[272,128]{1,0:T(8,128)(2,1)S(1)} %add_convert_fusion.mine_ref, bf16[272,128]{1,0:T(8,128)(2,1)S(1)} %collective-permute-done.15.other_ref, bf16[512,512]{1,0:T(8,128)(2,1)S(1)} %bitcast.36, ...), custom_call_target="tpu_custom_call" | custom-call | bytes 1 | tf_op jit(solution)/shard_map/scan/pallas_call | solution.py:440
  58.7 2.5 %collective-permute-start.21 = (bf16[128,512]{1,0:T(8,128)(2,1)S(1)}, bf16[128,512]{1,0:T(8,128)(2,1)S(1)}, u32[]{:S(2)}, u32[]{:S(2)}) collective-permute-start(bf16[128,512]{1,0:T(8,128)(2,1)S(1)} %gate_rows.1.earlier_ref.refs_0_), channel_id=1, source_target_pairs={{0,4},{1,5},{2,6},{3,7},{4,0},{5,1},{6,2},{7,3},{8,12},{9,13},{10,... | collective-permute-start | bytes 393224 | tf_op jit(solution)/shard_map/ppermute | solution.py:17
  62.3 4.0 %stage_mix.1.refs_8_ = bf16[8,512,1024]{2,1,0:T(8,128)(2,1)S(1)} custom-call(s32[11]{0:T(128)S(1)} %concatenate.6.place_ref, bf16[4096,1024]{1,0:T(8,128)(2,1)} %w_ref.6, bf16[128,512]{1,0:T(8,128)(2,1)S(1)} %gate_rows.1.earlier_ref.refs_0_), custom_call_target="tpu_custom_call" | custom-call | bytes 8388608 | tf_op jit(solution)/shard_map/stage_mix/pallas_call | solution.py:68
  67.3 4.2 %collective-permute-done.21.refs_4_ = bf16[128,512]{1,0:T(8,128)(2,1)S(1)} collective-permute-done((bf16[128,512]{1,0:T(8,128)(2,1)S(1)}, bf16[128,512]{1,0:T(8,128)(2,1)S(1)}, u32[]{:S(2)}, u32[]{:S(2)}) %collective-permute-start.21) | collective-permute-done | bytes 131104 | tf_op jit(solution)/shard_map/ppermute | solution.py:17
  73.6 1.8 %mix_out.1 = (f32[32,1024]{1,0:T(8,128)S(1)}, bf16[32,1024]{1,0:T(8,128)(2,1)S(1)}, bf16[32,1024]{1,0:T(8,128)(2,1)S(1)}, bf16[32,1024]{1,0:T(8,128)(2,1)S(1)}) custom-call(s32[11]{0:T(128)S(1)} %concatenate.6.place_ref, bf16[128,512]{1,0:T(8,128)(2,1)S(1)} %gate_rows.1.earlier_ref.refs_0_, bf16[128,512]{1,0:T(8,128)(2,1)S(1)} %collective-permute-done.18.refs_1_, ...), custom_call_target="tpu_custom_call" | custom-call | tf_op jit(solution)/shard_map/mix_out/pallas_call | solution.py:68
  77.5 1.5 %collective-permute-start.26 = (bf16[32,1024]{1,0:T(8,128)(2,1)S(1)}, bf16[32,1024]{1,0:T(8,128)(2,1)S(1)}, u32[]{:S(2)}, u32[]{:S(2)}) collective-permute-start(bf16[32,1024]{1,0:T(8,128)(2,1)S(1)} %get-tuple-element.125), channel_id=1, source_target_pairs={{0,16},{8,24},{16,0},{24,8},{1,17},{9,25},{17,1},{25,9},{2,18},{10... | collective-permute-start | bytes 196616 | tf_op jit(solution)/shard_map/ppermute | solution.py:17
  79.0 2.3 %collective-permute-done.27 = bf16[32,1024]{1,0:T(8,128)(2,1)S(1)} collective-permute-done((bf16[32,1024]{1,0:T(8,128)(2,1)S(1)}, bf16[32,1024]{1,0:T(8,128)(2,1)S(1)}, u32[]{:S(2)}, u32[]{:S(2)}) %collective-permute-start.27) | collective-permute-done | bytes 65568 | tf_op jit(solution)/shard_map/ppermute | solution.py:17
  85.6 1.8 %collective-permute-done.30.refs_3_ = bf16[32,1024]{1,0:T(8,128)(2,1)S(1)} collective-permute-done((bf16[32,1024]{1,0:T(8,128)(2,1)S(1)}, bf16[32,1024]{1,0:T(8,128)(2,1)S(1)}, u32[]{:S(2)}, u32[]{:S(2)}) %collective-permute-start.30) | collective-permute-done | bytes 65568 | tf_op jit(solution)/shard_map/ppermute | solution.py:17
  89.1 1.9 %query.1 = (bf16[64,2688]{1,0:T(8,128)(2,1)S(1)}, bf16[64,2688]{1,0:T(8,128)(2,1)S(1)}) custom-call(s32[11]{0:T(128)S(1)} %concatenate.6.place_ref, bf16[32,1024]{1,0:T(8,128)(2,1)S(1)} %add_convert_fusion.2.refs_0_, bf16[32,1024]{1,0:T(8,128)(2,1)S(1)} %collective-permute-done.28.refs_1_, bf16[32,1024]{1,0:T(8,128)(2,1)S(1)} %collective-permute-done.29.refs_2_, ...), custom_call_target="tpu_custom_call" | custom-call | tf_op jit(solution)/shard_map/query/pallas_call | solution.py:68
  93.3 3.1 %collective-permute-start.33 = (bf16[16,2688]{1,0:T(8,128)(2,1)S(1)}, bf16[16,2688]{1,0:T(8,128)(2,1)S(1)}, u32[]{:S(2)}, u32[]{:S(2)}) collective-permute-start(bf16[16,2688]{1,0:T(8,128)(2,1)S(1)} %get-tuple-element.132), channel_id=1, source_target_pairs={{0,4},{1,5},{2,6},{3,7},{4,0},{5,1},{6,2},{7,3},{8,12},{9,13},{10,... | collective-permute-start | bytes 258056 | tf_op jit(solution)/shard_map/ppermute | solution.py:17
  96.5 1.9 %collective-permute-start.34 = (bf16[16,2688]{1,0:T(8,128)(2,1)S(1)}, bf16[16,2688]{1,0:T(8,128)(2,1)S(1)}, u32[]{:S(2)}, u32[]{:S(2)}) collective-permute-start(bf16[16,2688]{1,0:T(8,128)(2,1)S(1)} %get-tuple-element.133), channel_id=1, source_target_pairs={{0,6},{1,7},{2,4},{3,5},{4,2},{5,3},{6,0},{7,1},{8,14},{9,15},{10,... | collective-permute-start | bytes 258056 | tf_op jit(solution)/shard_map/ppermute | solution.py:17
  98.4 2.8 %collective-permute-done.32 = bf16[16,2688]{1,0:T(8,128)(2,1)S(1)} collective-permute-done((bf16[16,2688]{1,0:T(8,128)(2,1)S(1)}, bf16[16,2688]{1,0:T(8,128)(2,1)S(1)}, u32[]{:S(2)}, u32[]{:S(2)}) %collective-permute-start.32) | collective-permute-done | bytes 86048 | tf_op jit(solution)/shard_map/ppermute | solution.py:17
  101.2 3.4 %collective-permute-done.34 = bf16[16,2688]{1,0:T(8,128)(2,1)S(1)} collective-permute-done((bf16[16,2688]{1,0:T(8,128)(2,1)S(1)}, bf16[16,2688]{1,0:T(8,128)(2,1)S(1)}, u32[]{:S(2)}, u32[]{:S(2)}) %collective-permute-start.34) | collective-permute-done | bytes 86048 | tf_op jit(solution)/shard_map/ppermute | solution.py:17
  106.4 2.0 %collective-permute-start.40 = (bf16[16,2048]{1,0:T(8,128)(2,1)S(1)}, bf16[16,2048]{1,0:T(8,128)(2,1)S(1)}, u32[]{:S(2)}, u32[]{:S(2)}) collective-permute-start(bf16[16,2048]{1,0:T(8,128)(2,1)S(1)} %bitcast.37), channel_id=1, source_target_pairs={{0,6},{1,7},{2,4},{3,5},{4,2},{5,3},{6,0},{7,1},{8,14},{9,15},{10,... | collective-permute-start | bytes 196616 | tf_op jit(solution)/shard_map/ppermute | solution.py:17
  108.4 2.4 %collective-permute-start.38 = (bf16[16,2048]{1,0:T(8,128)(2,1)S(1)}, bf16[16,2048]{1,0:T(8,128)(2,1)S(1)}, u32[]{:S(2)}, u32[]{:S(2)}) collective-permute-start(bf16[16,2048]{1,0:T(8,128)(2,1)S(1)} %bitcast.39), channel_id=1, source_target_pairs={{0,4},{1,5},{2,6},{3,7},{4,0},{5,1},{6,2},{7,3},{8,12},{9,13},{10,... | collective-permute-start | bytes 196616 | tf_op jit(solution)/shard_map/ppermute | solution.py:17
  110.9 2.7 %stage_head.1.refs_9_ = bf16[4,512,1024]{2,1,0:T(8,128)(2,1)S(1)} custom-call(s32[11]{0:T(128)S(1)} %concatenate.6.place_ref, bf16[2048,1024]{1,0:T(8,128)(2,1)} %w_ref.7, bf16[16,2048]{1,0:T(8,128)(2,1)S(1)} %bitcast.41), custom_call_target="tpu_custom_call" | custom-call | bytes 4194304 | tf_op jit(solution)/shard_map/stage_head/pallas_call | solution.py:68
  115.6 1.9 %head_out.1 = (f32[32,1024]{1,0:T(8,128)S(1)}, bf16[32,1024]{1,0:T(8,128)(2,1)S(1)}, bf16[32,1024]{1,0:T(8,128)(2,1)S(1)}, bf16[32,1024]{1,0:T(8,128)(2,1)S(1)}) custom-call(s32[11]{0:T(128)S(1)} %concatenate.6.place_ref, bf16[16,2048]{1,0:T(8,128)(2,1)S(1)} %bitcast.42, bf16[16,2048]{1,0:T(8,128)(2,1)S(1)} %collective-permute-done.35.refs_1_, ...), custom_call_target="tpu_custom_call" | custom-call | tf_op jit(solution)/shard_map/head_out/pallas_call | solution.py:68
  (138 shorter events, 38.3 us)
Async XLA Ops:
  0.6 9.0 %collective-permute-start.2 = (bf16[32,1024]{1,0:T(8,128)(2,1)}, bf16[32,1024]{1,0:T(8,128)(2,1)S(1)}, u32[]{:S(2)}, u32[]{:S(2)}) collective-permute-start(bf16[32,1024]{1,0:T(8,128)(2,1)} %hidden_ref.1), channel_id=1, source_target_pairs={{0,24},{8,16},{16,8},{24,0},{1,25},{9,17},{17,9},{25,1},{2,26},{10... | collective-permute-start | bytes 196616 | tf_op jit(solution)/shard_map/ppermute | solution.py:17
  4.6 5.0 %collective-permute-start = (bf16[32,1024]{1,0:T(8,128)(2,1)}, bf16[32,1024]{1,0:T(8,128)(2,1)S(1)}, u32[]{:S(2)}, u32[]{:S(2)}) collective-permute-start(bf16[32,1024]{1,0:T(8,128)(2,1)} %hidden_ref.1), channel_id=1, source_target_pairs={{0,8},{8,0},{16,24},{24,16},{1,9},{9,1},{17,25},{25,17},{2,10},{10... | collective-permute-start | bytes 196616 | tf_op jit(solution)/shard_map/ppermute | solution.py:17
  5.1 4.5 %collective-permute-start.1 = (bf16[32,1024]{1,0:T(8,128)(2,1)}, bf16[32,1024]{1,0:T(8,128)(2,1)S(1)}, u32[]{:S(2)}, u32[]{:S(2)}) collective-permute-start(bf16[32,1024]{1,0:T(8,128)(2,1)} %hidden_ref.1), channel_id=1, source_target_pairs={{0,16},{8,24},{16,0},{24,8},{1,17},{9,25},{17,1},{25,9},{2,18},{10... | collective-permute-start | bytes 196616 | tf_op jit(solution)/shard_map/ppermute | solution.py:17
  14.2 14.2 %collective-permute-start.5 = (bf16[528,128]{1,0:T(8,128)(2,1)S(1)}, bf16[528,128]{1,0:T(8,128)(2,1)S(1)}, u32[]{:S(2)}, u32[]{:S(2)}) collective-permute-start(bf16[528,128]{1,0:T(8,128)(2,1)S(1)} %get-tuple-element.85), channel_id=1, source_target_pairs={{0,4},{1,5},{2,6},{3,7},{4,0},{5,1},{6,2},{7,3},{8,12},{9,13},{10,... | collective-permute-start | bytes 405512 | tf_op jit(solution)/shard_map/ppermute | solution.py:17
  17.1 11.3 %collective-permute-start.6 = (bf16[528,128]{1,0:T(8,128)(2,1)S(1)}, bf16[528,128]{1,0:T(8,128)(2,1)S(1)}, u32[]{:S(2)}, u32[]{:S(2)}) collective-permute-start(bf16[528,128]{1,0:T(8,128)(2,1)S(1)} %get-tuple-element.86), channel_id=1, source_target_pairs={{0,6},{1,7},{2,4},{3,5},{4,2},{5,3},{6,0},{7,1},{8,14},{9,15},{10,... | collective-permute-start | bytes 405512 | tf_op jit(solution)/shard_map/ppermute | solution.py:17
  18.4 10.0 %collective-permute-start.4 = (bf16[528,128]{1,0:T(8,128)(2,1)S(1)}, bf16[528,128]{1,0:T(8,128)(2,1)S(1)}, u32[]{:S(2)}, u32[]{:S(2)}) collective-permute-start(bf16[528,128]{1,0:T(8,128)(2,1)S(1)} %get-tuple-element.84.earlier_ref), channel_id=1, source_target_pairs={{0,2},{1,3},{2,0},{3,1},{4,6},{5,7},{6,4},{7,5},{8,10},{9,11},{10,... | collective-permute-start | bytes 405512 | tf_op jit(solution)/shard_map/ppermute | solution.py:17
  32.0 9.7 %collective-permute-start.9 = (bf16[272,128]{1,0:T(8,128)(2,1)S(1)}, bf16[272,128]{1,0:T(8,128)(2,1)S(1)}, u32[]{:S(2)}, u32[]{:S(2)}) collective-permute-start(bf16[272,128]{1,0:T(8,128)(2,1)S(1)} %get-tuple-element.107), channel_id=1, source_target_pairs={{0,2},{1,3},{2,0},{3,1},{4,6},{5,7},{6,4},{7,5},{8,10},{9,11},{10,... | collective-permute-start | bytes 208904 | tf_op jit(solution)/shard_map/ppermute | solution.py:17
  34.3 7.4 %collective-permute-start.10 = (bf16[272,128]{1,0:T(8,128)(2,1)S(1)}, bf16[272,128]{1,0:T(8,128)(2,1)S(1)}, u32[]{:S(2)}, u32[]{:S(2)}) collective-permute-start(bf16[272,128]{1,0:T(8,128)(2,1)S(1)} %get-tuple-element.107), channel_id=1, source_target_pairs={{0,4},{1,5},{2,6},{3,7},{4,0},{5,1},{6,2},{7,3},{8,12},{9,13},{10,... | collective-permute-start | bytes 208904 | tf_op jit(solution)/shard_map/ppermute | solution.py:17
  36.3 7.4 %collective-permute-start.11 = (bf16[272,128]{1,0:T(8,128)(2,1)S(1)}, bf16[272,128]{1,0:T(8,128)(2,1)S(1)}, u32[]{:S(2)}, u32[]{:S(2)}) collective-permute-start(bf16[272,128]{1,0:T(8,128)(2,1)S(1)} %get-tuple-element.107), channel_id=1, source_target_pairs={{0,6},{1,7},{2,4},{3,5},{4,2},{5,3},{6,0},{7,1},{8,14},{9,15},{10,... | collective-permute-start | bytes 208904 | tf_op jit(solution)/shard_map/ppermute | solution.py:17
  37.7 9.6 %collective-permute-start.16 = (bf16[1024,128]{1,0:T(8,128)(2,1)S(1)}, bf16[1024,128]{1,0:T(8,128)(2,1)S(1)}, u32[]{:S(2)}, u32[]{:S(2)}) collective-permute-start(bf16[1024,128]{1,0:T(8,128)(2,1)S(1)} %get-tuple-element.116), channel_id=1, source_target_pairs={{0,2},{1,3},{2,0},{3,1},{4,6},{5,7},{6,4},{7,5},{8,10},{9,11},{10,... | collective-permute-start | bytes 786440 | tf_op jit(solution)/shard_map/ppermute | solution.py:17
  43.7 6.2 %collective-permute-start.12 = (bf16[272,128]{1,0:T(8,128)(2,1)S(1)}, bf16[272,128]{1,0:T(8,128)(2,1)S(1)}, u32[]{:S(2)}, u32[]{:S(2)}) collective-permute-start(bf16[272,128]{1,0:T(8,128)(2,1)S(1)} %fusion.11), channel_id=1, source_target_pairs={{0,8},{8,0},{16,24},{24,16},{1,9},{9,1},{17,25},{25,17},{2,10},{10... | collective-permute-start | bytes 208904 | tf_op jit(solution)/shard_map/ppermute | solution.py:17
  45.3 5.0 %collective-permute-start.13 = (bf16[272,128]{1,0:T(8,128)(2,1)S(1)}, bf16[272,128]{1,0:T(8,128)(2,1)S(1)}, u32[]{:S(2)}, u32[]{:S(2)}) collective-permute-start(bf16[272,128]{1,0:T(8,128)(2,1)S(1)} %fusion.11), channel_id=1, source_target_pairs={{0,16},{8,24},{16,0},{24,8},{1,17},{9,25},{17,1},{25,9},{2,18},{10... | collective-permute-start | bytes 208904 | tf_op jit(solution)/shard_map/ppermute | solution.py:17
  46.8 5.2 %collective-permute-start.14 = (bf16[272,128]{1,0:T(8,128)(2,1)S(1)}, bf16[272,128]{1,0:T(8,128)(2,1)S(1)}, u32[]{:S(2)}, u32[]{:S(2)}) collective-permute-start(bf16[272,128]{1,0:T(8,128)(2,1)S(1)} %fusion.11), channel_id=1, source_target_pairs={{0,24},{8,16},{16,8},{24,0},{1,25},{9,17},{17,9},{25,1},{2,26},{10... | collective-permute-start | bytes 208904 | tf_op jit(solution)/shard_map/ppermute | solution.py:17
  47.4 10.6 %collective-permute-start.17 = (bf16[512,128]{1,0:T(8,128)(2,1)S(1)}, bf16[512,128]{1,0:T(8,128)(2,1)S(1)}, u32[]{:S(2)}, u32[]{:S(2)}) collective-permute-start(bf16[512,128]{1,0:T(8,128)(2,1)S(1)} %slice.62), channel_id=1, source_target_pairs={{0,4},{1,5},{2,6},{3,7},{4,0},{5,1},{6,2},{7,3},{8,12},{9,13},{10,... | collective-permute-start | bytes 393224 | tf_op jit(solution)/shard_map/ppermute | solution.py:17
  58.7 12.8 %collective-permute-start.21 = (bf16[128,512]{1,0:T(8,128)(2,1)S(1)}, bf16[128,512]{1,0:T(8,128)(2,1)S(1)}, u32[]{:S(2)}, u32[]{:S(2)}) collective-permute-start(bf16[128,512]{1,0:T(8,128)(2,1)S(1)} %gate_rows.1.earlier_ref.refs_0_), channel_id=1, source_target_pairs={{0,4},{1,5},{2,6},{3,7},{4,0},{5,1},{6,2},{7,3},{8,12},{9,13},{10,... | collective-permute-start | bytes 393224 | tf_op jit(solution)/shard_map/ppermute | solution.py:17
  61.2 10.3 %collective-permute-start.22 = (bf16[128,512]{1,0:T(8,128)(2,1)S(1)}, bf16[128,512]{1,0:T(8,128)(2,1)S(1)}, u32[]{:S(2)}, u32[]{:S(2)}) collective-permute-start(bf16[128,512]{1,0:T(8,128)(2,1)S(1)} %gate_rows.1.earlier_ref.refs_0_), channel_id=1, source_target_pairs={{0,6},{1,7},{2,4},{3,5},{4,2},{5,3},{6,0},{7,1},{8,14},{9,15},{10,... | collective-permute-start | bytes 393224 | tf_op jit(solution)/shard_map/ppermute | solution.py:17
  62.3 9.9 %collective-permute-start.19 = (bf16[128,512]{1,0:T(8,128)(2,1)S(1)}, bf16[128,512]{1,0:T(8,128)(2,1)S(1)}, u32[]{:S(2)}, u32[]{:S(2)}) collective-permute-start(bf16[128,512]{1,0:T(8,128)(2,1)S(1)} %gate_rows.1.earlier_ref.refs_0_), channel_id=1, source_target_pairs={{0,2},{1,3},{2,0},{3,1},{4,6},{5,7},{6,4},{7,5},{8,10},{9,11},{10,... | collective-permute-start | bytes 393224 | tf_op jit(solution)/shard_map/ppermute | solution.py:17
  62.3 9.9 %collective-permute-start.18 = (bf16[128,512]{1,0:T(8,128)(2,1)S(1)}, bf16[128,512]{1,0:T(8,128)(2,1)S(1)}, u32[]{:S(2)}, u32[]{:S(2)}) collective-permute-start(bf16[128,512]{1,0:T(8,128)(2,1)S(1)} %gate_rows.1.earlier_ref.refs_0_), channel_id=1, source_target_pairs={{0,1},{1,0},{2,3},{3,2},{4,5},{5,4},{6,7},{7,6},{8,9},{9,8},{10,11... | collective-permute-start | bytes 393224 | tf_op jit(solution)/shard_map/ppermute | solution.py:17
  75.4 5.8 %collective-permute-start.27 = (bf16[32,1024]{1,0:T(8,128)(2,1)S(1)}, bf16[32,1024]{1,0:T(8,128)(2,1)S(1)}, u32[]{:S(2)}, u32[]{:S(2)}) collective-permute-start(bf16[32,1024]{1,0:T(8,128)(2,1)S(1)} %get-tuple-element.126), channel_id=1, source_target_pairs={{0,24},{8,16},{16,8},{24,0},{1,25},{9,17},{17,9},{25,1},{2,26},{10... | collective-permute-start | bytes 196616 | tf_op jit(solution)/shard_map/ppermute | solution.py:17
  76.0 5.3 %collective-permute-start.25 = (bf16[32,1024]{1,0:T(8,128)(2,1)S(1)}, bf16[32,1024]{1,0:T(8,128)(2,1)S(1)}, u32[]{:S(2)}, u32[]{:S(2)}) collective-permute-start(bf16[32,1024]{1,0:T(8,128)(2,1)S(1)} %get-tuple-element.124), channel_id=1, source_target_pairs={{0,8},{8,0},{16,24},{24,16},{1,9},{9,1},{17,25},{25,17},{2,10},{10... | collective-permute-start | bytes 196616 | tf_op jit(solution)/shard_map/ppermute | solution.py:17
  77.5 4.5 %collective-permute-start.26 = (bf16[32,1024]{1,0:T(8,128)(2,1)S(1)}, bf16[32,1024]{1,0:T(8,128)(2,1)S(1)}, u32[]{:S(2)}, u32[]{:S(2)}) collective-permute-start(bf16[32,1024]{1,0:T(8,128)(2,1)S(1)} %get-tuple-element.125), channel_id=1, source_target_pairs={{0,16},{8,24},{16,0},{24,8},{1,17},{9,25},{17,1},{25,9},{2,18},{10... | collective-permute-start | bytes 196616 | tf_op jit(solution)/shard_map/ppermute | solution.py:17
  82.0 5.3 %collective-permute-start.30 = (bf16[32,1024]{1,0:T(8,128)(2,1)S(1)}, bf16[32,1024]{1,0:T(8,128)(2,1)S(1)}, u32[]{:S(2)}, u32[]{:S(2)}) collective-permute-start(bf16[32,1024]{1,0:T(8,128)(2,1)S(1)} %add_convert_fusion.2.refs_0_), channel_id=1, source_target_pairs={{0,24},{8,16},{16,8},{24,0},{1,25},{9,17},{17,9},{25,1},{2,26},{10... | collective-permute-start | bytes 196616 | tf_op jit(solution)/shard_map/ppermute | solution.py:17
  83.3 4.4 %collective-permute-start.28 = (bf16[32,1024]{1,0:T(8,128)(2,1)S(1)}, bf16[32,1024]{1,0:T(8,128)(2,1)S(1)}, u32[]{:S(2)}, u32[]{:S(2)}) collective-permute-start(bf16[32,1024]{1,0:T(8,128)(2,1)S(1)} %add_convert_fusion.2.refs_0_), channel_id=1, source_target_pairs={{0,8},{8,0},{16,24},{24,16},{1,9},{9,1},{17,25},{25,17},{2,10},{10... | collective-permute-start | bytes 196616 | tf_op jit(solution)/shard_map/ppermute | solution.py:17
  93.3 11.3 %collective-permute-start.33 = (bf16[16,2688]{1,0:T(8,128)(2,1)S(1)}, bf16[16,2688]{1,0:T(8,128)(2,1)S(1)}, u32[]{:S(2)}, u32[]{:S(2)}) collective-permute-start(bf16[16,2688]{1,0:T(8,128)(2,1)S(1)} %get-tuple-element.132), channel_id=1, source_target_pairs={{0,4},{1,5},{2,6},{3,7},{4,0},{5,1},{6,2},{7,3},{8,12},{9,13},{10,... | collective-permute-start | bytes 258056 | tf_op jit(solution)/shard_map/ppermute | solution.py:17
  96.5 4.8 %collective-permute-start.32 = (bf16[16,2688]{1,0:T(8,128)(2,1)S(1)}, bf16[16,2688]{1,0:T(8,128)(2,1)S(1)}, u32[]{:S(2)}, u32[]{:S(2)}) collective-permute-start(bf16[16,2688]{1,0:T(8,128)(2,1)S(1)} %get-tuple-element.131), channel_id=1, source_target_pairs={{0,2},{1,3},{2,0},{3,1},{4,6},{5,7},{6,4},{7,5},{8,10},{9,11},{10,... | collective-permute-start | bytes 258056 | tf_op jit(solution)/shard_map/ppermute | solution.py:17
  96.5 8.2 %collective-permute-start.34 = (bf16[16,2688]{1,0:T(8,128)(2,1)S(1)}, bf16[16,2688]{1,0:T(8,128)(2,1)S(1)}, u32[]{:S(2)}, u32[]{:S(2)}) collective-permute-start(bf16[16,2688]{1,0:T(8,128)(2,1)S(1)} %get-tuple-element.133), channel_id=1, source_target_pairs={{0,6},{1,7},{2,4},{3,5},{4,2},{5,3},{6,0},{7,1},{8,14},{9,15},{10,... | collective-permute-start | bytes 258056 | tf_op jit(solution)/shard_map/ppermute | solution.py:17
  106.4 7.2 %collective-permute-start.40 = (bf16[16,2048]{1,0:T(8,128)(2,1)S(1)}, bf16[16,2048]{1,0:T(8,128)(2,1)S(1)}, u32[]{:S(2)}, u32[]{:S(2)}) collective-permute-start(bf16[16,2048]{1,0:T(8,128)(2,1)S(1)} %bitcast.37), channel_id=1, source_target_pairs={{0,6},{1,7},{2,4},{3,5},{4,2},{5,3},{6,0},{7,1},{8,14},{9,15},{10,... | collective-permute-start | bytes 196616 | tf_op jit(solution)/shard_map/ppermute | solution.py:17
  108.4 5.8 %collective-permute-start.36 = (bf16[16,2048]{1,0:T(8,128)(2,1)S(1)}, bf16[16,2048]{1,0:T(8,128)(2,1)S(1)}, u32[]{:S(2)}, u32[]{:S(2)}) collective-permute-start(bf16[16,2048]{1,0:T(8,128)(2,1)S(1)} %bitcast.38), channel_id=1, source_target_pairs={{0,2},{1,3},{2,0},{3,1},{4,6},{5,7},{6,4},{7,5},{8,10},{9,11},{10,... | collective-permute-start | bytes 196616 | tf_op jit(solution)/shard_map/ppermute | solution.py:17
  108.4 5.9 %collective-permute-start.38 = (bf16[16,2048]{1,0:T(8,128)(2,1)S(1)}, bf16[16,2048]{1,0:T(8,128)(2,1)S(1)}, u32[]{:S(2)}, u32[]{:S(2)}) collective-permute-start(bf16[16,2048]{1,0:T(8,128)(2,1)S(1)} %bitcast.39), channel_id=1, source_target_pairs={{0,4},{1,5},{2,6},{3,7},{4,0},{5,1},{6,2},{7,3},{8,12},{9,13},{10,... | collective-permute-start | bytes 196616 | tf_op jit(solution)/shard_map/ppermute | solution.py:17
  117.5 5.9 %collective-permute-start.44 = (bf16[32,1024]{1,0:T(8,128)(2,1)S(1)}, bf16[32,1024]{1,0:T(8,128)(2,1)S(1)}, u32[]{:S(2)}, u32[]{:S(2)}) collective-permute-start(bf16[32,1024]{1,0:T(8,128)(2,1)S(1)} %get-tuple-element.139), channel_id=1, source_target_pairs={{0,24},{8,16},{16,8},{24,0},{1,25},{9,17},{17,9},{25,1},{2,26},{10... | collective-permute-start | bytes 196616 | tf_op jit(solution)/shard_map/ppermute | solution.py:17
  118.3 5.2 %collective-permute-start.42 = (bf16[32,1024]{1,0:T(8,128)(2,1)S(1)}, bf16[32,1024]{1,0:T(8,128)(2,1)S(1)}, u32[]{:S(2)}, u32[]{:S(2)}) collective-permute-start(bf16[32,1024]{1,0:T(8,128)(2,1)S(1)} %get-tuple-element.137), channel_id=1, source_target_pairs={{0,8},{8,0},{16,24},{24,16},{1,9},{9,1},{17,25},{25,17},{2,10},{10... | collective-permute-start | bytes 196616 | tf_op jit(solution)/shard_map/ppermute | solution.py:17
  119.8 4.4 %collective-permute-start.43 = (bf16[32,1024]{1,0:T(8,128)(2,1)S(1)}, bf16[32,1024]{1,0:T(8,128)(2,1)S(1)}, u32[]{:S(2)}, u32[]{:S(2)}) collective-permute-start(bf16[32,1024]{1,0:T(8,128)(2,1)S(1)} %get-tuple-element.138), channel_id=1, source_target_pairs={{0,16},{8,24},{16,0},{24,8},{1,17},{9,25},{17,1},{25,9},{2,18},{10... | collective-permute-start | bytes 196616 | tf_op jit(solution)/shard_map/ppermute | solution.py:17
  (27 other events, 189.7 us)

commit v5 on v4

--- a/solution.py
+++ b/solution.py
@@ -402,12 +402,11 @@
     steps, lanes = own // block, batch // 128
 
     def kernel(place_ref, mine_ref, other_ref, dtw_ref, params_ref, state_ref, *refs):
-        xa_ref, new_ref, value_ref, low, behind, packed, sems = refs
+        xa_ref, packed, value_ref, low, behind = refs
         core = place_ref[place_ref.shape[0] - 1]
         first = jnp.broadcast_to(core, mine_ref.shape) == 0
         low[:half] = jnp.where(first, mine_ref[...], other_ref[...])
         low[half:] = jnp.where(first, other_ref[...], mine_ref[...])
-        copies = []
         for i in range(steps):
             here = slice(i * block, (i + 1) * block)
             pre = dot(dtw_ref[here, :], low[:rank, :]) + params_ref[here, taps + 2 : taps + 3]
@@ -419,22 +418,17 @@
                 rate = params_ref[here, taps + 4 + n : taps + 5 + n]
                 bm = low[rank + n : rank + n + 1, :].astype(F32)
                 cm = low[rank + nstate + n : rank + nstate + n + 1, :].astype(F32)
-                fresh = jnp.exp(-step * rate) * state_ref[n, here, :] + drive * bm
+                fresh = jnp.exp2(step * rate) * state_ref[n, here, :] + drive * bm
                 for c in range(lanes):
                     behind[i % 2, c, pl.ds(n, block, stride=nstate), :] = fresh[
                         :, c * 128 : (c + 1) * 128
                     ]
                 value = value + fresh * cm
             for c in range(lanes):
-                packed[i, :, :, c * 128 : (c + 1) * 128] = (
+                packed[here, :, c * 128 : (c + 1) * 128] = (
                     behind[i % 2, c].reshape(block, nstate, 128).astype(BF16)
                 )
-            copy = pltpu.make_async_copy(packed.at[i], new_ref.at[pl.ds(i * block, block)], sems.at[i])
-            copy.start()
-            copies.append(copy)
             value_ref[here, :] = value
-        for copy in copies:
-            copy.wait()
 
     pairs = [in_vmem(a) for a in (mine, other, dt_rows, params, state, xa)]
     return pl.pallas_call(
@@ -444,23 +438,52 @@
             grid=(),
             in_specs=[spec for _, spec in pairs],
             out_specs=[
-                pl.BlockSpec(memory_space=pltpu.HBM),
+                pl.BlockSpec(memory_space=pltpu.VMEM),
                 pl.BlockSpec(memory_space=pltpu.VMEM),
             ],
             scratch_shapes=[
                 pltpu.VMEM((2 * half, batch), BF16),
                 pltpu.VMEM((2, lanes, block * nstate, 128), F32),
-                pltpu.VMEM((steps, block, nstate, batch), BF16),
-                pltpu.SemaphoreType.DMA((steps,)),
             ],
         ),
         out_shape=[
-            pltpu.HBM((own, nstate, batch), BF16),
+            pltpu.VMEM((own, nstate, batch), BF16),
             pltpu.VMEM((own, batch), F32),
         ],
         compiler_params=pltpu.CompilerParams(vmem_limit_bytes=18 * MIB),
         cost_estimate=pl.CostEstimate(flops=0, bytes_accessed=1, transcendentals=0),
         name="scan",
+    )(place, *[array for array, _ in pairs])
+
+
+def store_state(place, state, earlier):
+    parts = 4
+    rows = state.shape[0] // parts
+
+    def kernel(place_ref, state_ref, earlier_ref, out_ref, sems):
+        pairs = [
+            (state_ref.at[i * rows : (i + 1) * rows], out_ref.at[i * rows : (i + 1) * rows])
+            for i in range(parts)
+        ]
+        for copy in fetch(pairs, sems):
+            copy.wait()
+
+    pairs = [in_vmem(state), anywhere(earlier)]
+    return pl.pallas_call(
+        kernel,
+        grid_spec=pltpu.PrefetchScalarGridSpec(
+            num_scalar_prefetch=1,
+            grid=(),
+            in_specs=[spec for _, spec in pairs],
+            out_specs=pl.BlockSpec(memory_space=pltpu.HBM),
+            scratch_shapes=[pltpu.SemaphoreType.DMA((parts,))],
+        ),
+        out_shape=pltpu.HBM(state.shape, BF16),
+        compiler_params=pltpu.CompilerParams(vmem_limit_bytes=4 * MIB),
+        cost_estimate=pl.CostEstimate(
+            flops=0, bytes_accessed=state.size * 2, transcendentals=0
+        ),
+        name="store_state",
     )(place, *[array for array, _ in pairs])
 
 
@@ -685,7 +708,7 @@
     alive = jnp.broadcast_to(alive[None, :].astype(F32), (8, batch))
     params = jnp.transpose(
         jnp.concatenate(
-            [conv_weight, conv_bias[None], dt_bias[None], d_skip[None], jnp.exp(a_log)], axis=0
+            [conv_weight, conv_bias[None], dt_bias[None], d_skip[None], -math.log2(math.e) * jnp.exp(a_log)], axis=0
         )
     )
     dt_rows = jnp.transpose(dt_proj)
@@ -699,7 +722,7 @@
     part, wire, z_odd, z_even = add_both(
         place, part, swap(give, "yz", 1), keep.reshape(chips * own, batch), z_received, chips
     )
-    got = swaps_chip([wire] * (chips - 1), (2, 1, 0), (2, 1, 0))
+    got = swaps_chip([wire] * (chips - 1), (0, 1, 2), (0, 1, 2))
     z_near = swap(z_odd, "yz", 2)
     old = ready_state(place, ssm_state, alive, part)
     got, old = lax.optimization_barrier((got, old))
@@ -719,7 +742,10 @@
     flattened = attention_projection.reshape(width, group_count * group_cols)
     weights = stage_rows(place, mixer_output, yz, gated, True, chips, "stage_mix")
     got = swaps_chip([gated] * (chips - 1), (0, 1, 2), (0, 0, 0))
-    *got[1:], weights, flattened = lax.optimization_barrier((*got[1:], weights, flattened))
+    ssm_new = store_state(place, ssm_new, gated)
+    *got[1:], weights, flattened, ssm_new = lax.optimization_barrier(
+        (*got[1:], weights, flattened, ssm_new)
+    )
     pieces = gather_yz(gated, got)
     own_rows, wires = mix_out(place, pieces, weights, gx, chips)
     first_out = (hidden_in.astype(F32) + total_of(own_rows, swaps_gx(wires))).astype(BF16)
@@ -727,7 +753,7 @@
     pieces = [first_out] + swaps_gx([first_out] * (gx - 1))
     give, keep = query(place, pieces, assign[None, :], norm_gain_b[None, :], flattened, chips)
     entries, wires = add_pairs(keep, swap(give, "yz", 1), chips, place, "add_query")
-    entries = total_of(entries, swaps_chip(wires, (2, 1, 0), (2, 0, 1)))
+    entries = total_of(entries, swaps_chip(wires, (1, 2, 0), (2, 0, 0)))
     scale = lax.rsqrt(entries[:, -1:] / whole_width + 1e-05)
     newest_entry = (entries[:, :-128] * scale).astype(BF16)
     newest_entry = newest_entry.reshape(slot_count, group_count, group_cols)

time: 125 us -> 124 us (level)
    pallas_call x0 -> x1, Pallas kernels: none -> 1.88 us  [store_state(): pl.pallas_call(kernel, grid_spec=pltpu.PrefetchScalarGridSpec(num_scalar_...]
  transfers between devices with their start and end apart: 45 -> 45, of which waited for: 27 -> 25; matrix products, arithmetic and copies ran while one was open for 3% -> 3% of each run, Pallas kernels for 22% -> 23%
where the time goes in v5:
time: 124 us
  starting transfers between devices  46.3 us (37%)
  Pallas kernels  38.4 us (31%)
  waiting for transfers between devices  31.4 us (25%)
  local copies, waits for them, and re-layouts  4.07 us (3%)
  other arithmetic  1.66 us (1%)
    ppermute x45, starting transfers between devices, swap(): return lax.ppermute(value, axis, [(i, i ^ bits) for i in range(size)])  46.3 us
    pallas_call x15, Pallas kernels, call(): pl.pallas_call(kernel, grid_spec=pltpu.PrefetchScalarGridSpec(num_scalar_...  32.9 us
    ppermute x45, waiting for transfers between devices, swap(): return lax.ppermute(value, axis, [(i, i ^ bits) for i in range(size)])  31.4 us
    pallas_call x1, Pallas kernels, scan(): pl.pallas_call(kernel, grid_spec=pltpu.PrefetchScalarGridSpec(num_scalar_...  3.57 us
  transfers between devices with their start and end apart: 45, of which 25 were waited for; matrix products, arithmetic and copies ran while one was open for 3% of the time, Pallas kernels for 23%

profile of v5, /device:TPU:0, one launch (start us, length us, event | category | flops | bytes accessed | tf_op | source)
XLA Modules:
  0.0 123.9 jit_solution(13974887872382307338)
XLA Ops:
  0.6 4.0 %collective-permute-start.2 = (bf16[32,1024]{1,0:T(8,128)(2,1)}, bf16[32,1024]{1,0:T(8,128)(2,1)S(1)}, u32[]{:S(2)}, u32[]{:S(2)}) collective-permute-start(bf16[32,1024]{1,0:T(8,128)(2,1)} %hidden_ref.1), channel_id=1, source_target_pairs={{0,24},{8,16},{16,8},{24,0},{1,25},{9,17},{17,9},{25,1},{2,26},{10... | collective-permute-start | bytes 196616 | tf_op jit(solution)/shard_map/ppermute | solution.py:17
  5.3 4.0 %stage_first.1 = (bf16[8,512,1024]{2,1,0:T(8,128)(2,1)S(1)}, bf16[32,1024]{1,0:T(8,128)(2,1)S(1)}, f32[1,1024]{1,0:T(1,128)S(1)}) custom-call(s32[11]{0:T(128)S(1)} %concatenate.6.place_ref, bf16[2,4096,1024]{2,1,0:T(8,128)(2,1)} %w_ref.5, bf16[32,1024]{1,0:T(8,128)(2,1)} %hidden_ref.1, f32[1,1024]{1,0:T(1,128)} %bitcast.57), custom_call_target="tpu_custom_call" | custom-call | bytes 8388608 | tf_op jit(solution)/shard_map/stage_first/pallas_call | solution.py:68
  9.6 2.0 %project_first.1 = (bf16[4,528,128]{2,1,0:T(8,128)(2,1)S(1)}, bf16[1024,128]{1,0:T(8,128)(2,1)S(1)}, f32[16,128]{1,0:T(8,128)S(1)}) custom-call(s32[11]{0:T(128)S(1)} %concatenate.6.place_ref, bf16[32,1024]{1,0:T(8,128)(2,1)S(1)} %get-tuple-element.76.refs_0_, bf16[32,1024]{1,0:T(8,128)(2,1)S(1)} %collective-permute-done.refs_1_, ...), custom_call_target="tpu_custom_call" | custom-call | tf_op jit(solution)/shard_map/project_first/pallas_call | solution.py:68
  11.7 1.8 %project_keep.1 = bf16[4,528,128]{2,1,0:T(8,128)(2,1)S(1)} custom-call(s32[11]{0:T(128)S(1)} %concatenate.6.place_ref, bf16[8,512,1024]{2,1,0:T(8,128)(2,1)S(1)} %get-tuple-element.75.refs_5_.w_ref, bf16[1024,128]{1,0:T(8,128)(2,1)S(1)} %get-tuple-element.81.gained_ref, f32[16,128]{1,0:T(8,128)S(1)} %get-tuple-element.82.squares_ref), custom_call_target="tpu_custom_call" | custom-call | tf_op jit(solution)/shard_map/project_keep/pallas_call | solution.py:68
  14.2 2.8 %collective-permute-start.5 = (bf16[528,128]{1,0:T(8,128)(2,1)S(1)}, bf16[528,128]{1,0:T(8,128)(2,1)S(1)}, u32[]{:S(2)}, u32[]{:S(2)}) collective-permute-start(bf16[528,128]{1,0:T(8,128)(2,1)S(1)} %get-tuple-element.86), channel_id=1, source_target_pairs={{0,4},{1,5},{2,6},{3,7},{4,0},{5,1},{6,2},{7,3},{8,12},{9,13},{10,... | collective-permute-start | bytes 405512 | tf_op jit(solution)/shard_map/ppermute | solution.py:17
  19.6 5.3 %project_gate.1 = (bf16[4,512,128]{2,1,0:T(8,128)(2,1)S(1)}, bf16[4,512,128]{2,1,0:T(8,128)(2,1)S(1)}, bf16[3,512,128]{2,1,0:T(8,128)(2,1)S(1)}, bf16[544,512]{1,0:T(8,128)(2,1)S(1)}) custom-call(s32[11]{0:T(128)S(1)} %concatenate.6.place_ref, bf16[2,4096,1024]{2,1,0:T(8,128)(2,1)} %w_ref.5, bf16[1024,128]{1,0:T(8,128)(2,1)S(1)} %get-tuple-element.81.gained_ref, ...), custom_call_target="tpu_custom_call" | custom-call | bytes 8388608 | tf_op jit(solution)/shard_map/project_gate/pallas_call | solution.py:68
  24.9 3.5 %collective-permute-done.4.refs_0_ = bf16[528,128]{1,0:T(8,128)(2,1)S(1)} collective-permute-done((bf16[528,128]{1,0:T(8,128)(2,1)S(1)}, bf16[528,128]{1,0:T(8,128)(2,1)S(1)}, u32[]{:S(2)}, u32[]{:S(2)}) %collective-permute-start.4) | collective-permute-done | bytes 135200 | tf_op jit(solution)/shard_map/ppermute | solution.py:17
  32.0 3.6 %collective-permute-start.11 = (bf16[272,128]{1,0:T(8,128)(2,1)S(1)}, bf16[272,128]{1,0:T(8,128)(2,1)S(1)}, u32[]{:S(2)}, u32[]{:S(2)}) collective-permute-start(bf16[272,128]{1,0:T(8,128)(2,1)S(1)} %get-tuple-element.108), channel_id=1, source_target_pairs={{0,6},{1,7},{2,4},{3,5},{4,2},{5,3},{6,0},{7,1},{8,14},{9,15},{10,... | collective-permute-start | bytes 208904 | tf_op jit(solution)/shard_map/ppermute | solution.py:17
  36.8 1.5 %collective-permute-start.16 = (bf16[1024,128]{1,0:T(8,128)(2,1)S(1)}, bf16[1024,128]{1,0:T(8,128)(2,1)S(1)}, u32[]{:S(2)}, u32[]{:S(2)}) collective-permute-start(bf16[1024,128]{1,0:T(8,128)(2,1)S(1)} %get-tuple-element.117), channel_id=1, source_target_pairs={{0,2},{1,3},{2,0},{3,1},{4,6},{5,7},{6,4},{7,5},{8,10},{9,11},{10,... | collective-permute-start | bytes 786440 | tf_op jit(solution)/shard_map/ppermute | solution.py:17
  38.3 3.5 %ready_state.1.state_ref = f32[16,512,128]{2,1,0:T(8,128)S(1)} custom-call(s32[11]{0:T(128)S(1)} %concatenate.6.place_ref, bf16[512,16,128]{2,1,0:T(8,128)(2,1)} %state_ref.1, f32[8,128]{1,0:T(8,128)S(1)} %broadcast_in_dim.66.refs_5_.alive_ref, f32[272,128]{1,0:T(8,128)S(1)} %get-tuple-element.107.earlier_ref), custom_call_target="tpu_custom_call" | custom-call | bytes 6291456 | tf_op jit(solution)/shard_map/ready_state/pallas_call | solution.py:68
  42.9 1.6 %collective-permute-start.12 = (bf16[272,128]{1,0:T(8,128)(2,1)S(1)}, bf16[272,128]{1,0:T(8,128)(2,1)S(1)}, u32[]{:S(2)}, u32[]{:S(2)}) collective-permute-start(bf16[272,128]{1,0:T(8,128)(2,1)S(1)} %fusion.11), channel_id=1, source_target_pairs={{0,8},{8,0},{16,24},{24,16},{1,9},{9,1},{17,25},{25,17},{2,10},{10... | collective-permute-start | bytes 208904 | tf_op jit(solution)/shard_map/ppermute | solution.py:17
  44.5 1.5 %collective-permute-start.13 = (bf16[272,128]{1,0:T(8,128)(2,1)S(1)}, bf16[272,128]{1,0:T(8,128)(2,1)S(1)}, u32[]{:S(2)}, u32[]{:S(2)}) collective-permute-start(bf16[272,128]{1,0:T(8,128)(2,1)S(1)} %fusion.11), channel_id=1, source_target_pairs={{0,16},{8,24},{16,0},{24,8},{1,17},{9,25},{17,1},{25,9},{2,18},{10... | collective-permute-start | bytes 208904 | tf_op jit(solution)/shard_map/ppermute | solution.py:17
  47.6 1.4 %collective-permute-start.17 = (bf16[512,128]{1,0:T(8,128)(2,1)S(1)}, bf16[512,128]{1,0:T(8,128)(2,1)S(1)}, u32[]{:S(2)}, u32[]{:S(2)}) collective-permute-start(bf16[512,128]{1,0:T(8,128)(2,1)S(1)} %slice.62), channel_id=1, source_target_pairs={{0,4},{1,5},{2,6},{3,7},{4,0},{5,1},{6,2},{7,3},{8,12},{9,13},{10,... | collective-permute-start | bytes 393224 | tf_op jit(solution)/shard_map/ppermute | solution.py:17
  49.1 2.1 %collective-permute-done.14 = bf16[272,128]{1,0:T(8,128)(2,1)S(1)} collective-permute-done((bf16[272,128]{1,0:T(8,128)(2,1)S(1)}, bf16[272,128]{1,0:T(8,128)(2,1)S(1)}, u32[]{:S(2)}, u32[]{:S(2)}) %collective-permute-start.14) | collective-permute-done | bytes 69664 | tf_op jit(solution)/shard_map/ppermute | solution.py:17
  52.6 3.6 %scan.1 = (bf16[512,16,128]{2,1,0:T(8,128)(2,1)S(1)}, f32[512,128]{1,0:T(8,128)S(1)}) custom-call(s32[11]{0:T(128)S(1)} %concatenate.6.place_ref, bf16[272,128]{1,0:T(8,128)(2,1)S(1)} %add_convert_fusion.mine_ref, bf16[272,128]{1,0:T(8,128)(2,1)S(1)} %collective-permute-done.15.other_ref, bf16[512,512]{1,0:T(8,128)(2,1)S(1)} %bitcast.36, ...), custom_call_target="tpu_custom_call" | custom-call | bytes 1 | tf_op jit(solution)/shard_map/scan/pallas_call | solution.py:434
  58.3 2.0 %collective-permute-start.22 = (bf16[128,512]{1,0:T(8,128)(2,1)S(1)}, bf16[128,512]{1,0:T(8,128)(2,1)S(1)}, u32[]{:S(2)}, u32[]{:S(2)}) collective-permute-start(bf16[128,512]{1,0:T(8,128)(2,1)S(1)} %gate_rows.1.earlier_ref.refs_0_), channel_id=1, source_target_pairs={{0,6},{1,7},{2,4},{3,5},{4,2},{5,3},{6,0},{7,1},{8,14},{9,15},{10,... | collective-permute-start | bytes 393224 | tf_op jit(solution)/shard_map/ppermute | solution.py:17
  60.8 1.9 %store_state.1 = bf16[512,16,128]{2,1,0:T(8,128)(2,1)} custom-call(s32[11]{0:T(128)S(1)} %concatenate.6.place_ref, bf16[512,16,128]{2,1,0:T(8,128)(2,1)S(1)} %get-tuple-element.121.state_ref, bf16[128,512]{1,0:T(8,128)(2,1)S(1)} %gate_rows.1.earlier_ref.refs_0_), custom_call_target="tpu_custom_call" | custom-call | bytes 2097152 | tf_op jit(solution)/shard_map/store_state/pallas_call | solution.py:472
  62.7 4.0 %stage_mix.1.refs_8_ = bf16[8,512,1024]{2,1,0:T(8,128)(2,1)S(1)} custom-call(s32[11]{0:T(128)S(1)} %concatenate.6.place_ref, bf16[4096,1024]{1,0:T(8,128)(2,1)} %w_ref.6, bf16[128,512]{1,0:T(8,128)(2,1)S(1)} %gate_rows.1.earlier_ref.refs_0_), custom_call_target="tpu_custom_call" | custom-call | bytes 8388608 | tf_op jit(solution)/shard_map/stage_mix/pallas_call | solution.py:68
  67.8 2.0 %collective-permute-done.21.refs_4_ = bf16[128,512]{1,0:T(8,128)(2,1)S(1)} collective-permute-done((bf16[128,512]{1,0:T(8,128)(2,1)S(1)}, bf16[128,512]{1,0:T(8,128)(2,1)S(1)}, u32[]{:S(2)}, u32[]{:S(2)}) %collective-permute-start.21) | collective-permute-done | bytes 131104 | tf_op jit(solution)/shard_map/ppermute | solution.py:17
  71.9 1.8 %mix_out.1 = (f32[32,1024]{1,0:T(8,128)S(1)}, bf16[32,1024]{1,0:T(8,128)(2,1)S(1)}, bf16[32,1024]{1,0:T(8,128)(2,1)S(1)}, bf16[32,1024]{1,0:T(8,128)(2,1)S(1)}) custom-call(s32[11]{0:T(128)S(1)} %concatenate.6.place_ref, bf16[128,512]{1,0:T(8,128)(2,1)S(1)} %gate_rows.1.earlier_ref.refs_0_, bf16[128,512]{1,0:T(8,128)(2,1)S(1)} %collective-permute-done.18.refs_1_, ...), custom_call_target="tpu_custom_call" | custom-call | tf_op jit(solution)/shard_map/mix_out/pallas_call | solution.py:68
  75.8 1.5 %collective-permute-start.26 = (bf16[32,1024]{1,0:T(8,128)(2,1)S(1)}, bf16[32,1024]{1,0:T(8,128)(2,1)S(1)}, u32[]{:S(2)}, u32[]{:S(2)}) collective-permute-start(bf16[32,1024]{1,0:T(8,128)(2,1)S(1)} %get-tuple-element.127), channel_id=1, source_target_pairs={{0,16},{8,24},{16,0},{24,8},{1,17},{9,25},{17,1},{25,9},{2,18},{10... | collective-permute-start | bytes 196616 | tf_op jit(solution)/shard_map/ppermute | solution.py:17
  77.3 2.3 %collective-permute-done.27 = bf16[32,1024]{1,0:T(8,128)(2,1)S(1)} collective-permute-done((bf16[32,1024]{1,0:T(8,128)(2,1)S(1)}, bf16[32,1024]{1,0:T(8,128)(2,1)S(1)}, u32[]{:S(2)}, u32[]{:S(2)}) %collective-permute-start.27) | collective-permute-done | bytes 65568 | tf_op jit(solution)/shard_map/ppermute | solution.py:17
  81.7 1.5 %collective-permute-start.28 = (bf16[32,1024]{1,0:T(8,128)(2,1)S(1)}, bf16[32,1024]{1,0:T(8,128)(2,1)S(1)}, u32[]{:S(2)}, u32[]{:S(2)}) collective-permute-start(bf16[32,1024]{1,0:T(8,128)(2,1)S(1)} %add_convert_fusion.2.refs_0_), channel_id=1, source_target_pairs={{0,8},{8,0},{16,24},{24,16},{1,9},{9,1},{17,25},{25,17},{2,10},{10... | collective-permute-start | bytes 196616 | tf_op jit(solution)/shard_map/ppermute | solution.py:17
  83.9 1.7 %collective-permute-done.30.refs_3_ = bf16[32,1024]{1,0:T(8,128)(2,1)S(1)} collective-permute-done((bf16[32,1024]{1,0:T(8,128)(2,1)S(1)}, bf16[32,1024]{1,0:T(8,128)(2,1)S(1)}, u32[]{:S(2)}, u32[]{:S(2)}) %collective-permute-start.30) | collective-permute-done | bytes 65568 | tf_op jit(solution)/shard_map/ppermute | solution.py:17
  87.4 1.9 %query.1 = (bf16[64,2688]{1,0:T(8,128)(2,1)S(1)}, bf16[64,2688]{1,0:T(8,128)(2,1)S(1)}) custom-call(s32[11]{0:T(128)S(1)} %concatenate.6.place_ref, bf16[32,1024]{1,0:T(8,128)(2,1)S(1)} %add_convert_fusion.2.refs_0_, bf16[32,1024]{1,0:T(8,128)(2,1)S(1)} %collective-permute-done.28.refs_1_, bf16[32,1024]{1,0:T(8,128)(2,1)S(1)} %collective-permute-done.29.refs_2_, ...), custom_call_target="tpu_custom_call" | custom-call | tf_op jit(solution)/shard_map/query/pallas_call | solution.py:68
  91.7 3.3 %collective-permute-start.33 = (bf16[16,2688]{1,0:T(8,128)(2,1)S(1)}, bf16[16,2688]{1,0:T(8,128)(2,1)S(1)}, u32[]{:S(2)}, u32[]{:S(2)}) collective-permute-start(bf16[16,2688]{1,0:T(8,128)(2,1)S(1)} %get-tuple-element.134), channel_id=1, source_target_pairs={{0,4},{1,5},{2,6},{3,7},{4,0},{5,1},{6,2},{7,3},{8,12},{9,13},{10,... | collective-permute-start | bytes 258056 | tf_op jit(solution)/shard_map/ppermute | solution.py:17
  95.0 1.6 %collective-permute-start.34 = (bf16[16,2688]{1,0:T(8,128)(2,1)S(1)}, bf16[16,2688]{1,0:T(8,128)(2,1)S(1)}, u32[]{:S(2)}, u32[]{:S(2)}) collective-permute-start(bf16[16,2688]{1,0:T(8,128)(2,1)S(1)} %get-tuple-element.135), channel_id=1, source_target_pairs={{0,6},{1,7},{2,4},{3,5},{4,2},{5,3},{6,0},{7,1},{8,14},{9,15},{10,... | collective-permute-start | bytes 258056 | tf_op jit(solution)/shard_map/ppermute | solution.py:17
  96.7 6.2 %collective-permute-done.32 = bf16[16,2688]{1,0:T(8,128)(2,1)S(1)} collective-permute-done((bf16[16,2688]{1,0:T(8,128)(2,1)S(1)}, bf16[16,2688]{1,0:T(8,128)(2,1)S(1)}, u32[]{:S(2)}, u32[]{:S(2)}) %collective-permute-start.32) | collective-permute-done | bytes 86048 | tf_op jit(solution)/shard_map/ppermute | solution.py:17
  104.7 2.0 %collective-permute-start.40 = (bf16[16,2048]{1,0:T(8,128)(2,1)S(1)}, bf16[16,2048]{1,0:T(8,128)(2,1)S(1)}, u32[]{:S(2)}, u32[]{:S(2)}) collective-permute-start(bf16[16,2048]{1,0:T(8,128)(2,1)S(1)} %bitcast.37), channel_id=1, source_target_pairs={{0,6},{1,7},{2,4},{3,5},{4,2},{5,3},{6,0},{7,1},{8,14},{9,15},{10,... | collective-permute-start | bytes 196616 | tf_op jit(solution)/shard_map/ppermute | solution.py:17
  106.7 2.4 %collective-permute-start.38 = (bf16[16,2048]{1,0:T(8,128)(2,1)S(1)}, bf16[16,2048]{1,0:T(8,128)(2,1)S(1)}, u32[]{:S(2)}, u32[]{:S(2)}) collective-permute-start(bf16[16,2048]{1,0:T(8,128)(2,1)S(1)} %bitcast.39), channel_id=1, source_target_pairs={{0,4},{1,5},{2,6},{3,7},{4,0},{5,1},{6,2},{7,3},{8,12},{9,13},{10,... | collective-permute-start | bytes 196616 | tf_op jit(solution)/shard_map/ppermute | solution.py:17
  109.1 2.7 %stage_head.1.refs_9_ = bf16[4,512,1024]{2,1,0:T(8,128)(2,1)S(1)} custom-call(s32[11]{0:T(128)S(1)} %concatenate.6.place_ref, bf16[2048,1024]{1,0:T(8,128)(2,1)} %w_ref.7, bf16[16,2048]{1,0:T(8,128)(2,1)S(1)} %bitcast.41), custom_call_target="tpu_custom_call" | custom-call | bytes 4194304 | tf_op jit(solution)/shard_map/stage_head/pallas_call | solution.py:68
  114.8 1.9 %head_out.1 = (f32[32,1024]{1,0:T(8,128)S(1)}, bf16[32,1024]{1,0:T(8,128)(2,1)S(1)}, bf16[32,1024]{1,0:T(8,128)(2,1)S(1)}, bf16[32,1024]{1,0:T(8,128)(2,1)S(1)}) custom-call(s32[11]{0:T(128)S(1)} %concatenate.6.place_ref, bf16[16,2048]{1,0:T(8,128)(2,1)S(1)} %bitcast.42, bf16[16,2048]{1,0:T(8,128)(2,1)S(1)} %collective-permute-done.35.refs_1_, ...), custom_call_target="tpu_custom_call" | custom-call | tf_op jit(solution)/shard_map/head_out/pallas_call | solution.py:68
  (139 shorter events, 39.6 us)
Async XLA Ops:
  0.6 9.0 %collective-permute-start.2 = (bf16[32,1024]{1,0:T(8,128)(2,1)}, bf16[32,1024]{1,0:T(8,128)(2,1)S(1)}, u32[]{:S(2)}, u32[]{:S(2)}) collective-permute-start(bf16[32,1024]{1,0:T(8,128)(2,1)} %hidden_ref.1), channel_id=1, source_target_pairs={{0,24},{8,16},{16,8},{24,0},{1,25},{9,17},{17,9},{25,1},{2,26},{10... | collective-permute-start | bytes 196616 | tf_op jit(solution)/shard_map/ppermute | solution.py:17
  4.6 5.0 %collective-permute-start = (bf16[32,1024]{1,0:T(8,128)(2,1)}, bf16[32,1024]{1,0:T(8,128)(2,1)S(1)}, u32[]{:S(2)}, u32[]{:S(2)}) collective-permute-start(bf16[32,1024]{1,0:T(8,128)(2,1)} %hidden_ref.1), channel_id=1, source_target_pairs={{0,8},{8,0},{16,24},{24,16},{1,9},{9,1},{17,25},{25,17},{2,10},{10... | collective-permute-start | bytes 196616 | tf_op jit(solution)/shard_map/ppermute | solution.py:17
  5.1 4.5 %collective-permute-start.1 = (bf16[32,1024]{1,0:T(8,128)(2,1)}, bf16[32,1024]{1,0:T(8,128)(2,1)S(1)}, u32[]{:S(2)}, u32[]{:S(2)}) collective-permute-start(bf16[32,1024]{1,0:T(8,128)(2,1)} %hidden_ref.1), channel_id=1, source_target_pairs={{0,16},{8,24},{16,0},{24,8},{1,17},{9,25},{17,1},{25,9},{2,18},{10... | collective-permute-start | bytes 196616 | tf_op jit(solution)/shard_map/ppermute | solution.py:17
  14.2 14.2 %collective-permute-start.5 = (bf16[528,128]{1,0:T(8,128)(2,1)S(1)}, bf16[528,128]{1,0:T(8,128)(2,1)S(1)}, u32[]{:S(2)}, u32[]{:S(2)}) collective-permute-start(bf16[528,128]{1,0:T(8,128)(2,1)S(1)} %get-tuple-element.86), channel_id=1, source_target_pairs={{0,4},{1,5},{2,6},{3,7},{4,0},{5,1},{6,2},{7,3},{8,12},{9,13},{10,... | collective-permute-start | bytes 405512 | tf_op jit(solution)/shard_map/ppermute | solution.py:17
  17.1 11.3 %collective-permute-start.6 = (bf16[528,128]{1,0:T(8,128)(2,1)S(1)}, bf16[528,128]{1,0:T(8,128)(2,1)S(1)}, u32[]{:S(2)}, u32[]{:S(2)}) collective-permute-start(bf16[528,128]{1,0:T(8,128)(2,1)S(1)} %get-tuple-element.87), channel_id=1, source_target_pairs={{0,6},{1,7},{2,4},{3,5},{4,2},{5,3},{6,0},{7,1},{8,14},{9,15},{10,... | collective-permute-start | bytes 405512 | tf_op jit(solution)/shard_map/ppermute | solution.py:17
  18.4 10.0 %collective-permute-start.4 = (bf16[528,128]{1,0:T(8,128)(2,1)S(1)}, bf16[528,128]{1,0:T(8,128)(2,1)S(1)}, u32[]{:S(2)}, u32[]{:S(2)}) collective-permute-start(bf16[528,128]{1,0:T(8,128)(2,1)S(1)} %get-tuple-element.85.earlier_ref), channel_id=1, source_target_pairs={{0,2},{1,3},{2,0},{3,1},{4,6},{5,7},{6,4},{7,5},{8,10},{9,11},{10,... | collective-permute-start | bytes 405512 | tf_op jit(solution)/shard_map/ppermute | solution.py:17
  32.0 9.8 %collective-permute-start.11 = (bf16[272,128]{1,0:T(8,128)(2,1)S(1)}, bf16[272,128]{1,0:T(8,128)(2,1)S(1)}, u32[]{:S(2)}, u32[]{:S(2)}) collective-permute-start(bf16[272,128]{1,0:T(8,128)(2,1)S(1)} %get-tuple-element.108), channel_id=1, source_target_pairs={{0,6},{1,7},{2,4},{3,5},{4,2},{5,3},{6,0},{7,1},{8,14},{9,15},{10,... | collective-permute-start | bytes 208904 | tf_op jit(solution)/shard_map/ppermute | solution.py:17
  35.6 7.2 %collective-permute-start.10 = (bf16[272,128]{1,0:T(8,128)(2,1)S(1)}, bf16[272,128]{1,0:T(8,128)(2,1)S(1)}, u32[]{:S(2)}, u32[]{:S(2)}) collective-permute-start(bf16[272,128]{1,0:T(8,128)(2,1)S(1)} %get-tuple-element.108), channel_id=1, source_target_pairs={{0,4},{1,5},{2,6},{3,7},{4,0},{5,1},{6,2},{7,3},{8,12},{9,13},{10,... | collective-permute-start | bytes 208904 | tf_op jit(solution)/shard_map/ppermute | solution.py:17
  36.3 6.6 %collective-permute-start.9 = (bf16[272,128]{1,0:T(8,128)(2,1)S(1)}, bf16[272,128]{1,0:T(8,128)(2,1)S(1)}, u32[]{:S(2)}, u32[]{:S(2)}) collective-permute-start(bf16[272,128]{1,0:T(8,128)(2,1)S(1)} %get-tuple-element.108), channel_id=1, source_target_pairs={{0,2},{1,3},{2,0},{3,1},{4,6},{5,7},{6,4},{7,5},{8,10},{9,11},{10,... | collective-permute-start | bytes 208904 | tf_op jit(solution)/shard_map/ppermute | solution.py:17
  36.8 10.8 %collective-permute-start.16 = (bf16[1024,128]{1,0:T(8,128)(2,1)S(1)}, bf16[1024,128]{1,0:T(8,128)(2,1)S(1)}, u32[]{:S(2)}, u32[]{:S(2)}) collective-permute-start(bf16[1024,128]{1,0:T(8,128)(2,1)S(1)} %get-tuple-element.117), channel_id=1, source_target_pairs={{0,2},{1,3},{2,0},{3,1},{4,6},{5,7},{6,4},{7,5},{8,10},{9,11},{10,... | collective-permute-start | bytes 786440 | tf_op jit(solution)/shard_map/ppermute | solution.py:17
  42.9 6.2 %collective-permute-start.12 = (bf16[272,128]{1,0:T(8,128)(2,1)S(1)}, bf16[272,128]{1,0:T(8,128)(2,1)S(1)}, u32[]{:S(2)}, u32[]{:S(2)}) collective-permute-start(bf16[272,128]{1,0:T(8,128)(2,1)S(1)} %fusion.11), channel_id=1, source_target_pairs={{0,8},{8,0},{16,24},{24,16},{1,9},{9,1},{17,25},{25,17},{2,10},{10... | collective-permute-start | bytes 208904 | tf_op jit(solution)/shard_map/ppermute | solution.py:17
  44.5 4.6 %collective-permute-start.13 = (bf16[272,128]{1,0:T(8,128)(2,1)S(1)}, bf16[272,128]{1,0:T(8,128)(2,1)S(1)}, u32[]{:S(2)}, u32[]{:S(2)}) collective-permute-start(bf16[272,128]{1,0:T(8,128)(2,1)S(1)} %fusion.11), channel_id=1, source_target_pairs={{0,16},{8,24},{16,0},{24,8},{1,17},{9,25},{17,1},{25,9},{2,18},{10... | collective-permute-start | bytes 208904 | tf_op jit(solution)/shard_map/ppermute | solution.py:17
  46.0 5.2 %collective-permute-start.14 = (bf16[272,128]{1,0:T(8,128)(2,1)S(1)}, bf16[272,128]{1,0:T(8,128)(2,1)S(1)}, u32[]{:S(2)}, u32[]{:S(2)}) collective-permute-start(bf16[272,128]{1,0:T(8,128)(2,1)S(1)} %fusion.11), channel_id=1, source_target_pairs={{0,24},{8,16},{16,8},{24,0},{1,25},{9,17},{17,9},{25,1},{2,26},{10... | collective-permute-start | bytes 208904 | tf_op jit(solution)/shard_map/ppermute | solution.py:17
  47.6 8.6 %collective-permute-start.17 = (bf16[512,128]{1,0:T(8,128)(2,1)S(1)}, bf16[512,128]{1,0:T(8,128)(2,1)S(1)}, u32[]{:S(2)}, u32[]{:S(2)}) collective-permute-start(bf16[512,128]{1,0:T(8,128)(2,1)S(1)} %slice.62), channel_id=1, source_target_pairs={{0,4},{1,5},{2,6},{3,7},{4,0},{5,1},{6,2},{7,3},{8,12},{9,13},{10,... | collective-permute-start | bytes 393224 | tf_op jit(solution)/shard_map/ppermute | solution.py:17
  57.0 12.9 %collective-permute-start.21 = (bf16[128,512]{1,0:T(8,128)(2,1)S(1)}, bf16[128,512]{1,0:T(8,128)(2,1)S(1)}, u32[]{:S(2)}, u32[]{:S(2)}) collective-permute-start(bf16[128,512]{1,0:T(8,128)(2,1)S(1)} %gate_rows.1.earlier_ref.refs_0_), channel_id=1, source_target_pairs={{0,4},{1,5},{2,6},{3,7},{4,0},{5,1},{6,2},{7,3},{8,12},{9,13},{10,... | collective-permute-start | bytes 393224 | tf_op jit(solution)/shard_map/ppermute | solution.py:17
  58.3 11.5 %collective-permute-start.22 = (bf16[128,512]{1,0:T(8,128)(2,1)S(1)}, bf16[128,512]{1,0:T(8,128)(2,1)S(1)}, u32[]{:S(2)}, u32[]{:S(2)}) collective-permute-start(bf16[128,512]{1,0:T(8,128)(2,1)S(1)} %gate_rows.1.earlier_ref.refs_0_), channel_id=1, source_target_pairs={{0,6},{1,7},{2,4},{3,5},{4,2},{5,3},{6,0},{7,1},{8,14},{9,15},{10,... | collective-permute-start | bytes 393224 | tf_op jit(solution)/shard_map/ppermute | solution.py:17
  60.3 10.2 %collective-permute-start.19 = (bf16[128,512]{1,0:T(8,128)(2,1)S(1)}, bf16[128,512]{1,0:T(8,128)(2,1)S(1)}, u32[]{:S(2)}, u32[]{:S(2)}) collective-permute-start(bf16[128,512]{1,0:T(8,128)(2,1)S(1)} %gate_rows.1.earlier_ref.refs_0_), channel_id=1, source_target_pairs={{0,2},{1,3},{2,0},{3,1},{4,6},{5,7},{6,4},{7,5},{8,10},{9,11},{10,... | collective-permute-start | bytes 393224 | tf_op jit(solution)/shard_map/ppermute | solution.py:17
  60.8 9.7 %collective-permute-start.18 = (bf16[128,512]{1,0:T(8,128)(2,1)S(1)}, bf16[128,512]{1,0:T(8,128)(2,1)S(1)}, u32[]{:S(2)}, u32[]{:S(2)}) collective-permute-start(bf16[128,512]{1,0:T(8,128)(2,1)S(1)} %gate_rows.1.earlier_ref.refs_0_), channel_id=1, source_target_pairs={{0,1},{1,0},{2,3},{3,2},{4,5},{5,4},{6,7},{7,6},{8,9},{9,8},{10,11... | collective-permute-start | bytes 393224 | tf_op jit(solution)/shard_map/ppermute | solution.py:17
  73.8 5.8 %collective-permute-start.27 = (bf16[32,1024]{1,0:T(8,128)(2,1)S(1)}, bf16[32,1024]{1,0:T(8,128)(2,1)S(1)}, u32[]{:S(2)}, u32[]{:S(2)}) collective-permute-start(bf16[32,1024]{1,0:T(8,128)(2,1)S(1)} %get-tuple-element.128), channel_id=1, source_target_pairs={{0,24},{8,16},{16,8},{24,0},{1,25},{9,17},{17,9},{25,1},{2,26},{10... | collective-permute-start | bytes 196616 | tf_op jit(solution)/shard_map/ppermute | solution.py:17
  75.1 4.5 %collective-permute-start.25 = (bf16[32,1024]{1,0:T(8,128)(2,1)S(1)}, bf16[32,1024]{1,0:T(8,128)(2,1)S(1)}, u32[]{:S(2)}, u32[]{:S(2)}) collective-permute-start(bf16[32,1024]{1,0:T(8,128)(2,1)S(1)} %get-tuple-element.126), channel_id=1, source_target_pairs={{0,8},{8,0},{16,24},{24,16},{1,9},{9,1},{17,25},{25,17},{2,10},{10... | collective-permute-start | bytes 196616 | tf_op jit(solution)/shard_map/ppermute | solution.py:17
  75.8 4.5 %collective-permute-start.26 = (bf16[32,1024]{1,0:T(8,128)(2,1)S(1)}, bf16[32,1024]{1,0:T(8,128)(2,1)S(1)}, u32[]{:S(2)}, u32[]{:S(2)}) collective-permute-start(bf16[32,1024]{1,0:T(8,128)(2,1)S(1)} %get-tuple-element.127), channel_id=1, source_target_pairs={{0,16},{8,24},{16,0},{24,8},{1,17},{9,25},{17,1},{25,9},{2,18},{10... | collective-permute-start | bytes 196616 | tf_op jit(solution)/shard_map/ppermute | solution.py:17
  80.3 5.2 %collective-permute-start.30 = (bf16[32,1024]{1,0:T(8,128)(2,1)S(1)}, bf16[32,1024]{1,0:T(8,128)(2,1)S(1)}, u32[]{:S(2)}, u32[]{:S(2)}) collective-permute-start(bf16[32,1024]{1,0:T(8,128)(2,1)S(1)} %add_convert_fusion.2.refs_0_), channel_id=1, source_target_pairs={{0,24},{8,16},{16,8},{24,0},{1,25},{9,17},{17,9},{25,1},{2,26},{10... | collective-permute-start | bytes 196616 | tf_op jit(solution)/shard_map/ppermute | solution.py:17
  81.7 4.4 %collective-permute-start.28 = (bf16[32,1024]{1,0:T(8,128)(2,1)S(1)}, bf16[32,1024]{1,0:T(8,128)(2,1)S(1)}, u32[]{:S(2)}, u32[]{:S(2)}) collective-permute-start(bf16[32,1024]{1,0:T(8,128)(2,1)S(1)} %add_convert_fusion.2.refs_0_), channel_id=1, source_target_pairs={{0,8},{8,0},{16,24},{24,16},{1,9},{9,1},{17,25},{25,17},{2,10},{10... | collective-permute-start | bytes 196616 | tf_op jit(solution)/shard_map/ppermute | solution.py:17
  91.7 11.2 %collective-permute-start.33 = (bf16[16,2688]{1,0:T(8,128)(2,1)S(1)}, bf16[16,2688]{1,0:T(8,128)(2,1)S(1)}, u32[]{:S(2)}, u32[]{:S(2)}) collective-permute-start(bf16[16,2688]{1,0:T(8,128)(2,1)S(1)} %get-tuple-element.134), channel_id=1, source_target_pairs={{0,4},{1,5},{2,6},{3,7},{4,0},{5,1},{6,2},{7,3},{8,12},{9,13},{10,... | collective-permute-start | bytes 258056 | tf_op jit(solution)/shard_map/ppermute | solution.py:17
  95.0 7.9 %collective-permute-start.34 = (bf16[16,2688]{1,0:T(8,128)(2,1)S(1)}, bf16[16,2688]{1,0:T(8,128)(2,1)S(1)}, u32[]{:S(2)}, u32[]{:S(2)}) collective-permute-start(bf16[16,2688]{1,0:T(8,128)(2,1)S(1)} %get-tuple-element.135), channel_id=1, source_target_pairs={{0,6},{1,7},{2,4},{3,5},{4,2},{5,3},{6,0},{7,1},{8,14},{9,15},{10,... | collective-permute-start | bytes 258056 | tf_op jit(solution)/shard_map/ppermute | solution.py:17
  96.6 6.3 %collective-permute-start.32 = (bf16[16,2688]{1,0:T(8,128)(2,1)S(1)}, bf16[16,2688]{1,0:T(8,128)(2,1)S(1)}, u32[]{:S(2)}, u32[]{:S(2)}) collective-permute-start(bf16[16,2688]{1,0:T(8,128)(2,1)S(1)} %get-tuple-element.133), channel_id=1, source_target_pairs={{0,2},{1,3},{2,0},{3,1},{4,6},{5,7},{6,4},{7,5},{8,10},{9,11},{10,... | collective-permute-start | bytes 258056 | tf_op jit(solution)/shard_map/ppermute | solution.py:17
  104.7 7.2 %collective-permute-start.40 = (bf16[16,2048]{1,0:T(8,128)(2,1)S(1)}, bf16[16,2048]{1,0:T(8,128)(2,1)S(1)}, u32[]{:S(2)}, u32[]{:S(2)}) collective-permute-start(bf16[16,2048]{1,0:T(8,128)(2,1)S(1)} %bitcast.37), channel_id=1, source_target_pairs={{0,6},{1,7},{2,4},{3,5},{4,2},{5,3},{6,0},{7,1},{8,14},{9,15},{10,... | collective-permute-start | bytes 196616 | tf_op jit(solution)/shard_map/ppermute | solution.py:17
  106.7 5.8 %collective-permute-start.36 = (bf16[16,2048]{1,0:T(8,128)(2,1)S(1)}, bf16[16,2048]{1,0:T(8,128)(2,1)S(1)}, u32[]{:S(2)}, u32[]{:S(2)}) collective-permute-start(bf16[16,2048]{1,0:T(8,128)(2,1)S(1)} %bitcast.38), channel_id=1, source_target_pairs={{0,2},{1,3},{2,0},{3,1},{4,6},{5,7},{6,4},{7,5},{8,10},{9,11},{10,... | collective-permute-start | bytes 196616 | tf_op jit(solution)/shard_map/ppermute | solution.py:17
  106.7 6.8 %collective-permute-start.38 = (bf16[16,2048]{1,0:T(8,128)(2,1)S(1)}, bf16[16,2048]{1,0:T(8,128)(2,1)S(1)}, u32[]{:S(2)}, u32[]{:S(2)}) collective-permute-start(bf16[16,2048]{1,0:T(8,128)(2,1)S(1)} %bitcast.39), channel_id=1, source_target_pairs={{0,4},{1,5},{2,6},{3,7},{4,0},{5,1},{6,2},{7,3},{8,12},{9,13},{10,... | collective-permute-start | bytes 196616 | tf_op jit(solution)/shard_map/ppermute | solution.py:17
  109.1 4.4 %collective-permute-start.35 = (bf16[16,2048]{1,0:T(8,128)(2,1)S(1)}, bf16[16,2048]{1,0:T(8,128)(2,1)S(1)}, u32[]{:S(2)}, u32[]{:S(2)}) collective-permute-start(bf16[16,2048]{1,0:T(8,128)(2,1)S(1)} %bitcast.40), channel_id=1, source_target_pairs={{0,1},{1,0},{2,3},{3,2},{4,5},{5,4},{6,7},{7,6},{8,9},{9,8},{10,11... | collective-permute-start | bytes 196616 | tf_op jit(solution)/shard_map/ppermute | solution.py:17
  116.7 5.8 %collective-permute-start.44 = (bf16[32,1024]{1,0:T(8,128)(2,1)S(1)}, bf16[32,1024]{1,0:T(8,128)(2,1)S(1)}, u32[]{:S(2)}, u32[]{:S(2)}) collective-permute-start(bf16[32,1024]{1,0:T(8,128)(2,1)S(1)} %get-tuple-element.141), channel_id=1, source_target_pairs={{0,24},{8,16},{16,8},{24,0},{1,25},{9,17},{17,9},{25,1},{2,26},{10... | collective-permute-start | bytes 196616 | tf_op jit(solution)/shard_map/ppermute | solution.py:17
  117.6 4.9 %collective-permute-start.42 = (bf16[32,1024]{1,0:T(8,128)(2,1)S(1)}, bf16[32,1024]{1,0:T(8,128)(2,1)S(1)}, u32[]{:S(2)}, u32[]{:S(2)}) collective-permute-start(bf16[32,1024]{1,0:T(8,128)(2,1)S(1)} %get-tuple-element.139), channel_id=1, source_target_pairs={{0,8},{8,0},{16,24},{24,16},{1,9},{9,1},{17,25},{25,17},{2,10},{10... | collective-permute-start | bytes 196616 | tf_op jit(solution)/shard_map/ppermute | solution.py:17
  (27 other events, 177.8 us)

commit v6 on v5

--- a/solution.py
+++ b/solution.py
@@ -520,9 +520,10 @@
         w_ref, own_ref = refs[count : count + 2]
         wire_refs = refs[count + 2 : -1]
         total = refs[-1]
-        for j in range(count):
-            term = dot(piece_refs[j][...], w_ref[j])
-            total[...] = term if j == 0 else total[...] + term
+        value = dot(piece_refs[0][...], w_ref[0])
+        for j in range(1, count):
+            value = value + dot(piece_refs[j][...], w_ref[j])
+        total[...] = value
         me = place_ref[2 * chips]
         for k in range(parts):
             start = pl.multiple_of((me ^ k) * rows, rows)
@@ -578,10 +579,9 @@
         give_ref[:, columns:] = squares[:half]
         keep_ref[:, columns:] = squares[half:]
         gained = (value * gain_ref[...]).astype(BF16)
-        for j in range(steps):
-            out = dot(gained, w_ref[:, j * block : (j + 1) * block]).astype(BF16)
-            give_ref[:, j * block : (j + 1) * block] = out[:half]
-            keep_ref[:, j * block : (j + 1) * block] = out[half:]
+        out = dot(gained, w_ref[...]).astype(BF16)
+        give_ref[:, :columns] = out[:half]
+        keep_ref[:, :columns] = out[half:]
 
     return call(
         kernel,
@@ -611,10 +611,11 @@
             start = pl.multiple_of((mine ^ j) * slots, slots)
             stacked[pl.ds(start, slots), :] = piece_refs[j][...]
         chosen = held_by(assign_ref)
-        for j in range(steps):
-            taken = dot(chosen, stacked[:, j * block : (j + 1) * block]).astype(BF16)
-            term = dot(taken, w_ref[j])
-            total[...] = term if j == 0 else total[...] + term
+        taken = dot(chosen, stacked[...]).astype(BF16)
+        value = dot(taken[:, :block], w_ref[0])
+        for j in range(1, steps):
+            value = value + dot(taken[:, j * block : (j + 1) * block], w_ref[j])
+        total[...] = value
         me = place_ref[2 * chips]
         for k in range(parts):
             start = pl.multiple_of((me ^ k) * rows, rows)

time: 124 us -> 124 us (level)
  no operation moved by 1% of the time
where the time goes in v6:
time: 124 us
  starting transfers between devices  46.3 us (37%)
  Pallas kernels  38 us (31%)
  waiting for transfers between devices  31.4 us (25%)
  local copies, waits for them, and re-layouts  4.07 us (3%)
  other arithmetic  1.66 us (1%)
    ppermute x45, starting transfers between devices, swap(): return lax.ppermute(value, axis, [(i, i ^ bits) for i in range(size)])  46.3 us
    pallas_call x15, Pallas kernels, call(): pl.pallas_call(kernel, grid_spec=pltpu.PrefetchScalarGridSpec(num_scalar_...  32.5 us
    ppermute x45, waiting for transfers between devices, swap(): return lax.ppermute(value, axis, [(i, i ^ bits) for i in range(size)])  31.4 us
    pallas_call x1, Pallas kernels, scan(): pl.pallas_call(kernel, grid_spec=pltpu.PrefetchScalarGridSpec(num_scalar_...  3.57 us
  transfers between devices with their start and end apart: 45, of which 25 were waited for; matrix products, arithmetic and copies ran while one was open for 3% of the time, Pallas kernels for 23%

profile of v6, /device:TPU:0, one launch (start us, length us, event | category | flops | bytes accessed | tf_op | source)
XLA Modules:
  0.0 123.5 jit_solution(7784763662503382186)
XLA Ops:
  0.6 4.0 %collective-permute-start.2 = (bf16[32,1024]{1,0:T(8,128)(2,1)}, bf16[32,1024]{1,0:T(8,128)(2,1)S(1)}, u32[]{:S(2)}, u32[]{:S(2)}) collective-permute-start(bf16[32,1024]{1,0:T(8,128)(2,1)} %hidden_ref.1), channel_id=1, source_target_pairs={{0,24},{8,16},{16,8},{24,0},{1,25},{9,17},{17,9},{25,1},{2,26},{10... | collective-permute-start | bytes 196616 | tf_op jit(solution)/shard_map/ppermute | solution.py:17
  5.3 4.0 %stage_first.1 = (bf16[8,512,1024]{2,1,0:T(8,128)(2,1)S(1)}, bf16[32,1024]{1,0:T(8,128)(2,1)S(1)}, f32[1,1024]{1,0:T(1,128)S(1)}) custom-call(s32[11]{0:T(128)S(1)} %concatenate.6.place_ref, bf16[2,4096,1024]{2,1,0:T(8,128)(2,1)} %w_ref.5, bf16[32,1024]{1,0:T(8,128)(2,1)} %hidden_ref.1, f32[1,1024]{1,0:T(1,128)} %bitcast.57), custom_call_target="tpu_custom_call" | custom-call | bytes 8388608 | tf_op jit(solution)/shard_map/stage_first/pallas_call | solution.py:68
  9.6 2.0 %project_first.1 = (bf16[4,528,128]{2,1,0:T(8,128)(2,1)S(1)}, bf16[1024,128]{1,0:T(8,128)(2,1)S(1)}, f32[16,128]{1,0:T(8,128)S(1)}) custom-call(s32[11]{0:T(128)S(1)} %concatenate.6.place_ref, bf16[32,1024]{1,0:T(8,128)(2,1)S(1)} %get-tuple-element.76.refs_0_, bf16[32,1024]{1,0:T(8,128)(2,1)S(1)} %collective-permute-done.refs_1_, ...), custom_call_target="tpu_custom_call" | custom-call | tf_op jit(solution)/shard_map/project_first/pallas_call | solution.py:68
  11.7 1.8 %project_keep.1 = bf16[4,528,128]{2,1,0:T(8,128)(2,1)S(1)} custom-call(s32[11]{0:T(128)S(1)} %concatenate.6.place_ref, bf16[8,512,1024]{2,1,0:T(8,128)(2,1)S(1)} %get-tuple-element.75.refs_5_.w_ref, bf16[1024,128]{1,0:T(8,128)(2,1)S(1)} %get-tuple-element.81.gained_ref, f32[16,128]{1,0:T(8,128)S(1)} %get-tuple-element.82.squares_ref), custom_call_target="tpu_custom_call" | custom-call | tf_op jit(solution)/shard_map/project_keep/pallas_call | solution.py:68
  14.2 2.8 %collective-permute-start.5 = (bf16[528,128]{1,0:T(8,128)(2,1)S(1)}, bf16[528,128]{1,0:T(8,128)(2,1)S(1)}, u32[]{:S(2)}, u32[]{:S(2)}) collective-permute-start(bf16[528,128]{1,0:T(8,128)(2,1)S(1)} %get-tuple-element.86), channel_id=1, source_target_pairs={{0,4},{1,5},{2,6},{3,7},{4,0},{5,1},{6,2},{7,3},{8,12},{9,13},{10,... | collective-permute-start | bytes 405512 | tf_op jit(solution)/shard_map/ppermute | solution.py:17
  19.6 5.3 %project_gate.1 = (bf16[4,512,128]{2,1,0:T(8,128)(2,1)S(1)}, bf16[4,512,128]{2,1,0:T(8,128)(2,1)S(1)}, bf16[3,512,128]{2,1,0:T(8,128)(2,1)S(1)}, bf16[544,512]{1,0:T(8,128)(2,1)S(1)}) custom-call(s32[11]{0:T(128)S(1)} %concatenate.6.place_ref, bf16[2,4096,1024]{2,1,0:T(8,128)(2,1)} %w_ref.5, bf16[1024,128]{1,0:T(8,128)(2,1)S(1)} %get-tuple-element.81.gained_ref, ...), custom_call_target="tpu_custom_call" | custom-call | bytes 8388608 | tf_op jit(solution)/shard_map/project_gate/pallas_call | solution.py:68
  24.9 3.5 %collective-permute-done.4.refs_0_ = bf16[528,128]{1,0:T(8,128)(2,1)S(1)} collective-permute-done((bf16[528,128]{1,0:T(8,128)(2,1)S(1)}, bf16[528,128]{1,0:T(8,128)(2,1)S(1)}, u32[]{:S(2)}, u32[]{:S(2)}) %collective-permute-start.4) | collective-permute-done | bytes 135200 | tf_op jit(solution)/shard_map/ppermute | solution.py:17
  32.0 3.6 %collective-permute-start.11 = (bf16[272,128]{1,0:T(8,128)(2,1)S(1)}, bf16[272,128]{1,0:T(8,128)(2,1)S(1)}, u32[]{:S(2)}, u32[]{:S(2)}) collective-permute-start(bf16[272,128]{1,0:T(8,128)(2,1)S(1)} %get-tuple-element.108), channel_id=1, source_target_pairs={{0,6},{1,7},{2,4},{3,5},{4,2},{5,3},{6,0},{7,1},{8,14},{9,15},{10,... | collective-permute-start | bytes 208904 | tf_op jit(solution)/shard_map/ppermute | solution.py:17
  36.8 1.5 %collective-permute-start.16 = (bf16[1024,128]{1,0:T(8,128)(2,1)S(1)}, bf16[1024,128]{1,0:T(8,128)(2,1)S(1)}, u32[]{:S(2)}, u32[]{:S(2)}) collective-permute-start(bf16[1024,128]{1,0:T(8,128)(2,1)S(1)} %get-tuple-element.117), channel_id=1, source_target_pairs={{0,2},{1,3},{2,0},{3,1},{4,6},{5,7},{6,4},{7,5},{8,10},{9,11},{10,... | collective-permute-start | bytes 786440 | tf_op jit(solution)/shard_map/ppermute | solution.py:17
  38.3 3.5 %ready_state.1.state_ref = f32[16,512,128]{2,1,0:T(8,128)S(1)} custom-call(s32[11]{0:T(128)S(1)} %concatenate.6.place_ref, bf16[512,16,128]{2,1,0:T(8,128)(2,1)} %state_ref.1, f32[8,128]{1,0:T(8,128)S(1)} %broadcast_in_dim.66.refs_5_.alive_ref, f32[272,128]{1,0:T(8,128)S(1)} %get-tuple-element.107.earlier_ref), custom_call_target="tpu_custom_call" | custom-call | bytes 6291456 | tf_op jit(solution)/shard_map/ready_state/pallas_call | solution.py:68
  42.9 1.6 %collective-permute-start.12 = (bf16[272,128]{1,0:T(8,128)(2,1)S(1)}, bf16[272,128]{1,0:T(8,128)(2,1)S(1)}, u32[]{:S(2)}, u32[]{:S(2)}) collective-permute-start(bf16[272,128]{1,0:T(8,128)(2,1)S(1)} %fusion.11), channel_id=1, source_target_pairs={{0,8},{8,0},{16,24},{24,16},{1,9},{9,1},{17,25},{25,17},{2,10},{10... | collective-permute-start | bytes 208904 | tf_op jit(solution)/shard_map/ppermute | solution.py:17
  44.5 1.5 %collective-permute-start.13 = (bf16[272,128]{1,0:T(8,128)(2,1)S(1)}, bf16[272,128]{1,0:T(8,128)(2,1)S(1)}, u32[]{:S(2)}, u32[]{:S(2)}) collective-permute-start(bf16[272,128]{1,0:T(8,128)(2,1)S(1)} %fusion.11), channel_id=1, source_target_pairs={{0,16},{8,24},{16,0},{24,8},{1,17},{9,25},{17,1},{25,9},{2,18},{10... | collective-permute-start | bytes 208904 | tf_op jit(solution)/shard_map/ppermute | solution.py:17
  47.6 1.4 %collective-permute-start.17 = (bf16[512,128]{1,0:T(8,128)(2,1)S(1)}, bf16[512,128]{1,0:T(8,128)(2,1)S(1)}, u32[]{:S(2)}, u32[]{:S(2)}) collective-permute-start(bf16[512,128]{1,0:T(8,128)(2,1)S(1)} %slice.62), channel_id=1, source_target_pairs={{0,4},{1,5},{2,6},{3,7},{4,0},{5,1},{6,2},{7,3},{8,12},{9,13},{10,... | collective-permute-start | bytes 393224 | tf_op jit(solution)/shard_map/ppermute | solution.py:17
  49.1 2.1 %collective-permute-done.14 = bf16[272,128]{1,0:T(8,128)(2,1)S(1)} collective-permute-done((bf16[272,128]{1,0:T(8,128)(2,1)S(1)}, bf16[272,128]{1,0:T(8,128)(2,1)S(1)}, u32[]{:S(2)}, u32[]{:S(2)}) %collective-permute-start.14) | collective-permute-done | bytes 69664 | tf_op jit(solution)/shard_map/ppermute | solution.py:17
  52.6 3.6 %scan.1 = (bf16[512,16,128]{2,1,0:T(8,128)(2,1)S(1)}, f32[512,128]{1,0:T(8,128)S(1)}) custom-call(s32[11]{0:T(128)S(1)} %concatenate.6.place_ref, bf16[272,128]{1,0:T(8,128)(2,1)S(1)} %add_convert_fusion.mine_ref, bf16[272,128]{1,0:T(8,128)(2,1)S(1)} %collective-permute-done.15.other_ref, bf16[512,512]{1,0:T(8,128)(2,1)S(1)} %bitcast.36, ...), custom_call_target="tpu_custom_call" | custom-call | bytes 1 | tf_op jit(solution)/shard_map/scan/pallas_call | solution.py:434
  58.3 2.0 %collective-permute-start.22 = (bf16[128,512]{1,0:T(8,128)(2,1)S(1)}, bf16[128,512]{1,0:T(8,128)(2,1)S(1)}, u32[]{:S(2)}, u32[]{:S(2)}) collective-permute-start(bf16[128,512]{1,0:T(8,128)(2,1)S(1)} %gate_rows.1.earlier_ref.refs_0_), channel_id=1, source_target_pairs={{0,6},{1,7},{2,4},{3,5},{4,2},{5,3},{6,0},{7,1},{8,14},{9,15},{10,... | collective-permute-start | bytes 393224 | tf_op jit(solution)/shard_map/ppermute | solution.py:17
  60.8 1.9 %store_state.1 = bf16[512,16,128]{2,1,0:T(8,128)(2,1)} custom-call(s32[11]{0:T(128)S(1)} %concatenate.6.place_ref, bf16[512,16,128]{2,1,0:T(8,128)(2,1)S(1)} %get-tuple-element.121.state_ref, bf16[128,512]{1,0:T(8,128)(2,1)S(1)} %gate_rows.1.earlier_ref.refs_0_), custom_call_target="tpu_custom_call" | custom-call | bytes 2097152 | tf_op jit(solution)/shard_map/store_state/pallas_call | solution.py:472
  62.7 4.0 %stage_mix.1.refs_8_ = bf16[8,512,1024]{2,1,0:T(8,128)(2,1)S(1)} custom-call(s32[11]{0:T(128)S(1)} %concatenate.6.place_ref, bf16[4096,1024]{1,0:T(8,128)(2,1)} %w_ref.6, bf16[128,512]{1,0:T(8,128)(2,1)S(1)} %gate_rows.1.earlier_ref.refs_0_), custom_call_target="tpu_custom_call" | custom-call | bytes 8388608 | tf_op jit(solution)/shard_map/stage_mix/pallas_call | solution.py:68
  67.8 2.0 %collective-permute-done.21.refs_4_ = bf16[128,512]{1,0:T(8,128)(2,1)S(1)} collective-permute-done((bf16[128,512]{1,0:T(8,128)(2,1)S(1)}, bf16[128,512]{1,0:T(8,128)(2,1)S(1)}, u32[]{:S(2)}, u32[]{:S(2)}) %collective-permute-start.21) | collective-permute-done | bytes 131104 | tf_op jit(solution)/shard_map/ppermute | solution.py:17
  71.9 1.8 %mix_out.1 = (f32[32,1024]{1,0:T(8,128)S(1)}, bf16[32,1024]{1,0:T(8,128)(2,1)S(1)}, bf16[32,1024]{1,0:T(8,128)(2,1)S(1)}, bf16[32,1024]{1,0:T(8,128)(2,1)S(1)}) custom-call(s32[11]{0:T(128)S(1)} %concatenate.6.place_ref, bf16[128,512]{1,0:T(8,128)(2,1)S(1)} %gate_rows.1.earlier_ref.refs_0_, bf16[128,512]{1,0:T(8,128)(2,1)S(1)} %collective-permute-done.18.refs_1_, ...), custom_call_target="tpu_custom_call" | custom-call | tf_op jit(solution)/shard_map/mix_out/pallas_call | solution.py:68
  75.8 1.5 %collective-permute-start.26 = (bf16[32,1024]{1,0:T(8,128)(2,1)S(1)}, bf16[32,1024]{1,0:T(8,128)(2,1)S(1)}, u32[]{:S(2)}, u32[]{:S(2)}) collective-permute-start(bf16[32,1024]{1,0:T(8,128)(2,1)S(1)} %get-tuple-element.127), channel_id=1, source_target_pairs={{0,16},{8,24},{16,0},{24,8},{1,17},{9,25},{17,1},{25,9},{2,18},{10... | collective-permute-start | bytes 196616 | tf_op jit(solution)/shard_map/ppermute | solution.py:17
  77.3 2.3 %collective-permute-done.27 = bf16[32,1024]{1,0:T(8,128)(2,1)S(1)} collective-permute-done((bf16[32,1024]{1,0:T(8,128)(2,1)S(1)}, bf16[32,1024]{1,0:T(8,128)(2,1)S(1)}, u32[]{:S(2)}, u32[]{:S(2)}) %collective-permute-start.27) | collective-permute-done | bytes 65568 | tf_op jit(solution)/shard_map/ppermute | solution.py:17
  81.7 1.5 %collective-permute-start.28 = (bf16[32,1024]{1,0:T(8,128)(2,1)S(1)}, bf16[32,1024]{1,0:T(8,128)(2,1)S(1)}, u32[]{:S(2)}, u32[]{:S(2)}) collective-permute-start(bf16[32,1024]{1,0:T(8,128)(2,1)S(1)} %add_convert_fusion.2.refs_0_), channel_id=1, source_target_pairs={{0,8},{8,0},{16,24},{24,16},{1,9},{9,1},{17,25},{25,17},{2,10},{10... | collective-permute-start | bytes 196616 | tf_op jit(solution)/shard_map/ppermute | solution.py:17
  83.9 1.7 %collective-permute-done.30.refs_3_ = bf16[32,1024]{1,0:T(8,128)(2,1)S(1)} collective-permute-done((bf16[32,1024]{1,0:T(8,128)(2,1)S(1)}, bf16[32,1024]{1,0:T(8,128)(2,1)S(1)}, u32[]{:S(2)}, u32[]{:S(2)}) %collective-permute-start.30) | collective-permute-done | bytes 65568 | tf_op jit(solution)/shard_map/ppermute | solution.py:17
  87.4 1.9 %query.1 = (bf16[64,2688]{1,0:T(8,128)(2,1)S(1)}, bf16[64,2688]{1,0:T(8,128)(2,1)S(1)}) custom-call(s32[11]{0:T(128)S(1)} %concatenate.6.place_ref, bf16[32,1024]{1,0:T(8,128)(2,1)S(1)} %add_convert_fusion.2.refs_0_, bf16[32,1024]{1,0:T(8,128)(2,1)S(1)} %collective-permute-done.28.refs_1_, bf16[32,1024]{1,0:T(8,128)(2,1)S(1)} %collective-permute-done.29.refs_2_, ...), custom_call_target="tpu_custom_call" | custom-call | tf_op jit(solution)/shard_map/query/pallas_call | solution.py:68
  91.7 3.3 %collective-permute-start.33 = (bf16[16,2688]{1,0:T(8,128)(2,1)S(1)}, bf16[16,2688]{1,0:T(8,128)(2,1)S(1)}, u32[]{:S(2)}, u32[]{:S(2)}) collective-permute-start(bf16[16,2688]{1,0:T(8,128)(2,1)S(1)} %get-tuple-element.134), channel_id=1, source_target_pairs={{0,4},{1,5},{2,6},{3,7},{4,0},{5,1},{6,2},{7,3},{8,12},{9,13},{10,... | collective-permute-start | bytes 258056 | tf_op jit(solution)/shard_map/ppermute | solution.py:17
  95.0 1.6 %collective-permute-start.34 = (bf16[16,2688]{1,0:T(8,128)(2,1)S(1)}, bf16[16,2688]{1,0:T(8,128)(2,1)S(1)}, u32[]{:S(2)}, u32[]{:S(2)}) collective-permute-start(bf16[16,2688]{1,0:T(8,128)(2,1)S(1)} %get-tuple-element.135), channel_id=1, source_target_pairs={{0,6},{1,7},{2,4},{3,5},{4,2},{5,3},{6,0},{7,1},{8,14},{9,15},{10,... | collective-permute-start | bytes 258056 | tf_op jit(solution)/shard_map/ppermute | solution.py:17
  96.7 6.2 %collective-permute-done.32 = bf16[16,2688]{1,0:T(8,128)(2,1)S(1)} collective-permute-done((bf16[16,2688]{1,0:T(8,128)(2,1)S(1)}, bf16[16,2688]{1,0:T(8,128)(2,1)S(1)}, u32[]{:S(2)}, u32[]{:S(2)}) %collective-permute-start.32) | collective-permute-done | bytes 86048 | tf_op jit(solution)/shard_map/ppermute | solution.py:17
  104.7 2.0 %collective-permute-start.40 = (bf16[16,2048]{1,0:T(8,128)(2,1)S(1)}, bf16[16,2048]{1,0:T(8,128)(2,1)S(1)}, u32[]{:S(2)}, u32[]{:S(2)}) collective-permute-start(bf16[16,2048]{1,0:T(8,128)(2,1)S(1)} %bitcast.37), channel_id=1, source_target_pairs={{0,6},{1,7},{2,4},{3,5},{4,2},{5,3},{6,0},{7,1},{8,14},{9,15},{10,... | collective-permute-start | bytes 196616 | tf_op jit(solution)/shard_map/ppermute | solution.py:17
  106.7 2.4 %collective-permute-start.38 = (bf16[16,2048]{1,0:T(8,128)(2,1)S(1)}, bf16[16,2048]{1,0:T(8,128)(2,1)S(1)}, u32[]{:S(2)}, u32[]{:S(2)}) collective-permute-start(bf16[16,2048]{1,0:T(8,128)(2,1)S(1)} %bitcast.39), channel_id=1, source_target_pairs={{0,4},{1,5},{2,6},{3,7},{4,0},{5,1},{6,2},{7,3},{8,12},{9,13},{10,... | collective-permute-start | bytes 196616 | tf_op jit(solution)/shard_map/ppermute | solution.py:17
  109.1 2.7 %stage_head.1.refs_9_ = bf16[4,512,1024]{2,1,0:T(8,128)(2,1)S(1)} custom-call(s32[11]{0:T(128)S(1)} %concatenate.6.place_ref, bf16[2048,1024]{1,0:T(8,128)(2,1)} %w_ref.7, bf16[16,2048]{1,0:T(8,128)(2,1)S(1)} %bitcast.41), custom_call_target="tpu_custom_call" | custom-call | bytes 4194304 | tf_op jit(solution)/shard_map/stage_head/pallas_call | solution.py:68
  114.8 1.5 %head_out.1 = (f32[32,1024]{1,0:T(8,128)S(1)}, bf16[32,1024]{1,0:T(8,128)(2,1)S(1)}, bf16[32,1024]{1,0:T(8,128)(2,1)S(1)}, bf16[32,1024]{1,0:T(8,128)(2,1)S(1)}) custom-call(s32[11]{0:T(128)S(1)} %concatenate.6.place_ref, bf16[16,2048]{1,0:T(8,128)(2,1)S(1)} %bitcast.42, bf16[16,2048]{1,0:T(8,128)(2,1)S(1)} %collective-permute-done.35.refs_1_, ...), custom_call_target="tpu_custom_call" | custom-call | tf_op jit(solution)/shard_map/head_out/pallas_call | solution.py:68
  (139 shorter events, 39.6 us)
Async XLA Ops:
  0.6 9.0 %collective-permute-start.2 = (bf16[32,1024]{1,0:T(8,128)(2,1)}, bf16[32,1024]{1,0:T(8,128)(2,1)S(1)}, u32[]{:S(2)}, u32[]{:S(2)}) collective-permute-start(bf16[32,1024]{1,0:T(8,128)(2,1)} %hidden_ref.1), channel_id=1, source_target_pairs={{0,24},{8,16},{16,8},{24,0},{1,25},{9,17},{17,9},{25,1},{2,26},{10... | collective-permute-start | bytes 196616 | tf_op jit(solution)/shard_map/ppermute | solution.py:17
  4.6 5.0 %collective-permute-start = (bf16[32,1024]{1,0:T(8,128)(2,1)}, bf16[32,1024]{1,0:T(8,128)(2,1)S(1)}, u32[]{:S(2)}, u32[]{:S(2)}) collective-permute-start(bf16[32,1024]{1,0:T(8,128)(2,1)} %hidden_ref.1), channel_id=1, source_target_pairs={{0,8},{8,0},{16,24},{24,16},{1,9},{9,1},{17,25},{25,17},{2,10},{10... | collective-permute-start | bytes 196616 | tf_op jit(solution)/shard_map/ppermute | solution.py:17
  5.1 4.5 %collective-permute-start.1 = (bf16[32,1024]{1,0:T(8,128)(2,1)}, bf16[32,1024]{1,0:T(8,128)(2,1)S(1)}, u32[]{:S(2)}, u32[]{:S(2)}) collective-permute-start(bf16[32,1024]{1,0:T(8,128)(2,1)} %hidden_ref.1), channel_id=1, source_target_pairs={{0,16},{8,24},{16,0},{24,8},{1,17},{9,25},{17,1},{25,9},{2,18},{10... | collective-permute-start | bytes 196616 | tf_op jit(solution)/shard_map/ppermute | solution.py:17
  14.2 14.2 %collective-permute-start.5 = (bf16[528,128]{1,0:T(8,128)(2,1)S(1)}, bf16[528,128]{1,0:T(8,128)(2,1)S(1)}, u32[]{:S(2)}, u32[]{:S(2)}) collective-permute-start(bf16[528,128]{1,0:T(8,128)(2,1)S(1)} %get-tuple-element.86), channel_id=1, source_target_pairs={{0,4},{1,5},{2,6},{3,7},{4,0},{5,1},{6,2},{7,3},{8,12},{9,13},{10,... | collective-permute-start | bytes 405512 | tf_op jit(solution)/shard_map/ppermute | solution.py:17
  17.1 11.3 %collective-permute-start.6 = (bf16[528,128]{1,0:T(8,128)(2,1)S(1)}, bf16[528,128]{1,0:T(8,128)(2,1)S(1)}, u32[]{:S(2)}, u32[]{:S(2)}) collective-permute-start(bf16[528,128]{1,0:T(8,128)(2,1)S(1)} %get-tuple-element.87), channel_id=1, source_target_pairs={{0,6},{1,7},{2,4},{3,5},{4,2},{5,3},{6,0},{7,1},{8,14},{9,15},{10,... | collective-permute-start | bytes 405512 | tf_op jit(solution)/shard_map/ppermute | solution.py:17
  18.4 10.0 %collective-permute-start.4 = (bf16[528,128]{1,0:T(8,128)(2,1)S(1)}, bf16[528,128]{1,0:T(8,128)(2,1)S(1)}, u32[]{:S(2)}, u32[]{:S(2)}) collective-permute-start(bf16[528,128]{1,0:T(8,128)(2,1)S(1)} %get-tuple-element.85.earlier_ref), channel_id=1, source_target_pairs={{0,2},{1,3},{2,0},{3,1},{4,6},{5,7},{6,4},{7,5},{8,10},{9,11},{10,... | collective-permute-start | bytes 405512 | tf_op jit(solution)/shard_map/ppermute | solution.py:17
  32.0 9.8 %collective-permute-start.11 = (bf16[272,128]{1,0:T(8,128)(2,1)S(1)}, bf16[272,128]{1,0:T(8,128)(2,1)S(1)}, u32[]{:S(2)}, u32[]{:S(2)}) collective-permute-start(bf16[272,128]{1,0:T(8,128)(2,1)S(1)} %get-tuple-element.108), channel_id=1, source_target_pairs={{0,6},{1,7},{2,4},{3,5},{4,2},{5,3},{6,0},{7,1},{8,14},{9,15},{10,... | collective-permute-start | bytes 208904 | tf_op jit(solution)/shard_map/ppermute | solution.py:17
  35.6 7.2 %collective-permute-start.10 = (bf16[272,128]{1,0:T(8,128)(2,1)S(1)}, bf16[272,128]{1,0:T(8,128)(2,1)S(1)}, u32[]{:S(2)}, u32[]{:S(2)}) collective-permute-start(bf16[272,128]{1,0:T(8,128)(2,1)S(1)} %get-tuple-element.108), channel_id=1, source_target_pairs={{0,4},{1,5},{2,6},{3,7},{4,0},{5,1},{6,2},{7,3},{8,12},{9,13},{10,... | collective-permute-start | bytes 208904 | tf_op jit(solution)/shard_map/ppermute | solution.py:17
  36.3 6.6 %collective-permute-start.9 = (bf16[272,128]{1,0:T(8,128)(2,1)S(1)}, bf16[272,128]{1,0:T(8,128)(2,1)S(1)}, u32[]{:S(2)}, u32[]{:S(2)}) collective-permute-start(bf16[272,128]{1,0:T(8,128)(2,1)S(1)} %get-tuple-element.108), channel_id=1, source_target_pairs={{0,2},{1,3},{2,0},{3,1},{4,6},{5,7},{6,4},{7,5},{8,10},{9,11},{10,... | collective-permute-start | bytes 208904 | tf_op jit(solution)/shard_map/ppermute | solution.py:17
  36.8 10.8 %collective-permute-start.16 = (bf16[1024,128]{1,0:T(8,128)(2,1)S(1)}, bf16[1024,128]{1,0:T(8,128)(2,1)S(1)}, u32[]{:S(2)}, u32[]{:S(2)}) collective-permute-start(bf16[1024,128]{1,0:T(8,128)(2,1)S(1)} %get-tuple-element.117), channel_id=1, source_target_pairs={{0,2},{1,3},{2,0},{3,1},{4,6},{5,7},{6,4},{7,5},{8,10},{9,11},{10,... | collective-permute-start | bytes 786440 | tf_op jit(solution)/shard_map/ppermute | solution.py:17
  42.9 6.2 %collective-permute-start.12 = (bf16[272,128]{1,0:T(8,128)(2,1)S(1)}, bf16[272,128]{1,0:T(8,128)(2,1)S(1)}, u32[]{:S(2)}, u32[]{:S(2)}) collective-permute-start(bf16[272,128]{1,0:T(8,128)(2,1)S(1)} %fusion.11), channel_id=1, source_target_pairs={{0,8},{8,0},{16,24},{24,16},{1,9},{9,1},{17,25},{25,17},{2,10},{10... | collective-permute-start | bytes 208904 | tf_op jit(solution)/shard_map/ppermute | solution.py:17
  44.5 4.6 %collective-permute-start.13 = (bf16[272,128]{1,0:T(8,128)(2,1)S(1)}, bf16[272,128]{1,0:T(8,128)(2,1)S(1)}, u32[]{:S(2)}, u32[]{:S(2)}) collective-permute-start(bf16[272,128]{1,0:T(8,128)(2,1)S(1)} %fusion.11), channel_id=1, source_target_pairs={{0,16},{8,24},{16,0},{24,8},{1,17},{9,25},{17,1},{25,9},{2,18},{10... | collective-permute-start | bytes 208904 | tf_op jit(solution)/shard_map/ppermute | solution.py:17
  46.0 5.2 %collective-permute-start.14 = (bf16[272,128]{1,0:T(8,128)(2,1)S(1)}, bf16[272,128]{1,0:T(8,128)(2,1)S(1)}, u32[]{:S(2)}, u32[]{:S(2)}) collective-permute-start(bf16[272,128]{1,0:T(8,128)(2,1)S(1)} %fusion.11), channel_id=1, source_target_pairs={{0,24},{8,16},{16,8},{24,0},{1,25},{9,17},{17,9},{25,1},{2,26},{10... | collective-permute-start | bytes 208904 | tf_op jit(solution)/shard_map/ppermute | solution.py:17
  47.6 8.6 %collective-permute-start.17 = (bf16[512,128]{1,0:T(8,128)(2,1)S(1)}, bf16[512,128]{1,0:T(8,128)(2,1)S(1)}, u32[]{:S(2)}, u32[]{:S(2)}) collective-permute-start(bf16[512,128]{1,0:T(8,128)(2,1)S(1)} %slice.62), channel_id=1, source_target_pairs={{0,4},{1,5},{2,6},{3,7},{4,0},{5,1},{6,2},{7,3},{8,12},{9,13},{10,... | collective-permute-start | bytes 393224 | tf_op jit(solution)/shard_map/ppermute | solution.py:17
  57.0 12.9 %collective-permute-start.21 = (bf16[128,512]{1,0:T(8,128)(2,1)S(1)}, bf16[128,512]{1,0:T(8,128)(2,1)S(1)}, u32[]{:S(2)}, u32[]{:S(2)}) collective-permute-start(bf16[128,512]{1,0:T(8,128)(2,1)S(1)} %gate_rows.1.earlier_ref.refs_0_), channel_id=1, source_target_pairs={{0,4},{1,5},{2,6},{3,7},{4,0},{5,1},{6,2},{7,3},{8,12},{9,13},{10,... | collective-permute-start | bytes 393224 | tf_op jit(solution)/shard_map/ppermute | solution.py:17
  58.3 11.5 %collective-permute-start.22 = (bf16[128,512]{1,0:T(8,128)(2,1)S(1)}, bf16[128,512]{1,0:T(8,128)(2,1)S(1)}, u32[]{:S(2)}, u32[]{:S(2)}) collective-permute-start(bf16[128,512]{1,0:T(8,128)(2,1)S(1)} %gate_rows.1.earlier_ref.refs_0_), channel_id=1, source_target_pairs={{0,6},{1,7},{2,4},{3,5},{4,2},{5,3},{6,0},{7,1},{8,14},{9,15},{10,... | collective-permute-start | bytes 393224 | tf_op jit(solution)/shard_map/ppermute | solution.py:17
  60.3 10.2 %collective-permute-start.19 = (bf16[128,512]{1,0:T(8,128)(2,1)S(1)}, bf16[128,512]{1,0:T(8,128)(2,1)S(1)}, u32[]{:S(2)}, u32[]{:S(2)}) collective-permute-start(bf16[128,512]{1,0:T(8,128)(2,1)S(1)} %gate_rows.1.earlier_ref.refs_0_), channel_id=1, source_target_pairs={{0,2},{1,3},{2,0},{3,1},{4,6},{5,7},{6,4},{7,5},{8,10},{9,11},{10,... | collective-permute-start | bytes 393224 | tf_op jit(solution)/shard_map/ppermute | solution.py:17
  60.8 9.7 %collective-permute-start.18 = (bf16[128,512]{1,0:T(8,128)(2,1)S(1)}, bf16[128,512]{1,0:T(8,128)(2,1)S(1)}, u32[]{:S(2)}, u32[]{:S(2)}) collective-permute-start(bf16[128,512]{1,0:T(8,128)(2,1)S(1)} %gate_rows.1.earlier_ref.refs_0_), channel_id=1, source_target_pairs={{0,1},{1,0},{2,3},{3,2},{4,5},{5,4},{6,7},{7,6},{8,9},{9,8},{10,11... | collective-permute-start | bytes 393224 | tf_op jit(solution)/shard_map/ppermute | solution.py:17
  73.8 5.8 %collective-permute-start.27 = (bf16[32,1024]{1,0:T(8,128)(2,1)S(1)}, bf16[32,1024]{1,0:T(8,128)(2,1)S(1)}, u32[]{:S(2)}, u32[]{:S(2)}) collective-permute-start(bf16[32,1024]{1,0:T(8,128)(2,1)S(1)} %get-tuple-element.128), channel_id=1, source_target_pairs={{0,24},{8,16},{16,8},{24,0},{1,25},{9,17},{17,9},{25,1},{2,26},{10... | collective-permute-start | bytes 196616 | tf_op jit(solution)/shard_map/ppermute | solution.py:17
  75.1 4.5 %collective-permute-start.25 = (bf16[32,1024]{1,0:T(8,128)(2,1)S(1)}, bf16[32,1024]{1,0:T(8,128)(2,1)S(1)}, u32[]{:S(2)}, u32[]{:S(2)}) collective-permute-start(bf16[32,1024]{1,0:T(8,128)(2,1)S(1)} %get-tuple-element.126), channel_id=1, source_target_pairs={{0,8},{8,0},{16,24},{24,16},{1,9},{9,1},{17,25},{25,17},{2,10},{10... | collective-permute-start | bytes 196616 | tf_op jit(solution)/shard_map/ppermute | solution.py:17
  75.8 4.5 %collective-permute-start.26 = (bf16[32,1024]{1,0:T(8,128)(2,1)S(1)}, bf16[32,1024]{1,0:T(8,128)(2,1)S(1)}, u32[]{:S(2)}, u32[]{:S(2)}) collective-permute-start(bf16[32,1024]{1,0:T(8,128)(2,1)S(1)} %get-tuple-element.127), channel_id=1, source_target_pairs={{0,16},{8,24},{16,0},{24,8},{1,17},{9,25},{17,1},{25,9},{2,18},{10... | collective-permute-start | bytes 196616 | tf_op jit(solution)/shard_map/ppermute | solution.py:17
  80.3 5.2 %collective-permute-start.30 = (bf16[32,1024]{1,0:T(8,128)(2,1)S(1)}, bf16[32,1024]{1,0:T(8,128)(2,1)S(1)}, u32[]{:S(2)}, u32[]{:S(2)}) collective-permute-start(bf16[32,1024]{1,0:T(8,128)(2,1)S(1)} %add_convert_fusion.2.refs_0_), channel_id=1, source_target_pairs={{0,24},{8,16},{16,8},{24,0},{1,25},{9,17},{17,9},{25,1},{2,26},{10... | collective-permute-start | bytes 196616 | tf_op jit(solution)/shard_map/ppermute | solution.py:17
  81.7 4.4 %collective-permute-start.28 = (bf16[32,1024]{1,0:T(8,128)(2,1)S(1)}, bf16[32,1024]{1,0:T(8,128)(2,1)S(1)}, u32[]{:S(2)}, u32[]{:S(2)}) collective-permute-start(bf16[32,1024]{1,0:T(8,128)(2,1)S(1)} %add_convert_fusion.2.refs_0_), channel_id=1, source_target_pairs={{0,8},{8,0},{16,24},{24,16},{1,9},{9,1},{17,25},{25,17},{2,10},{10... | collective-permute-start | bytes 196616 | tf_op jit(solution)/shard_map/ppermute | solution.py:17
  91.7 11.2 %collective-permute-start.33 = (bf16[16,2688]{1,0:T(8,128)(2,1)S(1)}, bf16[16,2688]{1,0:T(8,128)(2,1)S(1)}, u32[]{:S(2)}, u32[]{:S(2)}) collective-permute-start(bf16[16,2688]{1,0:T(8,128)(2,1)S(1)} %get-tuple-element.134), channel_id=1, source_target_pairs={{0,4},{1,5},{2,6},{3,7},{4,0},{5,1},{6,2},{7,3},{8,12},{9,13},{10,... | collective-permute-start | bytes 258056 | tf_op jit(solution)/shard_map/ppermute | solution.py:17
  95.0 7.9 %collective-permute-start.34 = (bf16[16,2688]{1,0:T(8,128)(2,1)S(1)}, bf16[16,2688]{1,0:T(8,128)(2,1)S(1)}, u32[]{:S(2)}, u32[]{:S(2)}) collective-permute-start(bf16[16,2688]{1,0:T(8,128)(2,1)S(1)} %get-tuple-element.135), channel_id=1, source_target_pairs={{0,6},{1,7},{2,4},{3,5},{4,2},{5,3},{6,0},{7,1},{8,14},{9,15},{10,... | collective-permute-start | bytes 258056 | tf_op jit(solution)/shard_map/ppermute | solution.py:17
  96.6 6.3 %collective-permute-start.32 = (bf16[16,2688]{1,0:T(8,128)(2,1)S(1)}, bf16[16,2688]{1,0:T(8,128)(2,1)S(1)}, u32[]{:S(2)}, u32[]{:S(2)}) collective-permute-start(bf16[16,2688]{1,0:T(8,128)(2,1)S(1)} %get-tuple-element.133), channel_id=1, source_target_pairs={{0,2},{1,3},{2,0},{3,1},{4,6},{5,7},{6,4},{7,5},{8,10},{9,11},{10,... | collective-permute-start | bytes 258056 | tf_op jit(solution)/shard_map/ppermute | solution.py:17
  104.7 7.2 %collective-permute-start.40 = (bf16[16,2048]{1,0:T(8,128)(2,1)S(1)}, bf16[16,2048]{1,0:T(8,128)(2,1)S(1)}, u32[]{:S(2)}, u32[]{:S(2)}) collective-permute-start(bf16[16,2048]{1,0:T(8,128)(2,1)S(1)} %bitcast.37), channel_id=1, source_target_pairs={{0,6},{1,7},{2,4},{3,5},{4,2},{5,3},{6,0},{7,1},{8,14},{9,15},{10,... | collective-permute-start | bytes 196616 | tf_op jit(solution)/shard_map/ppermute | solution.py:17
  106.7 5.8 %collective-permute-start.36 = (bf16[16,2048]{1,0:T(8,128)(2,1)S(1)}, bf16[16,2048]{1,0:T(8,128)(2,1)S(1)}, u32[]{:S(2)}, u32[]{:S(2)}) collective-permute-start(bf16[16,2048]{1,0:T(8,128)(2,1)S(1)} %bitcast.38), channel_id=1, source_target_pairs={{0,2},{1,3},{2,0},{3,1},{4,6},{5,7},{6,4},{7,5},{8,10},{9,11},{10,... | collective-permute-start | bytes 196616 | tf_op jit(solution)/shard_map/ppermute | solution.py:17
  106.7 6.8 %collective-permute-start.38 = (bf16[16,2048]{1,0:T(8,128)(2,1)S(1)}, bf16[16,2048]{1,0:T(8,128)(2,1)S(1)}, u32[]{:S(2)}, u32[]{:S(2)}) collective-permute-start(bf16[16,2048]{1,0:T(8,128)(2,1)S(1)} %bitcast.39), channel_id=1, source_target_pairs={{0,4},{1,5},{2,6},{3,7},{4,0},{5,1},{6,2},{7,3},{8,12},{9,13},{10,... | collective-permute-start | bytes 196616 | tf_op jit(solution)/shard_map/ppermute | solution.py:17
  109.1 4.4 %collective-permute-start.35 = (bf16[16,2048]{1,0:T(8,128)(2,1)S(1)}, bf16[16,2048]{1,0:T(8,128)(2,1)S(1)}, u32[]{:S(2)}, u32[]{:S(2)}) collective-permute-start(bf16[16,2048]{1,0:T(8,128)(2,1)S(1)} %bitcast.40), channel_id=1, source_target_pairs={{0,1},{1,0},{2,3},{3,2},{4,5},{5,4},{6,7},{7,6},{8,9},{9,8},{10,11... | collective-permute-start | bytes 196616 | tf_op jit(solution)/shard_map/ppermute | solution.py:17
  116.3 5.8 %collective-permute-start.44 = (bf16[32,1024]{1,0:T(8,128)(2,1)S(1)}, bf16[32,1024]{1,0:T(8,128)(2,1)S(1)}, u32[]{:S(2)}, u32[]{:S(2)}) collective-permute-start(bf16[32,1024]{1,0:T(8,128)(2,1)S(1)} %get-tuple-element.141), channel_id=1, source_target_pairs={{0,24},{8,16},{16,8},{24,0},{1,25},{9,17},{17,9},{25,1},{2,26},{10... | collective-permute-start | bytes 196616 | tf_op jit(solution)/shard_map/ppermute | solution.py:17
  117.2 4.9 %collective-permute-start.42 = (bf16[32,1024]{1,0:T(8,128)(2,1)S(1)}, bf16[32,1024]{1,0:T(8,128)(2,1)S(1)}, u32[]{:S(2)}, u32[]{:S(2)}) collective-permute-start(bf16[32,1024]{1,0:T(8,128)(2,1)S(1)} %get-tuple-element.139), channel_id=1, source_target_pairs={{0,8},{8,0},{16,24},{24,16},{1,9},{9,1},{17,25},{25,17},{2,10},{10... | collective-permute-start | bytes 196616 | tf_op jit(solution)/shard_map/ppermute | solution.py:17
  (27 other events, 177.8 us)
